TPU v7x, 32 devices: a whole 2x2x4 slice. The times are simulated.
32 devices in a mesh: groups: 2 (over x), expert: 16 (over z, y, core).
Axes of the slice: x: 2, y: 2, z: 4, core: 2. Of those that a mesh axis runs over, the one named last changes fastest.
Arguments:
- tokens: bfloat16 [4096, 4096], P(('groups', 'expert')), parts along dimension 0, may hold values from -6 to 6
- token_grad_in: bfloat16 [4096, 4096], P(('groups', 'expert')), parts along dimension 0, may hold values from -6 to 6
- expert_ids: int32 [4096, 1], P(('groups', 'expert')), parts along dimension 0, may hold values from 0 to 4; in each aligned block of 128 rows (0 to 127, 128 to 255, ...) at most 27 rows name the same one
- gate_weight: bfloat16 [16, 4096, 1376], P('expert'), may hold values from -0.09375 to 0.09375
- up_weight: bfloat16 [16, 4096, 1376], P('expert'), may hold values from -0.09375 to 0.09375
- down_weight: bfloat16 [16, 1376, 4096], P('expert'), may hold values from -0.078125 to 0.078125
Outputs:
- input_grad: bfloat16 [4096, 4096], P(('groups', 'expert')), parts along dimension 0
- down_grad: bfloat16 [32, 1376, 4096], P(('groups', 'expert')), parts along dimension 0
There are 2 independent parts, one for each index of `groups`. A program takes and returns all parts, laid end to end along the dimension named above; an argument that names none is the same for every part. Nothing has to cross between parts.
Inputs may be any that keep to these rules, and one draw needn't show every extreme that they name: `expert_ids`: among the 128 tokens of one device no value appears more than 27 times, and some value appears exactly 27 times; 4 marks a token that no routed expert takes.
All inputs are finite; a program needn't handle non-finite values.
Results may differ from a plain program's by a relative error of at most 0.0058.
Values may be sent and summed in bfloat16 or wider, within the bound.
No kernel may reach another device: no remote copies, remote signals or barrier semaphores. Data moves between devices by JAX's collectives and lax.ppermute only.
A program may use at most 128 MiB of HBM per device.

v0:
```python
import jax
import jax.numpy as jnp
from jax import lax
from jax.sharding import PartitionSpec as P

EXPERTS = 4


def expert_work(got_tokens, got_grad, w_gate, w_up, w_down):
    senders, slots, model_width = got_tokens.shape
    flat_tokens = got_tokens.reshape(senders * slots, model_width)
    flat_grad = got_grad.reshape(senders * slots, model_width)
    gate_pre = jnp.dot(flat_tokens, w_gate, preferred_element_type=jnp.float32)
    up_value = jnp.dot(flat_tokens, w_up, preferred_element_type=jnp.float32)
    sigmoid_g = jax.nn.sigmoid(gate_pre)
    activated = gate_pre * sigmoid_g
    hidden = (activated * up_value).astype(jnp.bfloat16)
    hidden_grad = lax.dot_general(
        flat_grad, w_down, (((1,), (1,)), ((), ())), preferred_element_type=jnp.float32
    )
    up_grad = (hidden_grad * activated).astype(jnp.bfloat16)
    gate_grad = (hidden_grad * up_value * sigmoid_g * (1.0 + gate_pre * (1.0 - sigmoid_g))).astype(
        jnp.bfloat16
    )
    partial_value = lax.dot_general(
        gate_grad, w_gate, (((1,), (1,)), ((), ())), preferred_element_type=jnp.float32
    )
    partial_value = partial_value + lax.dot_general(
        up_grad, w_up, (((1,), (1,)), ((), ())), preferred_element_type=jnp.float32
    )
    partial_value = partial_value.astype(jnp.bfloat16).reshape(senders, slots, model_width)
    return (partial_value, hidden.reshape(senders, slots, w_gate.shape[1]))


def shards(tokens, token_grad_in, expert_ids, gate_weight, up_weight, down_weight):
    devices = lax.axis_size("expert")
    tok_rows, model_width = tokens.shape
    group_size = devices // EXPERTS
    capacity = (tok_rows + EXPERTS) // (EXPERTS + 1) + 1
    token_ids = expert_ids[:, 0]
    onehot = (token_ids[:, None] == jnp.arange(EXPERTS + 1, dtype=jnp.int32)[None, :]).astype(
        jnp.int32
    )
    before = jnp.cumsum(onehot, axis=0) - onehot
    slot_index = jnp.sum(before * onehot, axis=1)
    target = token_ids * capacity + slot_index
    placement = (
        target[:, None] == jnp.arange(EXPERTS * capacity, dtype=jnp.int32)[None, :]
    ).astype(jnp.bfloat16)
    packed_tokens = jnp.einsum(
        "tc,td->cd", placement, tokens, preferred_element_type=jnp.float32
    ).astype(jnp.bfloat16)
    packed_grad = jnp.einsum(
        "tc,td->cd", placement, token_grad_in, preferred_element_type=jnp.float32
    ).astype(jnp.bfloat16)
    shape_four = (EXPERTS, group_size, capacity, model_width)
    out_tokens = jnp.broadcast_to(
        packed_tokens.reshape(EXPERTS, 1, capacity, model_width), shape_four
    ).reshape(devices, capacity, model_width)
    out_grad = jnp.broadcast_to(
        packed_grad.reshape(EXPERTS, 1, capacity, model_width), shape_four
    ).reshape(devices, capacity, model_width)
    w_gate = gate_weight[0]
    w_up = up_weight[0]
    w_down = down_weight[0]
    got_tokens, got_grad = (
        lax.all_to_all(out_tokens, "expert", split_axis=0, concat_axis=0, tiled=True),
        lax.all_to_all(out_grad, "expert", split_axis=0, concat_axis=0, tiled=True),
    )
    partial_value, hidden = expert_work(got_tokens, got_grad, w_gate, w_up, w_down)
    returned = lax.all_to_all(partial_value, "expert", split_axis=0, concat_axis=0, tiled=True)
    weight_grad = jnp.einsum(
        "nkh,nkd->hd", hidden, got_grad, preferred_element_type=jnp.float32
    ).astype(jnp.bfloat16)
    summed = jnp.sum(returned.reshape(shape_four).astype(jnp.float32), axis=1).reshape(
        EXPERTS * capacity, model_width
    )
    input_grad = jnp.dot(
        placement.astype(jnp.float32), summed, precision=lax.Precision.HIGHEST
    ).astype(jnp.bfloat16)
    return (input_grad, weight_grad[None])


def solution(mesh):
    placed = (
        P(("groups", "expert"), None),
        P(("groups", "expert"), None),
        P(("groups", "expert"), None),
        P("expert", None, None),
        P("expert", None, None),
        P("expert", None, None),
    )
    return jax.shard_map(
        shards,
        mesh=mesh,
        in_specs=placed,
        out_specs=(P(("groups", "expert"), None), P(("groups", "expert"), None, None)),
        check_vma=False,
    )
```

profile of v0, /device:TPU:13, one launch (start us, length us, event | category | flops | bytes accessed | tf_op | source)
XLA Modules:
  0.0 354.0 jit_solution(15835113013537398571)
XLA Ops:
  0.6 0.8 fusion.16
  1.7 0.8 select_reduce_fusion
  3.9 2.5 broadcast_in_dim.23
  6.5 6.7 %all-to-all-start.1 = ((bf16[16,27,4096]{2,1,0:T(8,128)(2,1)}), bf16[16,27,4096]{2,1,0:T(8,128)(2,1)}, u32[]{:S(2)}, u32[]{:S(2)}) async-start(bf16[16,27,4096]{2,1,0:T(8,128)(2,1)} %bitcast.44), calls=%async_computation.1 | async-start | bytes 8388608 | tf_op jit(solution)/shard_map/all_to_all | solution.py:67
  14.0 91.7 %all-to-all-done.1 = bf16[16,27,4096]{2,1,0:T(8,128)(2,1)} async-done(((bf16[16,27,4096]{2,1,0:T(8,128)(2,1)}), bf16[16,27,4096]{2,1,0:T(8,128)(2,1)}, u32[]{:S(2)}, u32[]{:S(2)}) %all-to-all-start.1) | async-done | bytes 3538976 | tf_op jit(solution)/shard_map/all_to_all | solution.py:67
  105.6 2.5 broadcast_in_dim.21
  108.1 4.9 %all-to-all-start = ((bf16[16,27,4096]{2,1,0:T(8,128)(2,1)}), bf16[16,27,4096]{2,1,0:T(8,128)(2,1)}, u32[]{:S(2)}, u32[]{:S(2)}) async-start(bf16[16,27,4096]{2,1,0:T(8,128)(2,1)} %bitcast.43), calls=%async_computation | async-start | bytes 8388608 | tf_op jit(solution)/shard_map/all_to_all | solution.py:68
  113.1 4.0 %reshape.36 = bf16[432,4096]{1,0:T(8,128)(2,1)} reshape(bf16[16,27,4096]{2,1,0:T(8,128)(2,1)} %all-to-all-done.1) | data formatting | bytes 7077888 | tf_op jit(solution)/shard_map/reshape | solution.py:11
  117.1 10.4 %fusion.3 = f32[432,1376]{1,0:T(8,128)S(1)} fusion(bf16[432,4096]{1,0:T(8,128)(2,1)} %reshape.36, bf16[1,4096,1376]{1,2,0:T(8,128)(2,1)} %param.9), kind=kOutput, calls=%fused_computation.4 | convolution fusion | flops 4869586944 | bytes 17188864 | tf_op jit(solution)/shard_map/dot_general | solution.py:13
  127.5 1.5 copy-done.4
  129.0 11.8 %multiply_convert_fusion = (bf16[432,1376]{1,0:T(8,128)(2,1)}, f32[432,1376]{1,0:T(8,128)}) fusion(f32[432,1376]{1,0:T(8,128)S(1)} %fusion.3, bf16[432,4096]{1,0:T(8,128)(2,1)S(1)} %copy-done.2, bf16[1,4096,1376]{1,2,0:T(8,128)(2,1)} %param.10), kind=kOutput, calls=%fused_computation.17 | convolution fusion | flops 4873153536 | bytes 20755456 | tf_op jit(solution)/shard_map/dot_general | solution.py:14
  140.8 64.8 %all-to-all-done = bf16[16,27,4096]{2,1,0:T(8,128)(2,1)} async-done(((bf16[16,27,4096]{2,1,0:T(8,128)(2,1)}), bf16[16,27,4096]{2,1,0:T(8,128)(2,1)}, u32[]{:S(2)}, u32[]{:S(2)}) %all-to-all-start) | async-done | bytes 3538976 | tf_op jit(solution)/shard_map/all_to_all | solution.py:68
  205.5 4.0 %reshape.34 = bf16[432,4096]{1,0:T(8,128)(2,1)} reshape(bf16[16,27,4096]{2,1,0:T(8,128)(2,1)} %all-to-all-done) | data formatting | bytes 7077888 | tf_op jit(solution)/shard_map/reshape | solution.py:12
  209.5 13.5 %fusion.9 = f32[432,1376]{1,0:T(8,128)} fusion(bf16[432,4096]{1,0:T(8,128)(2,1)} %reshape.34, bf16[1,1376,4096]{2,1,0:T(8,128)(2,1)} %param.11), kind=kOutput, calls=%fused_computation.10 | convolution fusion | flops 4869586944 | bytes 17188864 | tf_op jit(solution)/shard_map/dot_general | solution.py:18
  223.0 12.1 %fusion.1 = f32[432,4096]{1,0:T(8,128)S(1)} fusion(bf16[1,4096,1376]{1,2,0:T(8,128)(2,1)} %param.9, f32[432,1376]{1,0:T(8,128)} %copy-done.4, f32[432,1376]{1,0:T(8,128)} %fusion.9, f32[432,1376]{1,0:T(8,128)} %get-tuple-element.3), kind=kOutput, calls=%fused_computation.2 | convolution fusion | flops 4875531264 | bytes 25483264 | tf_op jit(solution)/shard_map/dot_general | solution.py:25
  235.2 9.1 %add_convert_fusion = bf16[432,4096]{1,0:T(8,128)(2,1)} fusion(f32[432,4096]{1,0:T(8,128)S(1)} %fusion.1, bf16[1,4096,1376]{1,2,0:T(8,128)(2,1)S(1)} %bitcast.48, f32[432,1376]{1,0:T(8,128)} %fusion.9, f32[432,1376]{1,0:T(8,128)S(1)} %copy-done.5), kind=kOutput, calls=%fused_computation.13 | convolution fusion | flops 4876692480 | bytes 26644480 | tf_op jit(solution)/shard_map/dot_general | solution.py:28
  244.3 4.0 %reshape.37 = bf16[16,27,4096]{2,1,0:T(8,128)(2,1)} reshape(bf16[432,4096]{1,0:T(8,128)(2,1)} %add_convert_fusion) | data formatting | bytes 7077888 | tf_op jit(solution)/shard_map/reshape | solution.py:31
  248.4 4.9 %all-to-all-start.2 = ((bf16[16,27,4096]{2,1,0:T(8,128)(2,1)}), bf16[16,27,4096]{2,1,0:T(8,128)(2,1)}, u32[]{:S(2)}, u32[]{:S(2)}) async-start(bf16[16,27,4096]{2,1,0:T(8,128)(2,1)} %reshape.37), calls=%async_computation.2 | async-start | bytes 8388608 | tf_op jit(solution)/shard_map/all_to_all | solution.py:71
  253.3 1.5 reshape.39
  254.8 10.4 %fusion = bf16[1,1376,4096]{2,1,0:T(8,128)(2,1)} fusion(bf16[16,27,1376]{2,1,0:T(8,128)(2,1)S(1)} %reshape.39, bf16[16,27,4096]{2,1,0:T(8,128)(2,1)} %all-to-all-done), kind=kOutput, calls=%fused_computation.1 | convolution fusion | flops 4875223040 | bytes 16000000 | tf_op jit(solution)/shard_map/nkh,nkd->hd/dot_general | solution.py:72
  265.2 80.6 %all-to-all-done.2 = bf16[16,27,4096]{2,1,0:T(8,128)(2,1)} async-done(((bf16[16,27,4096]{2,1,0:T(8,128)(2,1)}), bf16[16,27,4096]{2,1,0:T(8,128)(2,1)}, u32[]{:S(2)}, u32[]{:S(2)}) %all-to-all-start.2) | async-done | bytes 3538976 | tf_op jit(solution)/shard_map/all_to_all | solution.py:71
  345.7 3.2 convert_reduce_fusion
  349.0 1.5 reshape.38
  350.5 3.6 %convolution_convert_fusion = bf16[128,4096]{1,0:T(8,128)(2,1)} fusion(f32[108,4096]{1,0:T(8,128)} %reshape.38, s32[128]{0:T(128)S(1)} %fusion.20), kind=kOutput, calls=%fused_computation.14 | convolution fusion | flops 680015360 | bytes 2818560 | tf_op jit(solution)/shard_map/dot_general | solution.py:78
  (24 shorter events, 2.4 us)
Async XLA Ops:
  0.6 2.5 copy-start
  6.5 6.7 %copy-start.3 = (bf16[128,4096]{1,0:T(8,128)(2,1)S(1)}, bf16[128,4096]{1,0:T(8,128)(2,1)}, u32[]{:S(2)}) copy-start(bf16[128,4096]{1,0:T(8,128)(2,1)} %param.7) | copy-start | bytes 3145732
  6.5 99.2 %all-to-all-start.1 = ((bf16[16,27,4096]{2,1,0:T(8,128)(2,1)}), bf16[16,27,4096]{2,1,0:T(8,128)(2,1)}, u32[]{:S(2)}, u32[]{:S(2)}) async-start(bf16[16,27,4096]{2,1,0:T(8,128)(2,1)} %bitcast.44), calls=%async_computation.1 | async-start | bytes 8388608 | tf_op jit(solution)/shard_map/all_to_all | solution.py:67
  108.1 97.4 %all-to-all-start = ((bf16[16,27,4096]{2,1,0:T(8,128)(2,1)}), bf16[16,27,4096]{2,1,0:T(8,128)(2,1)}, u32[]{:S(2)}, u32[]{:S(2)}) async-start(bf16[16,27,4096]{2,1,0:T(8,128)(2,1)} %bitcast.43), calls=%async_computation | async-start | bytes 8388608 | tf_op jit(solution)/shard_map/all_to_all | solution.py:68
  117.1 11.9 %copy-start.2 = (bf16[432,4096]{1,0:T(8,128)(2,1)S(1)}, bf16[432,4096]{1,0:T(8,128)(2,1)}, u32[]{:S(2)}) copy-start(bf16[432,4096]{1,0:T(8,128)(2,1)} %reshape.36) | copy-start | bytes 10616836
  127.5 1.5 copy-start.4
  209.5 25.6 %slice-start = ((s8[11272192]{0:T(1024)(128)(4,1)}), s8[2883584]{0:T(1024)(128)(4,1)S(1)}, s32[]{:S(2)}) async-start(s8[11272192]{0:T(1024)(128)(4,1)} %bitcast.47), calls=%async_computation.3 | async-start | bytes 5767168
  209.5 25.6 %slice-start.1 = ((s8[11272192]{0:T(1024)(128)(4,1)}), s8[4194304]{0:T(1024)(128)(4,1)S(1)}, s32[]{:S(2)}) async-start(s8[11272192]{0:T(1024)(128)(4,1)} %bitcast.47), calls=%async_computation.4 | async-start | bytes 8388608
  223.0 12.2 %slice-start.2 = ((s8[11272192]{0:T(1024)(128)(4,1)}), s8[4194304]{0:T(1024)(128)(4,1)S(1)}, s32[]{:S(2)}) async-start(s8[11272192]{0:T(1024)(128)(4,1)} %bitcast.47), calls=%async_computation.5 | async-start | bytes 8388608
  223.0 12.2 %copy-start.5 = (f32[432,1376]{1,0:T(8,128)S(1)}, f32[432,1376]{1,0:T(8,128)}, u32[]{:S(2)}) copy-start(f32[432,1376]{1,0:T(8,128)} %copy-done.4) | copy-start | bytes 7133188
  248.4 97.4 %all-to-all-start.2 = ((bf16[16,27,4096]{2,1,0:T(8,128)(2,1)}), bf16[16,27,4096]{2,1,0:T(8,128)(2,1)}, u32[]{:S(2)}, u32[]{:S(2)}) async-start(bf16[16,27,4096]{2,1,0:T(8,128)(2,1)} %reshape.37), calls=%async_computation.2 | async-start | bytes 8388608 | tf_op jit(solution)/shard_map/all_to_all | solution.py:71
  345.7 8.3 %copy-start.1 = (bf16[128,4096]{1,0:T(8,128)(2,1)S(1)}, bf16[128,4096]{1,0:T(8,128)(2,1)}, u32[]{:S(2)}) copy-start(bf16[128,4096]{1,0:T(8,128)(2,1)} %param.6) | copy-start | bytes 3145732
where the time goes:
time: 355 us; the launch traced here: 354 us
  waiting for transfers between devices  237 us (67%)
  matrix products  71.9 us (20%)
  local copies, waits for them, and re-layouts  22.2 us (6%)
  starting transfers between devices  16.5 us (5%)
  other arithmetic  5.73 us (2%)
    all_to_all x1, waiting for transfers between devices, shards(): lax.all_to_all(out_tokens, 'expert', split_axis=0, concat_axis=0, tiled=T...  91.7 us
    all_to_all x1, waiting for transfers between devices, shards(): lax.all_to_all(partial_value, 'expert', split_axis=0, concat_axis=0, tile...  80.6 us
    all_to_all x1, waiting for transfers between devices, shards(): lax.all_to_all(out_grad, 'expert', split_axis=0, concat_axis=0, tiled=True)  64.8 us
    dot_general x1, matrix products, expert_work(): lax.dot_general(flat_grad, w_down, (((1,), (1,)), ((), ())), preferred_el...  13.5 us
    dot_general x1, matrix products, expert_work(): lax.dot_general(gate_grad, w_gate, (((1,), (1,)), ((), ())), preferred_el...  12.1 us
    dot_general x1, matrix products, expert_work(): up_value = jnp.dot(flat_tokens, w_up, preferred_element_type=jnp.float32)  11.8 us
    dot_general x1, matrix products, expert_work(): gate_pre = jnp.dot(flat_tokens, w_gate, preferred_element_type=jnp.float32)  10.4 us
    dot_general x1, matrix products, shards(): jnp.einsum('nkh,nkd->hd', hidden, got_grad, preferred_element_type=jnp.fl...  10.4 us
  transfers between devices with their start and end apart: 3, of which 3 were waited for; matrix products, arithmetic and copies ran while one was open for 11% of the time, Pallas kernels for 0%

commit v1 on v0

v1 whole, which is shorter than its diff:
```python
import functools

import jax
import jax.numpy as jnp
from jax import lax
from jax.experimental import pallas as pl
from jax.experimental.pallas import tpu as pltpu
from jax.sharding import PartitionSpec as P

EXPERTS = 4
F32, BF16 = jnp.float32, jnp.bfloat16
NT = (((1,), (1,)), ((), ()))
TN = (((0,), (0,)), ((), ()))
VMEM = 56 * 1024 * 1024


def params():
    return pltpu.CompilerParams(vmem_limit_bytes=VMEM, dimension_semantics=("arbitrary",))


def cost(flops, nbytes):
    return pl.CostEstimate(flops=flops, bytes_accessed=nbytes, transcendentals=0)


def whole(shape):
    return pl.BlockSpec(shape, lambda k, s: (0,) * len(shape))


def slot_map(ids, plane, slots, which, capacity):
    rows = ids.shape[0]
    lane = lax.broadcasted_iota(jnp.int32, (rows, 128), 1)
    onehot = jnp.where(ids == lane, 1.0, 0.0)
    row_i = lax.broadcasted_iota(jnp.int32, (rows, rows), 0)
    col_i = lax.broadcasted_iota(jnp.int32, (rows, rows), 1)
    earlier = jnp.where(col_i < row_i, 1.0, 0.0).astype(BF16)
    before = jnp.dot(earlier, onehot.astype(BF16), preferred_element_type=F32)
    slot = jnp.sum(before * onehot, axis=1, keepdims=True).astype(jnp.int32)
    shift = ids - plane
    shift = jnp.where(shift < 0, shift + EXPERTS, shift)
    target = shift * slots + which * capacity + slot
    target = jnp.where(ids < EXPERTS, target, -1)
    place = lax.broadcasted_iota(jnp.int32, (rows, EXPERTS * slots), 1)
    return jnp.where(target == place, 1.0, 0.0).astype(BF16)


def pack(info, ids, other_ids, mine, other, slots, capacity):
    width = mine.shape[1]

    def body(s, ids_ref, oids_ref, mine_ref, other_ref, *outs):
        p = slot_map(ids_ref[...], s[0], slots, s[1], capacity)
        q = slot_map(oids_ref[...], s[0], slots, 1 - s[1], capacity)
        got = lax.dot_general(p, mine_ref[...], TN, preferred_element_type=F32)
        got = got + lax.dot_general(q, other_ref[...], TN, preferred_element_type=F32)
        got = got.astype(BF16)
        for d in range(EXPERTS):
            outs[d][...] = got[d * slots : (d + 1) * slots]

    return pl.pallas_call(
        body,
        grid_spec=pltpu.PrefetchScalarGridSpec(
            num_scalar_prefetch=1,
            grid=(1,),
            in_specs=[whole(a.shape) for a in (ids, other_ids, mine, other)],
            out_specs=[whole((slots, width))] * EXPERTS,
        ),
        out_shape=[jax.ShapeDtypeStruct((slots, width), BF16)] * EXPERTS,
        compiler_params=params(),
        cost_estimate=cost(4 * 256 * 224 * width, 4 * 256 * width),
        name="pack",
    )(info, ids, other_ids, mine, other)


def unpack(info, ids, other_ids, pieces, slots, capacity):
    rows, width = ids.shape[0], pieces[0].shape[1]

    def body(s, ids_ref, oids_ref, *refs):
        p = slot_map(ids_ref[...], s[0], slots, s[1], capacity)
        q = slot_map(oids_ref[...], s[0], slots, 1 - s[1], capacity)
        z = jnp.concatenate([r[...].astype(F32) for r in refs[:EXPERTS]], axis=0).astype(BF16)
        refs[EXPERTS][...] = jnp.dot(p, z, preferred_element_type=F32).astype(BF16)
        refs[EXPERTS + 1][...] = jnp.dot(q, z, preferred_element_type=F32).astype(BF16)

    return pl.pallas_call(
        body,
        grid_spec=pltpu.PrefetchScalarGridSpec(
            num_scalar_prefetch=1,
            grid=(1,),
            in_specs=[whole(a.shape) for a in (ids, other_ids, *pieces)],
            out_specs=[whole((rows, width))] * 2,
        ),
        out_shape=[jax.ShapeDtypeStruct((rows, width), BF16)] * 2,
        compiler_params=params(),
        cost_estimate=cost(4 * 256 * 224 * width, 4 * 256 * width),
        name="unpack",
    )(info, ids, other_ids, *pieces)


def gate_up(info, own, other, w_gate, w_up, hb=512):
    hidden, model = w_gate.shape
    half = model // 2
    sizes = [a.shape[0] for a in own]
    m, n = sum(sizes), len(own)

    def body(s, *refs):
        xo, xt = refs[:n], refs[n : 2 * n]
        g_ref, u_ref, act_ref, dact_ref, hid_ref, xa, xb = refs[2 * n :]

        @pl.when(pl.program_id(0) == 0)
        def _():
            at = 0
            for i, rows in enumerate(sizes):
                xa[at : at + rows] = xo[i][...]
                xb[at : at + rows] = xt[i][...]
                at += rows

        mine = pl.ds(pl.multiple_of(s[1] * half, 128), half)
        others = pl.ds(pl.multiple_of((1 - s[1]) * half, 128), half)
        a, b = xa[...], xb[...]

        def product(w_ref):
            return lax.dot_general(
                a, w_ref[:, mine], NT, preferred_element_type=F32
            ) + lax.dot_general(b, w_ref[:, others], NT, preferred_element_type=F32)

        g, u = product(g_ref), product(u_ref)
        sig = jax.nn.sigmoid(g)
        act = g * sig
        act_ref[...] = act
        dact_ref[...] = u * sig * (1.0 + g * (1.0 - sig))
        hid_ref[...] = (act * u).T.astype(BF16)

    return pl.pallas_call(
        body,
        grid_spec=pltpu.PrefetchScalarGridSpec(
            num_scalar_prefetch=1,
            grid=(pl.cdiv(hidden, hb),),
            in_specs=[whole(a.shape) for a in (*own, *other)]
            + [pl.BlockSpec((hb, model), lambda k, s: (k, 0))] * 2,
            out_specs=[
                pl.BlockSpec((m, hb), lambda k, s: (0, k)),
                pl.BlockSpec((m, hb), lambda k, s: (0, k)),
                pl.BlockSpec((hb, m), lambda k, s: (k, 0)),
            ],
            scratch_shapes=[pltpu.VMEM((m, half), BF16)] * 2,
        ),
        out_shape=[
            jax.ShapeDtypeStruct((m, hidden), F32),
            jax.ShapeDtypeStruct((m, hidden), F32),
            jax.ShapeDtypeStruct((hidden, m), BF16),
        ],
        compiler_params=params(),
        cost_estimate=cost(4 * m * model * hidden, 4 * model * hidden),
        name="gate_up",
    )(info, *own, *other, w_gate, w_up)


def hidden_grads(info, own, other, w_down, act, dact, row0, hb=512):
    hidden, model = w_down.shape
    half = model // 2
    sizes = [a.shape[0] for a in own]
    m, n = sum(sizes), len(own)
    full = act.shape[0]

    def body(s, *refs):
        xo, xt = refs[:n], refs[n : 2 * n]
        w_ref, a_ref, da_ref, ug_ref, gg_ref, xa, xb = refs[2 * n :]

        @pl.when(pl.program_id(0) == 0)
        def _():
            at = 0
            for i, rows in enumerate(sizes):
                xa[at : at + rows] = xo[i][...]
                xb[at : at + rows] = xt[i][...]
                at += rows

        mine = pl.ds(pl.multiple_of(s[1] * half, 128), half)
        others = pl.ds(pl.multiple_of((1 - s[1]) * half, 128), half)
        h = lax.dot_general(xa[...], w_ref[:, mine], NT, preferred_element_type=F32)
        h = h + lax.dot_general(xb[...], w_ref[:, others], NT, preferred_element_type=F32)
        ug_ref[...] = (h * a_ref[row0 : row0 + m]).astype(BF16)
        gg_ref[...] = (h * da_ref[row0 : row0 + m]).astype(BF16)

    return pl.pallas_call(
        body,
        grid_spec=pltpu.PrefetchScalarGridSpec(
            num_scalar_prefetch=1,
            grid=(pl.cdiv(hidden, hb),),
            in_specs=[whole(a.shape) for a in (*own, *other)]
            + [pl.BlockSpec((hb, model), lambda k, s: (k, 0))]
            + [pl.BlockSpec((full, hb), lambda k, s: (0, k))] * 2,
            out_specs=[pl.BlockSpec((m, hb), lambda k, s: (0, k))] * 2,
            scratch_shapes=[pltpu.VMEM((m, half), BF16)] * 2,
        ),
        out_shape=[jax.ShapeDtypeStruct((m, hidden), BF16)] * 2,
        compiler_params=params(),
        cost_estimate=cost(2 * m * model * hidden, 2 * model * hidden),
        name="hidden_grads",
    )(info, *own, *other, w_down, act, dact)


def partial_half(info, gate_grad, up_grad, w_gate, w_up, kept, db=1024):
    hidden, model = w_gate.shape
    half = model // 2
    db = min(db, half)
    steps = half // db
    m = gate_grad.shape[0]

    def column(k, s):
        side = s[1] if kept else 1 - s[1]
        return (0, side * steps + k)

    def body(s, g_ref, u_ref, wg_ref, wu_ref, o_ref):
        o = jnp.dot(g_ref[...], wg_ref[...], preferred_element_type=F32)
        o = o + jnp.dot(u_ref[...], wu_ref[...], preferred_element_type=F32)
        o_ref[...] = o.astype(BF16)

    return pl.pallas_call(
        body,
        grid_spec=pltpu.PrefetchScalarGridSpec(
            num_scalar_prefetch=1,
            grid=(steps,),
            in_specs=[whole((m, hidden))] * 2 + [pl.BlockSpec((hidden, db), column)] * 2,
            out_specs=pl.BlockSpec((m, db), lambda k, s: (0, k)),
        ),
        out_shape=jax.ShapeDtypeStruct((m, half), BF16),
        compiler_params=params(),
        cost_estimate=cost(4 * m * half * hidden, 4 * half * hidden),
        name="partial",
    )(info, gate_grad, up_grad, w_gate, w_up)


def down_grads(info, hidden_t, own, other, db=1024):
    hidden, m = hidden_t.shape
    half = own[0].shape[1]
    db = min(db, half)
    steps = half // db
    sizes = [a.shape[0] for a in own]
    n = len(own)

    def body(s, h_ref, *refs):
        go, gt, o_ref, g = refs[:n], refs[n : 2 * n], refs[2 * n], refs[2 * n + 1]

        def fill(parts):
            at = 0
            for i, rows in enumerate(sizes):
                g[at : at + rows] = parts[i][...]
                at += rows

        @pl.when(pl.program_id(0) < steps)
        def _():
            fill(go)

        @pl.when(pl.program_id(0) >= steps)
        def _():
            fill(gt)

        o_ref[...] = jnp.dot(h_ref[...], g[...], preferred_element_type=F32).astype(BF16)

    return pl.pallas_call(
        body,
        grid_spec=pltpu.PrefetchScalarGridSpec(
            num_scalar_prefetch=1,
            grid=(2 * steps,),
            in_specs=[whole(hidden_t.shape)]
            + [pl.BlockSpec((r, db), lambda k, s: (0, jnp.minimum(k, steps - 1))) for r in sizes]
            + [pl.BlockSpec((r, db), lambda k, s: (0, jnp.maximum(k - steps, 0))) for r in sizes],
            out_specs=pl.BlockSpec(
                (hidden, db), lambda k, s: (0, lax.rem(k + s[1] * steps, 2 * steps))
            ),
            scratch_shapes=[pltpu.VMEM((m, db), BF16)],
        ),
        out_shape=jax.ShapeDtypeStruct((hidden, 2 * half), BF16),
        compiler_params=params(),
        cost_estimate=cost(4 * m * half * hidden, 4 * half * hidden),
        name="down_grads",
    )(info, hidden_t, *own, *other)


GROUPS = ((0,), (1, 3), (2,))
CHUNKS = ((0, 2), (1,))


def shards(tokens, token_grad_in, expert_ids, gate_weight, up_weight, down_weight):
    devices = lax.axis_size("expert")
    rows, model = tokens.shape
    half = model // 2
    share = devices // EXPERTS
    capacity = (rows + EXPERTS) // (EXPERTS + 1) + 1
    slots = -(-2 * capacity // 8) * 8
    bits = [b for b in range(1, share.bit_length() - 1)]
    index = lax.axis_index("expert")
    core = lax.rem(index, 2)
    info = jnp.stack([index // share, core]).astype(jnp.int32)

    def flip(x, bit):
        return lax.ppermute(x, "expert", [(i, i ^ (1 << bit)) for i in range(devices)])

    def plane_shift(x, d):
        return lax.ppermute(
            x, "expert", [(i, (i + d * share) % devices) for i in range(devices)]
        )

    def split(x):
        mine = lax.dynamic_slice_in_dim(x, core * half, half, 1)
        others = lax.dynamic_slice_in_dim(x, (1 - core) * half, half, 1)
        return mine, flip(others, 0)

    other_ids = flip(expert_ids, 0)

    def forward(x):
        mine, other = split(x)
        pieces = pack(info, expert_ids, other_ids, mine, other, slots, capacity)
        pieces = [pieces[0]] + [plane_shift(pieces[d], d) for d in range(1, EXPERTS)]
        own, others = [], []
        for group in GROUPS:
            part = jnp.concatenate([pieces[d] for d in group], axis=0)
            for bit in bits:
                part = jnp.concatenate([part, flip(part, bit)], axis=0)
            own.append(part)
            others.append(flip(part, 0))
        return own, others

    w_gate = jnp.swapaxes(gate_weight[0], 0, 1)
    w_up = jnp.swapaxes(up_weight[0], 0, 1)
    w_down = down_weight[0]

    x_own, x_other = forward(tokens)
    g_own, g_other = forward(token_grad_in)
    sizes = [a.shape[0] for a in x_own]
    order = [g for chunk in CHUNKS for g in chunk]
    act, dact, hidden_t = gate_up(
        info, [x_own[g] for g in order], [x_other[g] for g in order], w_gate, w_up
    )
    pieces = {}
    row0 = 0
    for chunk in CHUNKS:
        up_grad, gate_grad = hidden_grads(
            info, [g_own[g] for g in chunk], [g_other[g] for g in chunk], w_down, act, dact, row0
        )
        row0 += sum(sizes[g] for g in chunk)
        sent = flip(partial_half(info, gate_grad, up_grad, w_gate, w_up, 0), 0)
        kept = partial_half(info, gate_grad, up_grad, w_gate, w_up, 1)
        at = 0
        for g in chunk:
            total = kept[at : at + sizes[g]].astype(F32) + sent[at : at + sizes[g]].astype(F32)
            at += sizes[g]
            for bit in reversed(bits):
                mid = total.shape[0] // 2
                total = total[:mid] + flip(total[mid:].astype(BF16), bit).astype(F32)
            for i, d in enumerate(GROUPS[g]):
                piece = total[i * slots : (i + 1) * slots].astype(BF16)
                pieces[d] = plane_shift(piece, EXPERTS - d) if d else piece
    down_grad = down_grads(
        info, hidden_t, [g_own[g] for g in order], [g_other[g] for g in order]
    )
    mine, theirs = unpack(
        info, expert_ids, other_ids, [pieces[d] for d in range(EXPERTS)], slots, capacity
    )
    got = flip(theirs, 0)
    input_grad = jnp.where(
        core == 0,
        jnp.concatenate([mine, got], axis=1),
        jnp.concatenate([got, mine], axis=1),
    )
    return (input_grad, down_grad[None])


def solution(mesh):
    placed = (
        P(("groups", "expert"), None),
        P(("groups", "expert"), None),
        P(("groups", "expert"), None),
        P("expert", None, None),
        P("expert", None, None),
        P("expert", None, None),
    )
    return jax.shard_map(
        shards,
        mesh=mesh,
        in_specs=placed,
        out_specs=(P(("groups", "expert"), None), P(("groups", "expert"), None, None)),
        check_vma=False,
    )
```

time: 355 us -> 220 us (0.62)
  the two profiles are of different devices: /device:TPU:13 before, /device:TPU:0 now
where the time goes in v1:
time: 220 us; the launch traced here: 219 us
  Pallas kernels  93.9 us (43%)
  waiting for transfers between devices  56.7 us (26%)
  starting transfers between devices  52.2 us (24%)
  local copies, waits for them, and re-layouts  10.8 us (5%)
  other arithmetic  4.59 us (2%)
    ppermute x9, starting transfers between devices, plane_shift(): lax.ppermute(x, 'expert', [(i, (i + d * share) % devices) for i in range(...  38.9 us
    ppermute x21, waiting for transfers between devices, flip(): lax.ppermute(x, 'expert', [(i, i ^ 1 << bit) for i in range(devices)])  33.8 us
    pallas_call x4, Pallas kernels, partial_half(): pl.pallas_call(body, grid_spec=pltpu.PrefetchScalarGridSpec(num_scalar_pr...  31 us
    ppermute x9, waiting for transfers between devices, plane_shift(): lax.ppermute(x, 'expert', [(i, (i + d * share) % devices) for i in range(...  22.9 us
    pallas_call x2, Pallas kernels, hidden_grads(): pl.pallas_call(body, grid_spec=pltpu.PrefetchScalarGridSpec(num_scalar_pr...  20 us
    pallas_call x1, Pallas kernels, gate_up(): pl.pallas_call(body, grid_spec=pltpu.PrefetchScalarGridSpec(num_scalar_pr...  19.6 us
    ppermute x21, starting transfers between devices, flip(): lax.ppermute(x, 'expert', [(i, i ^ 1 << bit) for i in range(devices)])  13.2 us
    pallas_call x1, Pallas kernels, down_grads(): pl.pallas_call(body, grid_spec=pltpu.PrefetchScalarGridSpec(num_scalar_pr...  11.9 us
  transfers between devices with their start and end apart: 30, of which 11 were waited for; matrix products, arithmetic and copies ran while one was open for 3% of the time, Pallas kernels for 41%

profile of v1, /device:TPU:0, one launch (start us, length us, event | category | flops | bytes accessed | tf_op | source)
XLA Modules:
  0.0 219.2 jit_solution(11525850507322422492)
XLA Ops:
  7.0 3.9 %pack.3 = (bf16[56,2048]{1,0:T(8,128)(2,1)}, bf16[56,2048]{1,0:T(8,128)(2,1)}, bf16[56,2048]{1,0:T(8,128)(2,1)}, bf16[56,2048]{1,0:T(8,128)(2,1)}) custom-call(s32[2]{0:T(128)} %pad_add_fusion.s, s32[128,1]{1,0:T(8,128)} %copy-done.11, s32[128,1]{1,0:T(8,128)} %copy-done.22, bf16[128,2048]{1,0:T(8,128)(2,1)} %get-tuple-element.39.mine_ref, ...), custom_call_target="tpu_custom_call" | custom-call | flops 469762048 | bytes 2097152 | tf_op jit(solution)/shard_map/pack/pallas_call | solution.py:58
  10.9 3.7 %collective-permute-start.9 = (bf16[56,2048]{1,0:T(8,128)(2,1)}, bf16[56,2048]{1,0:T(8,128)(2,1)S(1)}, u32[]{:S(2)}, u32[]{:S(2)}) collective-permute-start(bf16[56,2048]{1,0:T(8,128)(2,1)} %get-tuple-element.22), channel_id=1, source_target_pairs={{0,8},{1,9},{2,10},{3,11},{4,12},{5,13},{6,14},{7,15},{8,0},{9,1},... | collective-permute-start | bytes 688136 | tf_op jit(solution)/shard_map/ppermute | solution.py:299
  21.8 3.9 %pack.2 = (bf16[56,2048]{1,0:T(8,128)(2,1)}, bf16[56,2048]{1,0:T(8,128)(2,1)}, bf16[56,2048]{1,0:T(8,128)(2,1)}, bf16[56,2048]{1,0:T(8,128)(2,1)}) custom-call(s32[2]{0:T(128)} %pad_add_fusion.s, s32[128,1]{1,0:T(8,128)} %copy-done.11, s32[128,1]{1,0:T(8,128)} %copy-done.22, bf16[128,2048]{1,0:T(8,128)(2,1)} %get-tuple-element.41.mine_ref, ...), custom_call_target="tpu_custom_call" | custom-call | flops 469762048 | bytes 2097152 | tf_op jit(solution)/shard_map/pack/pallas_call | solution.py:58
  27.7 10.7 %collective-permute-start.3 = (bf16[56,2048]{1,0:T(8,128)(2,1)}, bf16[56,2048]{1,0:T(8,128)(2,1)S(1)}, u32[]{:S(2)}, u32[]{:S(2)}) collective-permute-start(bf16[56,2048]{1,0:T(8,128)(2,1)} %get-tuple-element.20), channel_id=1, source_target_pairs={{0,8},{1,9},{2,10},{3,11},{4,12},{5,13},{6,14},{7,15},{8,0},{9,1},... | collective-permute-start | bytes 688136 | tf_op jit(solution)/shard_map/ppermute | solution.py:299
  38.5 3.9 %collective-permute-start.20 = (bf16[56,2048]{1,0:T(8,128)(2,1)}, bf16[56,2048]{1,0:T(8,128)(2,1)S(1)}, u32[]{:S(2)}, u32[]{:S(2)}) collective-permute-start(bf16[56,2048]{1,0:T(8,128)(2,1)} %get-tuple-element.30), channel_id=1, source_target_pairs={{0,12},{1,13},{2,14},{3,15},{4,0},{5,1},{6,2},{7,3},{8,4},{9,5},{1... | collective-permute-start | bytes 688136 | tf_op jit(solution)/shard_map/ppermute | solution.py:299
  42.5 8.2 %collective-permute-done.19 = bf16[56,2048]{1,0:T(8,128)(2,1)S(1)} collective-permute-done((bf16[56,2048]{1,0:T(8,128)(2,1)}, bf16[56,2048]{1,0:T(8,128)(2,1)S(1)}, u32[]{:S(2)}, u32[]{:S(2)}) %collective-permute-start.19) | collective-permute-done | bytes 229408 | tf_op jit(solution)/shard_map/ppermute | solution.py:299
  52.2 3.3 %collective-permute-done.20 = bf16[56,2048]{1,0:T(8,128)(2,1)S(1)} collective-permute-done((bf16[56,2048]{1,0:T(8,128)(2,1)}, bf16[56,2048]{1,0:T(8,128)(2,1)S(1)}, u32[]{:S(2)}, u32[]{:S(2)}) %collective-permute-start.20) | collective-permute-done | bytes 229408 | tf_op jit(solution)/shard_map/ppermute | solution.py:299
  57.8 6.1 %collective-permute-done.13 = bf16[112,2048]{1,0:T(8,128)(2,1)S(1)} collective-permute-done((bf16[112,2048]{1,0:T(8,128)(2,1)S(1)}, bf16[112,2048]{1,0:T(8,128)(2,1)S(1)}, u32[]{:S(2)}, u32[]{:S(2)}) %collective-permute-start.13) | collective-permute-done | bytes 458784 | tf_op jit(solution)/shard_map/ppermute | solution.py:296
  64.0 12.0 %collective-permute-done.10 = bf16[56,2048]{1,0:T(8,128)(2,1)S(1)} collective-permute-done((bf16[56,2048]{1,0:T(8,128)(2,1)S(1)}, bf16[56,2048]{1,0:T(8,128)(2,1)S(1)}, u32[]{:S(2)}, u32[]{:S(2)}) %collective-permute-start.10) | collective-permute-done | bytes 229408 | tf_op jit(solution)/shard_map/ppermute | solution.py:296
  77.6 4.5 %collective-permute-done.4 = bf16[56,2048]{1,0:T(8,128)(2,1)S(1)} collective-permute-done((bf16[56,2048]{1,0:T(8,128)(2,1)S(1)}, bf16[56,2048]{1,0:T(8,128)(2,1)S(1)}, u32[]{:S(2)}, u32[]{:S(2)}) %collective-permute-start.4) | collective-permute-done | bytes 229408 | tf_op jit(solution)/shard_map/ppermute | solution.py:296
  85.1 19.6 %gate_up.1 = (f32[448,1376]{1,0:T(8,128)}, f32[448,1376]{1,0:T(8,128)}, bf16[1376,448]{1,0:T(8,128)(2,1)}) custom-call(s32[2]{0:T(128)} %pad_add_fusion.s, bf16[112,2048]{1,0:T(8,128)(2,1)} %copy-done.9, bf16[112,2048]{1,0:T(8,128)(2,1)} %copy-done.10, bf16[224,2048]{1,0:T(8,128)(2,1)} %copy-done.12, bf16[112,2048]{1,0:T(8,128)(2,1)} %copy-done.17, ...), custom_call_target="tpu_custom_call" | custom-call | flops 10099884032 | bytes 22544384 | tf_op jit(solution)/shard_map/gate_up/pallas_call | solution.py:132
  105.6 10.0 %hidden_grads.2 = (bf16[224,1376]{1,0:T(8,128)(2,1)}, bf16[224,1376]{1,0:T(8,128)(2,1)}) custom-call(s32[2]{0:T(128)} %pad_add_fusion.s, bf16[112,2048]{1,0:T(8,128)(2,1)} %copy-done.3, bf16[112,2048]{1,0:T(8,128)(2,1)} %copy-done.4, bf16[112,2048]{1,0:T(8,128)(2,1)} %copy-done.7, bf16[112,2048]{1,0:T(8,128)(2,1)} %copy-done.8, bf16[1376,4096]{1,0:T(8,128)(2,1)} %bitcast.20, ...), custom_call_target="tpu_custom_call" | custom-call | flops 2524971008 | bytes 11272192 | tf_op jit(solution)/shard_map/hidden_grads/pallas_call | solution.py:183
  115.6 7.7 %partial.5 = bf16[224,2048]{1,0:T(8,128)(2,1)} custom-call(s32[2]{0:T(128)} %pad_add_fusion.s, bf16[224,1376]{1,0:T(8,128)(2,1)} %get-tuple-element.27.g_ref, bf16[224,1376]{1,0:T(8,128)(2,1)} %get-tuple-element.28.u_ref, bf16[1376,4096]{1,0:T(8,128)(2,1)} %bitcast.11, bf16[1376,4096]{1,0:T(8,128)(2,1)} %bitcast.16), custom_call_target="tpu_custom_call" | custom-call | flops 2524971008 | bytes 11272192 | tf_op jit(solution)/shard_map/partial/pallas_call | solution.py:217
  124.4 10.1 %hidden_grads.3 = (bf16[224,1376]{1,0:T(8,128)(2,1)}, bf16[224,1376]{1,0:T(8,128)(2,1)}) custom-call(s32[2]{0:T(128)} %pad_add_fusion.s, bf16[224,2048]{1,0:T(8,128)(2,1)} %copy-done.1, bf16[224,2048]{1,0:T(8,128)(2,1)} %copy-done.5, bf16[1376,4096]{1,0:T(8,128)(2,1)} %bitcast.21, f32[448,1376]{1,0:T(8,128)} %get-tuple-element.25.refs_5_.refs_3_, ...), custom_call_target="tpu_custom_call" | custom-call | flops 2524971008 | bytes 11272192 | tf_op jit(solution)/shard_map/hidden_grads/pallas_call | solution.py:183
  134.5 7.8 %partial.7 = bf16[224,2048]{1,0:T(8,128)(2,1)} custom-call(s32[2]{0:T(128)} %pad_add_fusion.s, bf16[224,1376]{1,0:T(8,128)(2,1)} %get-tuple-element.31.g_ref, bf16[224,1376]{1,0:T(8,128)(2,1)} %get-tuple-element.32.u_ref, bf16[1376,4096]{1,0:T(8,128)(2,1)} %bitcast.12, bf16[1376,4096]{1,0:T(8,128)(2,1)} %bitcast.17), custom_call_target="tpu_custom_call" | custom-call | flops 2524971008 | bytes 11272192 | tf_op jit(solution)/shard_map/partial/pallas_call | solution.py:217
  142.6 7.8 %partial.6 = bf16[224,2048]{1,0:T(8,128)(2,1)} custom-call(s32[2]{0:T(128)} %pad_add_fusion.s, bf16[224,1376]{1,0:T(8,128)(2,1)} %get-tuple-element.31.g_ref, bf16[224,1376]{1,0:T(8,128)(2,1)} %get-tuple-element.32.u_ref, bf16[1376,4096]{1,0:T(8,128)(2,1)} %bitcast.13, bf16[1376,4096]{1,0:T(8,128)(2,1)} %bitcast.18), custom_call_target="tpu_custom_call" | custom-call | flops 2524971008 | bytes 11272192 | tf_op jit(solution)/shard_map/partial/pallas_call | solution.py:217
  150.4 7.7 %partial.4 = bf16[224,2048]{1,0:T(8,128)(2,1)} custom-call(s32[2]{0:T(128)} %pad_add_fusion.s, bf16[224,1376]{1,0:T(8,128)(2,1)} %get-tuple-element.27.g_ref, bf16[224,1376]{1,0:T(8,128)(2,1)} %get-tuple-element.28.u_ref, bf16[1376,4096]{1,0:T(8,128)(2,1)} %bitcast.14, bf16[1376,4096]{1,0:T(8,128)(2,1)} %bitcast.19), custom_call_target="tpu_custom_call" | custom-call | flops 2524971008 | bytes 11272192 | tf_op jit(solution)/shard_map/partial/pallas_call | solution.py:217
  163.8 9.4 %collective-permute-done.26 = bf16[56,2048]{1,0:T(8,128)(2,1)S(1)} collective-permute-done((bf16[56,2048]{1,0:T(8,128)(2,1)S(1)}, bf16[56,2048]{1,0:T(8,128)(2,1)S(1)}, u32[]{:S(2)}, u32[]{:S(2)}) %collective-permute-start.26) | collective-permute-done | bytes 229408 | tf_op jit(solution)/shard_map/ppermute | solution.py:296
  173.2 9.6 %collective-permute-start.27 = (bf16[56,2048]{1,0:T(8,128)(2,1)S(1)}, bf16[56,2048]{1,0:T(8,128)(2,1)S(1)}, u32[]{:S(2)}, u32[]{:S(2)}) collective-permute-start(bf16[56,2048]{1,0:T(8,128)(2,1)S(1)} %fusion.1), channel_id=1, source_target_pairs={{0,8},{1,9},{2,10},{3,11},{4,12},{5,13},{6,14},{7,15},{8,0},{9,1},... | collective-permute-start | bytes 688136 | tf_op jit(solution)/shard_map/ppermute | solution.py:299
  183.0 7.1 %collective-permute-start.28 = (bf16[56,2048]{1,0:T(8,128)(2,1)S(1)}, bf16[56,2048]{1,0:T(8,128)(2,1)S(1)}, u32[]{:S(2)}, u32[]{:S(2)}) collective-permute-start(bf16[56,2048]{1,0:T(8,128)(2,1)S(1)} %get-tuple-element.42), channel_id=1, source_target_pairs={{0,4},{1,5},{2,6},{3,7},{4,8},{5,9},{6,10},{7,11},{8,12},{9,13},{1... | collective-permute-start | bytes 688136 | tf_op jit(solution)/shard_map/ppermute | solution.py:299
  190.8 6.5 %collective-permute-done.27.refs_2_ = bf16[56,2048]{1,0:T(8,128)(2,1)S(1)} collective-permute-done((bf16[56,2048]{1,0:T(8,128)(2,1)S(1)}, bf16[56,2048]{1,0:T(8,128)(2,1)S(1)}, u32[]{:S(2)}, u32[]{:S(2)}) %collective-permute-start.27) | collective-permute-done | bytes 229408 | tf_op jit(solution)/shard_map/ppermute | solution.py:299
  197.4 4.4 %collective-permute-done.25.refs_1_ = bf16[56,2048]{1,0:T(8,128)(2,1)S(1)} collective-permute-done((bf16[56,2048]{1,0:T(8,128)(2,1)S(1)}, bf16[56,2048]{1,0:T(8,128)(2,1)S(1)}, u32[]{:S(2)}, u32[]{:S(2)}) %collective-permute-start.25) | collective-permute-done | bytes 229408 | tf_op jit(solution)/shard_map/ppermute | solution.py:299
  202.5 3.6 %unpack.1 = (bf16[128,2048]{1,0:T(8,128)(2,1)}, bf16[128,2048]{1,0:T(8,128)(2,1)}) custom-call(s32[2]{0:T(128)} %pad_add_fusion.s, s32[128,1]{1,0:T(8,128)} %copy-done.11, s32[128,1]{1,0:T(8,128)} %copy-done.22, bf16[56,2048]{1,0:T(8,128)(2,1)} %fusion.2.refs_0_, bf16[56,2048]{1,0:T(8,128)(2,1)} %copy-done.21, bf16[56,2048]{1,0:T(8,128)(2,1)} %copy-done.19, ...), custom_call_target="tpu_custom_call" | custom-call | flops 469762048 | bytes 2097152 | tf_op jit(solution)/shard_map/unpack/pallas_call | solution.py:83
  206.1 11.9 %down_grads.1 = bf16[1376,4096]{1,0:T(8,128)(2,1)} custom-call(s32[2]{0:T(128)} %pad_add_fusion.s, bf16[1376,448]{1,0:T(8,128)(2,1)} %get-tuple-element.35.h_ref, bf16[112,2048]{1,0:T(8,128)(2,1)} %copy-done.3, bf16[112,2048]{1,0:T(8,128)(2,1)} %copy-done.4, bf16[224,2048]{1,0:T(8,128)(2,1)} %copy-done.1, bf16[112,2048]{1,0:T(8,128)(2,1)} %copy-done.7, ...), custom_call_target="tpu_custom_call" | custom-call | flops 5049942016 | bytes 11272192 | tf_op jit(solution)/shard_map/down_grads/pallas_call | solution.py:259
  (123 shorter events, 34.7 us)
Async XLA Ops:
  4.2 16.8 %collective-permute-start.1 = (bf16[128,2048]{1,0:T(8,128)(2,1)S(1)}, bf16[128,2048]{1,0:T(8,128)(2,1)S(1)}, u32[]{:S(2)}, u32[]{:S(2)}) collective-permute-start(bf16[128,2048]{1,0:T(8,128)(2,1)S(1)} %get-tuple-element.40), channel_id=1, source_target_pairs={{0,1},{1,0},{2,3},{3,2},{4,5},{5,4},{6,7},{7,6},{8,9},{9,8},{10,11... | collective-permute-start | bytes 1572872 | tf_op jit(solution)/shard_map/ppermute | solution.py:296
  10.9 44.6 %collective-permute-start.9 = (bf16[56,2048]{1,0:T(8,128)(2,1)}, bf16[56,2048]{1,0:T(8,128)(2,1)S(1)}, u32[]{:S(2)}, u32[]{:S(2)}) collective-permute-start(bf16[56,2048]{1,0:T(8,128)(2,1)} %get-tuple-element.22), channel_id=1, source_target_pairs={{0,8},{1,9},{2,10},{3,11},{4,12},{5,13},{6,14},{7,15},{8,0},{9,1},... | collective-permute-start | bytes 688136 | tf_op jit(solution)/shard_map/ppermute | solution.py:299
  14.7 13.0 %collective-permute-start.11 = (bf16[56,2048]{1,0:T(8,128)(2,1)}, bf16[56,2048]{1,0:T(8,128)(2,1)S(1)}, u32[]{:S(2)}, u32[]{:S(2)}) collective-permute-start(bf16[56,2048]{1,0:T(8,128)(2,1)} %get-tuple-element.23), channel_id=1, source_target_pairs={{0,4},{1,5},{2,6},{3,7},{4,8},{5,9},{6,10},{7,11},{8,12},{9,13},{1... | collective-permute-start | bytes 688136 | tf_op jit(solution)/shard_map/ppermute | solution.py:299
  16.2 22.1 %collective-permute-start.12 = (bf16[56,2048]{1,0:T(8,128)(2,1)}, bf16[56,2048]{1,0:T(8,128)(2,1)S(1)}, u32[]{:S(2)}, u32[]{:S(2)}) collective-permute-start(bf16[56,2048]{1,0:T(8,128)(2,1)} %get-tuple-element.24), channel_id=1, source_target_pairs={{0,12},{1,13},{2,14},{3,15},{4,0},{5,1},{6,2},{7,3},{8,4},{9,5},{1... | collective-permute-start | bytes 688136 | tf_op jit(solution)/shard_map/ppermute | solution.py:299
  18.5 20.0 %collective-permute-start.8 = (bf16[56,2048]{1,0:T(8,128)(2,1)}, bf16[56,2048]{1,0:T(8,128)(2,1)S(1)}, u32[]{:S(2)}, u32[]{:S(2)}) collective-permute-start(bf16[56,2048]{1,0:T(8,128)(2,1)} %get-tuple-element.21), channel_id=1, source_target_pairs={{0,2},{1,3},{2,0},{3,1},{4,6},{5,7},{6,4},{7,5},{8,10},{9,11},{10,... | collective-permute-start | bytes 688136 | tf_op jit(solution)/shard_map/ppermute | solution.py:296
  25.7 16.6 %collective-permute-start.2 = (bf16[56,2048]{1,0:T(8,128)(2,1)}, bf16[56,2048]{1,0:T(8,128)(2,1)S(1)}, u32[]{:S(2)}, u32[]{:S(2)}) collective-permute-start(bf16[56,2048]{1,0:T(8,128)(2,1)} %get-tuple-element.19), channel_id=1, source_target_pairs={{0,2},{1,3},{2,0},{3,1},{4,6},{5,7},{6,4},{7,5},{8,10},{9,11},{10,... | collective-permute-start | bytes 688136 | tf_op jit(solution)/shard_map/ppermute | solution.py:296
  27.7 29.5 %collective-permute-start.3 = (bf16[56,2048]{1,0:T(8,128)(2,1)}, bf16[56,2048]{1,0:T(8,128)(2,1)S(1)}, u32[]{:S(2)}, u32[]{:S(2)}) collective-permute-start(bf16[56,2048]{1,0:T(8,128)(2,1)} %get-tuple-element.20), channel_id=1, source_target_pairs={{0,8},{1,9},{2,10},{3,11},{4,12},{5,13},{6,14},{7,15},{8,0},{9,1},... | collective-permute-start | bytes 688136 | tf_op jit(solution)/shard_map/ppermute | solution.py:299
  38.4 12.3 %collective-permute-start.19 = (bf16[56,2048]{1,0:T(8,128)(2,1)}, bf16[56,2048]{1,0:T(8,128)(2,1)S(1)}, u32[]{:S(2)}, u32[]{:S(2)}) collective-permute-start(bf16[56,2048]{1,0:T(8,128)(2,1)} %get-tuple-element.29), channel_id=1, source_target_pairs={{0,4},{1,5},{2,6},{3,7},{4,8},{5,9},{6,10},{7,11},{8,12},{9,13},{1... | collective-permute-start | bytes 688136 | tf_op jit(solution)/shard_map/ppermute | solution.py:299
  38.5 17.0 %collective-permute-start.20 = (bf16[56,2048]{1,0:T(8,128)(2,1)}, bf16[56,2048]{1,0:T(8,128)(2,1)S(1)}, u32[]{:S(2)}, u32[]{:S(2)}) collective-permute-start(bf16[56,2048]{1,0:T(8,128)(2,1)} %get-tuple-element.30), channel_id=1, source_target_pairs={{0,12},{1,13},{2,14},{3,15},{4,0},{5,1},{6,2},{7,3},{8,4},{9,5},{1... | collective-permute-start | bytes 688136 | tf_op jit(solution)/shard_map/ppermute | solution.py:299
  42.4 40.4 %collective-permute-start.14 = (bf16[112,2048]{1,0:T(8,128)(2,1)S(1)}, bf16[112,2048]{1,0:T(8,128)(2,1)S(1)}, u32[]{:S(2)}, u32[]{:S(2)}) collective-permute-start(bf16[112,2048]{1,0:T(8,128)(2,1)S(1)} %constant_dynamic-update-slice_fusion.4.refs_0_), channel_id=1, source_target_pairs={{0,1},{1,0},{2,3},{3,2},{4,5},{5,4},{6,7},{7,6},{8,9},{9,8},{10,11... | collective-permute-start | bytes 1376264 | tf_op jit(solution)/shard_map/ppermute | solution.py:296
  50.6 13.2 %collective-permute-start.13 = (bf16[112,2048]{1,0:T(8,128)(2,1)S(1)}, bf16[112,2048]{1,0:T(8,128)(2,1)S(1)}, u32[]{:S(2)}, u32[]{:S(2)}) collective-permute-start(bf16[112,2048]{1,0:T(8,128)(2,1)S(1)} %pad_maximum_fusion), channel_id=1, source_target_pairs={{0,2},{1,3},{2,0},{3,1},{4,6},{5,7},{6,4},{7,5},{8,10},{9,11},{10,... | collective-permute-start | bytes 1376264 | tf_op jit(solution)/shard_map/ppermute | solution.py:296
  55.5 49.2 %collective-permute-start.5 = (bf16[112,2048]{1,0:T(8,128)(2,1)S(1)}, bf16[112,2048]{1,0:T(8,128)(2,1)S(1)}, u32[]{:S(2)}, u32[]{:S(2)}) collective-permute-start(bf16[112,2048]{1,0:T(8,128)(2,1)S(1)} %constant_dynamic-update-slice_fusion.refs_0_), channel_id=1, source_target_pairs={{0,1},{1,0},{2,3},{3,2},{4,5},{5,4},{6,7},{7,6},{8,9},{9,8},{10,11... | collective-permute-start | bytes 1376264 | tf_op jit(solution)/shard_map/ppermute | solution.py:296
  55.6 26.6 %collective-permute-start.21 = (bf16[112,2048]{1,0:T(8,128)(2,1)S(1)}, bf16[112,2048]{1,0:T(8,128)(2,1)S(1)}, u32[]{:S(2)}, u32[]{:S(2)}) collective-permute-start(bf16[112,2048]{1,0:T(8,128)(2,1)S(1)} %pad_maximum_fusion.1), channel_id=1, source_target_pairs={{0,2},{1,3},{2,0},{3,1},{4,6},{5,7},{6,4},{7,5},{8,10},{9,11},{10,... | collective-permute-start | bytes 1376264 | tf_op jit(solution)/shard_map/ppermute | solution.py:296
  57.2 18.9 %collective-permute-start.10 = (bf16[56,2048]{1,0:T(8,128)(2,1)S(1)}, bf16[56,2048]{1,0:T(8,128)(2,1)S(1)}, u32[]{:S(2)}, u32[]{:S(2)}) collective-permute-start(bf16[56,2048]{1,0:T(8,128)(2,1)S(1)} %collective-permute-done.9), channel_id=1, source_target_pairs={{0,2},{1,3},{2,0},{3,1},{4,6},{5,7},{6,4},{7,5},{8,10},{9,11},{10,... | collective-permute-start | bytes 688136 | tf_op jit(solution)/shard_map/ppermute | solution.py:296
  63.9 20.0 %collective-permute-start.16 = (bf16[224,2048]{1,0:T(8,128)(2,1)S(1)}, bf16[224,2048]{1,0:T(8,128)(2,1)S(1)}, u32[]{:S(2)}, u32[]{:S(2)}) collective-permute-start(bf16[224,2048]{1,0:T(8,128)(2,1)S(1)} %constant_dynamic-update-slice_fusion.8.refs_2_), channel_id=1, source_target_pairs={{0,1},{1,0},{2,3},{3,2},{4,5},{5,4},{6,7},{7,6},{8,9},{9,8},{10,11... | collective-permute-start | bytes 2752520 | tf_op jit(solution)/shard_map/ppermute | solution.py:296
  82.2 22.6 %collective-permute-start.6 = (bf16[112,2048]{1,0:T(8,128)(2,1)S(1)}, bf16[112,2048]{1,0:T(8,128)(2,1)S(1)}, u32[]{:S(2)}, u32[]{:S(2)}) collective-permute-start(bf16[112,2048]{1,0:T(8,128)(2,1)S(1)} %constant_dynamic-update-slice_fusion.2.refs_1_), channel_id=1, source_target_pairs={{0,1},{1,0},{2,3},{3,2},{4,5},{5,4},{6,7},{7,6},{8,9},{9,8},{10,11... | collective-permute-start | bytes 1376264 | tf_op jit(solution)/shard_map/ppermute | solution.py:296
  82.8 40.7 %collective-permute-start.22 = (bf16[224,2048]{1,0:T(8,128)(2,1)S(1)}, bf16[224,2048]{1,0:T(8,128)(2,1)S(1)}, u32[]{:S(2)}, u32[]{:S(2)}) collective-permute-start(bf16[224,2048]{1,0:T(8,128)(2,1)S(1)} %constant_dynamic-update-slice_fusion.11.refs_0_.refs_2_), channel_id=1, source_target_pairs={{0,1},{1,0},{2,3},{3,2},{4,5},{5,4},{6,7},{7,6},{8,9},{9,8},{10,11... | collective-permute-start | bytes 2752520 | tf_op jit(solution)/shard_map/ppermute | solution.py:296
  123.3 34.8 %collective-permute-start.17 = (bf16[224,2048]{1,0:T(8,128)(2,1)}, bf16[224,2048]{1,0:T(8,128)(2,1)S(1)}, u32[]{:S(2)}, u32[]{:S(2)}) collective-permute-start(bf16[224,2048]{1,0:T(8,128)(2,1)} %partial.5), channel_id=1, source_target_pairs={{0,1},{1,0},{2,3},{3,2},{4,5},{5,4},{6,7},{7,6},{8,9},{9,8},{10,11... | collective-permute-start | bytes 2752520 | tf_op jit(solution)/shard_map/ppermute | solution.py:296
  142.2 19.6 %collective-permute-start.23 = (bf16[224,2048]{1,0:T(8,128)(2,1)}, bf16[224,2048]{1,0:T(8,128)(2,1)S(1)}, u32[]{:S(2)}, u32[]{:S(2)}) collective-permute-start(bf16[224,2048]{1,0:T(8,128)(2,1)} %partial.7), channel_id=1, source_target_pairs={{0,1},{1,0},{2,3},{3,2},{4,5},{5,4},{6,7},{7,6},{8,9},{9,8},{10,11... | collective-permute-start | bytes 2752520 | tf_op jit(solution)/shard_map/ppermute | solution.py:296
  159.7 30.4 %collective-permute-start.18 = (bf16[56,2048]{1,0:T(8,128)(2,1)S(1)}, bf16[56,2048]{1,0:T(8,128)(2,1)S(1)}, u32[]{:S(2)}, u32[]{:S(2)}) collective-permute-start(bf16[56,2048]{1,0:T(8,128)(2,1)S(1)} %slice.83), channel_id=1, source_target_pairs={{0,2},{1,3},{2,0},{3,1},{4,6},{5,7},{6,4},{7,5},{8,10},{9,11},{10,... | collective-permute-start | bytes 688136 | tf_op jit(solution)/shard_map/ppermute | solution.py:296
  162.2 20.6 %collective-permute-start.24 = (bf16[112,2048]{1,0:T(8,128)(2,1)S(1)}, bf16[112,2048]{1,0:T(8,128)(2,1)S(1)}, u32[]{:S(2)}, u32[]{:S(2)}) collective-permute-start(bf16[112,2048]{1,0:T(8,128)(2,1)S(1)} %slice.81), channel_id=1, source_target_pairs={{0,2},{1,3},{2,0},{3,1},{4,6},{5,7},{6,4},{7,5},{8,10},{9,11},{10,... | collective-permute-start | bytes 1376264 | tf_op jit(solution)/shard_map/ppermute | solution.py:296
  173.2 24.2 %collective-permute-start.27 = (bf16[56,2048]{1,0:T(8,128)(2,1)S(1)}, bf16[56,2048]{1,0:T(8,128)(2,1)S(1)}, u32[]{:S(2)}, u32[]{:S(2)}) collective-permute-start(bf16[56,2048]{1,0:T(8,128)(2,1)S(1)} %fusion.1), channel_id=1, source_target_pairs={{0,8},{1,9},{2,10},{3,11},{4,12},{5,13},{6,14},{7,15},{8,0},{9,1},... | collective-permute-start | bytes 688136 | tf_op jit(solution)/shard_map/ppermute | solution.py:299
  183.0 14.4 %collective-permute-start.28 = (bf16[56,2048]{1,0:T(8,128)(2,1)S(1)}, bf16[56,2048]{1,0:T(8,128)(2,1)S(1)}, u32[]{:S(2)}, u32[]{:S(2)}) collective-permute-start(bf16[56,2048]{1,0:T(8,128)(2,1)S(1)} %get-tuple-element.42), channel_id=1, source_target_pairs={{0,4},{1,5},{2,6},{3,7},{4,8},{5,9},{6,10},{7,11},{8,12},{9,13},{1... | collective-permute-start | bytes 688136 | tf_op jit(solution)/shard_map/ppermute | solution.py:299
  206.1 11.9 %collective-permute-start.29 = (bf16[128,2048]{1,0:T(8,128)(2,1)}, bf16[128,2048]{1,0:T(8,128)(2,1)S(1)}, u32[]{:S(2)}, u32[]{:S(2)}) collective-permute-start(bf16[128,2048]{1,0:T(8,128)(2,1)} %get-tuple-element.34), channel_id=1, source_target_pairs={{0,1},{1,0},{2,3},{3,2},{4,5},{5,4},{6,7},{7,6},{8,9},{9,8},{10,11... | collective-permute-start | bytes 1572872 | tf_op jit(solution)/shard_map/ppermute | solution.py:296
  (29 other events, 205.5 us)

commit v2 on v0

v2 whole, which is shorter than its diff:
```python
import jax
import jax.numpy as jnp
from jax import lax
from jax.experimental import pallas as pl
from jax.experimental.pallas import tpu as pltpu
from jax.sharding import PartitionSpec as P

EXPERTS = 4
F32, BF16 = jnp.float32, jnp.bfloat16
NT = (((1,), (1,)), ((), ()))
TN = (((0,), (0,)), ((), ()))
MIB = 1024 * 1024
HBLOCK = 512
LIMIT = 12


def limit(rows):
    return LIMIT if rows <= 448 else 28


def cost(flops, nbytes):
    return pl.CostEstimate(flops=flops, bytes_accessed=nbytes, transcendentals=0)


def on_core(body, info, args, outs, name, flops, limit, deps=(), scratch=(), far=(), hbm=0):
    if hbm:
        args = (*args[:-hbm], *[in_hbm(x) for x in args[-hbm:]])
    n, d = len(args), len(deps) + len(far)

    def run(s, *refs):
        body(s, refs[:n], refs[n + d : n + d + len(outs)], refs[n + d + len(outs) :])

    vmem = pl.BlockSpec(memory_space=pltpu.VMEM)
    nbytes = sum(a.size * a.dtype.itemsize for a in args)
    return pl.pallas_call(
        run,
        in_specs=[pl.BlockSpec(memory_space=pltpu.SMEM)]
        + [vmem] * (n - hbm)
        + [pl.BlockSpec(memory_space=pltpu.HBM)] * hbm
        + [pl.BlockSpec(memory_space=pl.ANY)] * len(deps)
        + [pl.BlockSpec(memory_space=pltpu.HBM)] * len(far),
        out_specs=[vmem] * len(outs),
        out_shape=outs,
        scratch_shapes=scratch,
        compiler_params=pltpu.CompilerParams(vmem_limit_bytes=limit * MIB),
        cost_estimate=cost(flops, nbytes),
        name=name,
    )(info, *args, *deps, *[in_hbm(x) for x in far])


def slot_map(ids, plane, slots, which, capacity):
    rows = ids.shape[0]
    lane = lax.broadcasted_iota(jnp.int32, (rows, 128), 1)
    onehot = jnp.where(ids == lane, 1.0, 0.0)
    row_i = lax.broadcasted_iota(jnp.int32, (rows, rows), 0)
    col_i = lax.broadcasted_iota(jnp.int32, (rows, rows), 1)
    earlier = jnp.where(col_i < row_i, 1.0, 0.0).astype(BF16)
    before = jnp.dot(earlier, onehot.astype(BF16), preferred_element_type=F32)
    slot = jnp.sum(before * onehot, axis=1, keepdims=True).astype(jnp.int32)
    shift = ids - plane
    shift = jnp.where(shift < 0, shift + EXPERTS, shift)
    target = shift * slots + which * capacity + slot
    target = jnp.where(ids < EXPERTS, target, -1)
    place = lax.broadcasted_iota(jnp.int32, (rows, EXPERTS * slots), 1)
    return jnp.where(target == place, 1.0, 0.0).astype(BF16)


def side(s, half, mine):
    return pl.ds(pl.multiple_of((s[1] if mine else 1 - s[1]) * half, 128), half)


def pack(info, ids, other_ids, tokens, grads, received, slots, capacity):
    rows, half = tokens.shape

    def body(s, refs, outs, _):
        ids_ref, oids_ref, tok_ref, grad_ref, got_ref = refs
        p = slot_map(ids_ref[...], s[0], slots, s[1], capacity)
        q = slot_map(oids_ref[...], s[0], slots, 1 - s[1], capacity)
        for i, ref in enumerate((tok_ref, grad_ref)):
            got = lax.dot_general(p, ref[...], TN, preferred_element_type=F32)
            got = got + lax.dot_general(
                q, got_ref[i * rows : (i + 1) * rows], TN, preferred_element_type=F32
            )
            got = got.astype(BF16)
            for d in range(EXPERTS):
                outs[i * EXPERTS + d][...] = got[d * slots : (d + 1) * slots]

    outs = [jax.ShapeDtypeStruct((slots, half), BF16)] * (2 * EXPERTS)
    args = (ids, other_ids, tokens, grads, received)
    made = on_core(body, info, args, outs, "pack", 8 * rows * 4 * slots * half, LIMIT)
    return made[:EXPERTS], made[EXPERTS:]


def unpack(info, ids, other_ids, pieces, slots, capacity, deps):
    rows, width = ids.shape[0], pieces[0].shape[1]

    def body(s, refs, outs, _):
        p = slot_map(refs[0][...], s[0], slots, s[1], capacity)
        q = slot_map(refs[1][...], s[0], slots, 1 - s[1], capacity)
        z = jnp.concatenate([r[...].astype(F32) for r in refs[2:]], axis=0).astype(BF16)
        outs[0][...] = jnp.dot(p, z, preferred_element_type=F32).astype(BF16)
        outs[1][...] = jnp.dot(q, z, preferred_element_type=F32).astype(BF16)

    outs = [jax.ShapeDtypeStruct((rows, width), BF16)] * 2
    args = (ids, other_ids, *pieces)
    flops = 4 * rows * EXPERTS * slots * width
    return on_core(body, info, args, outs, "unpack", flops, LIMIT, (), (), deps)


def stack(to, refs, parts):
    at = 0
    for which, row, rows in parts:
        to[at : at + rows] = refs[which][row : row + rows]
        at += rows


def join(info, arrays, parts, deps=()):
    def body(s, refs, outs, _):
        stack(outs[0], refs, parts)

    rows, width = sum(p[2] for p in parts), arrays[0].shape[1]
    outs = [jax.ShapeDtypeStruct((rows, width), arrays[0].dtype)]
    return on_core(body, info, arrays, outs, "join", 0, LIMIT, deps)[0]


def joined(info, arrays, deps=()):
    return join(info, arrays, [(i, 0, a.shape[0]) for i, a in enumerate(arrays)], deps)


def add_split(info, a, b, parts):
    rows, width = sum(p[2] for p in parts), a.shape[1]
    mid = rows // 2
    each = min(mid, min(p[2] for p in parts))
    pieces = [(row + i, each) for _, row, n in parts for i in range(0, n, each)]

    def body(s, refs, outs, _):
        x, y = refs
        for i, (row, n) in enumerate(pieces):
            cut, at = slice(row, row + n), i * each
            total = x[cut].astype(F32) + y[cut].astype(F32)
            if at < mid:
                outs[1][at : at + n] = total
            else:
                outs[0][at - mid : at - mid + n] = total.astype(BF16)

    outs = [
        jax.ShapeDtypeStruct((rows - mid, width), BF16),
        jax.ShapeDtypeStruct((mid, width), F32),
    ]
    return on_core(body, info, (a, b), outs, "add_split", 2 * a.size, LIMIT)


def add_pieces(info, a, b, count, deps=()):
    rows, width = a.shape
    each = rows // count

    def body(s, refs, outs, _):
        for i, out in enumerate(outs):
            cut = slice(i * each, (i + 1) * each)
            out[...] = (refs[0][cut].astype(F32) + refs[1][cut].astype(F32)).astype(BF16)

    outs = [jax.ShapeDtypeStruct((each, width), BF16)] * count
    return on_core(body, info, (a, b), outs, "add_pieces", 2 * a.size, LIMIT, deps)


def in_vmem(x):
    return pltpu.with_memory_space_constraint(x, pltpu.VMEM)


def in_hbm(x):
    return pltpu.with_memory_space_constraint(x, pltpu.HBM)


def load(info, w, name, deps=()):
    def body(s, w_ref, *rest):
        out_ref, sem = rest[-2:]
        copy = pltpu.make_async_copy(w_ref, out_ref, sem)
        copy.start()
        copy.wait()

    return pl.pallas_call(
        body,
        in_specs=[pl.BlockSpec(memory_space=pltpu.SMEM)]
        + [pl.BlockSpec(memory_space=pltpu.HBM)]
        + [pl.BlockSpec(memory_space=pl.ANY)] * len(deps),
        out_specs=pl.BlockSpec(memory_space=pltpu.VMEM),
        out_shape=pltpu.VMEM(w.shape, w.dtype),
        scratch_shapes=[pltpu.SemaphoreType.DMA],
        compiler_params=pltpu.CompilerParams(vmem_limit_bytes=LIMIT * MIB),
        cost_estimate=cost(0, 2 * w.size * 2),
        name=name,
    )(info, in_hbm(w), *deps)


def cuts_of(size, step):
    return [(at, min(at + step, size)) for at in range(0, size, step)]


def wide_dot(s, own, other, w_ref, cut):
    half = own.shape[1]
    return lax.dot_general(
        own, w_ref[cut, side(s, half, True)], NT, preferred_element_type=F32
    ) + lax.dot_general(other, w_ref[cut, side(s, half, False)], NT, preferred_element_type=F32)


def gate_up(info, own, other, w_gate, w_up, deps=()):
    hidden, model = w_gate.shape
    m = own.shape[0]

    def body(s, refs, outs, _):
        own_ref, other_ref, g_ref, u_ref = refs
        act_ref, dact_ref, hid_ref = outs
        for at, to in cuts_of(hidden, HBLOCK):
            cut = slice(at, to)
            g = wide_dot(s, own_ref[...], other_ref[...], g_ref, cut)
            u = wide_dot(s, own_ref[...], other_ref[...], u_ref, cut)
            sig = jax.nn.sigmoid(g)
            act = g * sig
            act_ref[:, cut] = act
            dact_ref[:, cut] = u * sig * (1.0 + g * (1.0 - sig))
            hid_ref[:, cut] = (act * u).astype(BF16)

    outs = [
        jax.ShapeDtypeStruct((m, hidden), F32),
        jax.ShapeDtypeStruct((m, hidden), F32),
        jax.ShapeDtypeStruct((m, hidden), BF16),
    ]
    args = (own, other, in_vmem(w_gate), in_vmem(w_up))
    return on_core(body, info, args, outs, "gate_up", 4 * m * model * hidden, limit(m), deps)


def hidden_grads(info, own, other, act, dact, w_down, far=()):
    hidden, model = w_down.shape
    m = own.shape[0]
    cuts = cuts_of(hidden, HBLOCK)

    def body(s, refs, outs, scratch):
        own_ref, other_ref, act_ref, dact_ref, d_hbm = refs
        ug_ref, gg_ref = outs
        d_ref, sem = scratch
        copies = [
            pltpu.make_async_copy(
                d_hbm.at[pl.ds(at, to - at)], d_ref.at[j % 2, pl.ds(0, to - at)], sem.at[j]
            )
            for j, (at, to) in enumerate(cuts)
        ]
        for copy in copies[:2]:
            copy.start()
        for j, (at, to) in enumerate(cuts):
            copies[j].wait()
            h = wide_dot(s, own_ref[...], other_ref[...], d_ref.at[j % 2], slice(0, to - at))
            if j + 2 < len(cuts):
                copies[j + 2].start()
            ug_ref[:, at:to] = (h * act_ref[:, at:to]).astype(BF16)
            gg_ref[:, at:to] = (h * dact_ref[:, at:to]).astype(BF16)

    outs = [jax.ShapeDtypeStruct((m, hidden), BF16)] * 2
    args = (own, other, act, dact, w_down)
    scratch = [
        pltpu.VMEM((2, HBLOCK, model), BF16),
        pltpu.SemaphoreType.DMA((len(cuts),)),
    ]
    flops = 2 * m * model * hidden
    return on_core(body, info, args, outs, "hidden_grads", flops, limit(m), (), scratch, far, 1)


def partial(info, up_grad, gate_grad, row0, m, w_gate, w_up, mine, deps=()):
    hidden, model = w_gate.shape
    half = model // 2

    def body(s, refs, outs, _):
        ug_ref, gg_ref, g_ref, u_ref = refs
        rows = slice(row0, row0 + m)
        o = jnp.dot(gg_ref[rows], g_ref[:, side(s, half, mine)], preferred_element_type=F32)
        o = o + jnp.dot(ug_ref[rows], u_ref[:, side(s, half, mine)], preferred_element_type=F32)
        outs[0][...] = o.astype(BF16)

    outs = [jax.ShapeDtypeStruct((m, half), BF16)]
    args = (up_grad, gate_grad, in_vmem(w_gate), in_vmem(w_up))
    flops = 4 * m * half * hidden
    return on_core(body, info, args, outs, "partial", flops, LIMIT, deps)[0]


def down_grads(info, hid, g, mine, filled=None, deps=(), db=1024):
    m, hidden = hid.shape
    half = g.shape[1]
    db = min(db, half)
    steps = half // db

    def column(k, s):
        return (0, k + (s[1] if mine else 1 - s[1]) * steps)

    def body(s, h_ref, g_ref, *refs):
        o = lax.dot_general(h_ref[...], g_ref[...], TN, preferred_element_type=F32)
        refs[-1][...] = o.astype(BF16)

    old = [] if filled is None else [in_hbm(filled)]
    return pl.pallas_call(
        body,
        grid_spec=pltpu.PrefetchScalarGridSpec(
            num_scalar_prefetch=1,
            grid=(steps,),
            in_specs=[pl.BlockSpec((m, hidden), lambda k, s: (0, 0))]
            + [pl.BlockSpec((m, db), lambda k, s: (0, k))]
            + [pl.BlockSpec(memory_space=pltpu.HBM)] * len(old)
            + [pl.BlockSpec(memory_space=pl.ANY)] * len(deps),
            out_specs=pl.BlockSpec((hidden, db), column),
        ),
        out_shape=jax.ShapeDtypeStruct((hidden, 2 * half), BF16),
        input_output_aliases={3: 0} if old else {},
        compiler_params=pltpu.CompilerParams(vmem_limit_bytes=limit(m) * MIB),
        cost_estimate=cost(2 * m * half * hidden, 2 * half * hidden),
        name="down_grads",
    )(info, hid, g, *old, *deps)


def shards(tokens, token_grad_in, expert_ids, gate_weight, up_weight, down_weight):
    devices = lax.axis_size("expert")
    rows, model = tokens.shape
    half = model // 2
    share = devices // EXPERTS
    capacity = (rows + EXPERTS) // (EXPERTS + 1) + 1
    slots = -(-2 * capacity // 8) * 8
    bits = [b for b in range(1, share.bit_length() - 1)]
    index = lax.axis_index("expert")
    core = lax.rem(index, 2)
    info = jnp.stack([index // share, core]).astype(jnp.int32)

    def flip(x, bit):
        return lax.ppermute(x, "expert", [(i, i ^ (1 << bit)) for i in range(devices)])

    def plane_shift(x, d):
        return lax.ppermute(
            x, "expert", [(i, (i + d * share) % devices) for i in range(devices)]
        )

    def after(x, *others):
        return lax.optimization_barrier((x, *others))[0]

    def spread(parts):
        for bit in bits:
            parts = parts + [flip(p, bit) for p in parts]
        return parts

    def fold(halves):
        for i, bit in enumerate(reversed(bits)):
            out, kept = halves
            got = flip(out, bit)
            if i + 1 < len(bits):
                halves = add_split(info, kept, got, [(0, 0, kept.shape[0])])
        return add_pieces(info, kept, got, 1)[0]

    w_gate = jnp.swapaxes(gate_weight[0], 0, 1)
    w_up = jnp.swapaxes(up_weight[0], 0, 1)
    w_down = down_weight[0]

    away, here = (1 - core) * half, core * half
    sent = jnp.concatenate(
        [
            lax.dynamic_slice_in_dim(tokens, away, half, 1),
            lax.dynamic_slice_in_dim(token_grad_in, away, half, 1),
        ],
        axis=0,
    )
    received = flip(sent, 0)
    other_ids = flip(expert_ids, 0)
    tok, grad = pack(
        info,
        expert_ids,
        other_ids,
        lax.dynamic_slice_in_dim(tokens, here, half, 1),
        lax.dynamic_slice_in_dim(token_grad_in, here, half, 1),
        received,
        slots,
        capacity,
    )

    t1, t3, t2 = plane_shift(tok[1], 1), plane_shift(tok[3], 3), plane_shift(tok[2], 2)
    near = spread([joined(info, [tok[0], grad[0]])])
    w_gate = load(info, w_gate, "load_gate", (tok[0],))
    w_up = load(info, w_up, "load_up", (tok[0],))
    chips = len(near)
    n = chips * slots

    def by_plane(x, near_row, deps):
        rows = [(c, near_row, slots) for c in range(chips)]
        rows += [(chips + c, i * slots, slots) for i in range(3) for c in range(chips)]
        return join(info, [*near, *x], rows, deps)

    t = joined(info, [t2, t1, t3], (w_gate, w_up, *near))
    g2 = plane_shift(after(grad[2], t), 2)
    g1 = plane_shift(after(grad[1], t), 1)
    g3 = plane_shift(after(grad[3], t), 3)
    t = by_plane(spread([t]), 0, (g1, g2, g3))
    t_other = flip(t, 0)
    g = spread([joined(info, [g2, g1, g3], (t,))])
    act, dact, hid = gate_up(info, t, t_other, w_gate, w_up)
    g = by_plane(g, slots, (hid,))
    g_other = flip(g, 0)
    down_grad = down_grads(info, hid, g, True)
    up_grad, gate_grad = hidden_grads(info, g, g_other, act, dact, w_down, (down_grad,))

    def back(row0, mine, deps=()):
        return partial(info, up_grad, gate_grad, row0, 2 * n, w_gate, w_up, mine, deps)

    def plane(i):
        return [(0, i * n, n)]

    got = flip(back(0, False), 0)
    kept = back(0, True)
    sum2 = add_split(info, kept, got, plane(1))
    sum0 = add_split(info, kept, got, plane(0))
    got = flip(back(2 * n, False, (sum2[0],)), 0)
    far2 = fold(sum2)
    piece2 = plane_shift(far2, EXPERTS - 2)
    kept = back(2 * n, True)
    sum1 = add_split(info, kept, got, plane(0))
    sum3 = add_split(info, kept, got, plane(1))
    piece1 = plane_shift(fold(sum1), EXPERTS - 1)
    down_grad = down_grads(info, hid, g_other, False, down_grad, (sum3[0], far2))
    piece3 = plane_shift(fold(sum3), EXPERTS - 3)
    piece0 = fold(sum0)
    pieces = {0: piece0, 1: piece1, 2: piece2, 3: piece3}
    mine, theirs = unpack(
        info,
        expert_ids,
        other_ids,
        [pieces[d] for d in range(EXPERTS)],
        slots,
        capacity,
        (down_grad,),
    )
    got = flip(theirs, 0)
    input_grad = jnp.where(
        core == 0,
        jnp.concatenate([mine, got], axis=1),
        jnp.concatenate([got, mine], axis=1),
    )
    return (input_grad, down_grad[None])


def solution(mesh):
    placed = (
        P(("groups", "expert"), None),
        P(("groups", "expert"), None),
        P(("groups", "expert"), None),
        P("expert", None, None),
        P("expert", None, None),
        P("expert", None, None),
    )
    return jax.shard_map(
        shards,
        mesh=mesh,
        in_specs=placed,
        out_specs=(P(("groups", "expert"), None), P(("groups", "expert"), None, None)),
        check_vma=False,
    )
```

time: 355 us -> 143 us (0.40)
  the two profiles are of different devices: /device:TPU:13 before, /device:TPU:0 now
where the time goes in v2:
time: 143 us
  Pallas kernels  68 us (48%)
  starting transfers between devices  37.8 us (26%)
  waiting for transfers between devices  32.8 us (23%)
  local copies, waits for them, and re-layouts  1.82 us (1%)
    pallas_call x21, Pallas kernels, on_core(): pl.pallas_call(run, in_specs=[pl.BlockSpec(memory_space=pltpu.SMEM)] + [v...  47.3 us
    ppermute x9, starting transfers between devices, plane_shift(): lax.ppermute(x, 'expert', [(i, (i + d * share) % devices) for i in range(...  26.5 us
    ppermute x9, waiting for transfers between devices, plane_shift(): lax.ppermute(x, 'expert', [(i, (i + d * share) % devices) for i in range(...  16.6 us
    ppermute x14, waiting for transfers between devices, flip(): lax.ppermute(x, 'expert', [(i, i ^ 1 << bit) for i in range(devices)])  16.2 us
    ppermute x14, starting transfers between devices, flip(): lax.ppermute(x, 'expert', [(i, i ^ 1 << bit) for i in range(devices)])  11.3 us
    pallas_call x2, Pallas kernels, down_grads(): pl.pallas_call(body, grid_spec=pltpu.PrefetchScalarGridSpec(num_scalar_pr...  11.2 us
    pallas_call x2, Pallas kernels, load(): pl.pallas_call(body, in_specs=[pl.BlockSpec(memory_space=pltpu.SMEM)] + [...  9.5 us
  transfers between devices with their start and end apart: 23, of which 13 were waited for; matrix products, arithmetic and copies ran while one was open for 0% of the time, Pallas kernels for 32%

profile of v2, /device:TPU:0, one launch (start us, length us, event | category | flops | bytes accessed | tf_op | source)
XLA Modules:
  0.0 142.7 jit_solution(8157013043922692198)
XLA Ops:
  5.4 2.1 %pack.1 = (bf16[56,2048]{1,0:T(8,128)(2,1)S(1)}, bf16[56,2048]{1,0:T(8,128)(2,1)S(1)}, bf16[56,2048]{1,0:T(8,128)(2,1)S(1)}, bf16[56,2048]{1,0:T(8,128)(2,1)S(1)...) custom-call(s32[2]{0:T(128)S(1)} %pad_add_fusion.s, ...), custom_call_target="tpu_custom_call" | custom-call | flops 469762048 | bytes 2098176 | tf_op jit(solution)/shard_map/pack/pallas_call | solution.py:35
  8.0 2.9 %collective-permute-start.2 = (bf16[112,2048]{1,0:T(8,128)(2,1)S(1)}, bf16[112,2048]{1,0:T(8,128)(2,1)S(1)}, u32[]{:S(2)}, u32[]{:S(2)}) collective-permute-start(bf16[112,2048]{1,0:T(8,128)(2,1)S(1)} %join.5.refs_5_.refs_0_), channel_id=1, source_target_pairs={{0,2},{1,3},{2,0},{3,1},{4,6},{5,7},{6,4},{7,5},{8,10},{9,11},{10,... | collective-permute-start | bytes 1376264 | tf_op jit(solution)/shard_map/ppermute | solution.py:330
  11.0 2.6 %collective-permute-start.3 = (bf16[56,2048]{1,0:T(8,128)(2,1)S(1)}, bf16[56,2048]{1,0:T(8,128)(2,1)S(1)}, u32[]{:S(2)}, u32[]{:S(2)}) collective-permute-start(bf16[56,2048]{1,0:T(8,128)(2,1)S(1)} %get-tuple-element.31), channel_id=1, source_target_pairs={{0,8},{1,9},{2,10},{3,11},{4,12},{5,13},{6,14},{7,15},{8,0},{9,1},... | collective-permute-start | bytes 688136 | tf_op jit(solution)/shard_map/ppermute | solution.py:333
  15.1 2.2 %collective-permute-start.5 = (bf16[56,2048]{1,0:T(8,128)(2,1)S(1)}, bf16[56,2048]{1,0:T(8,128)(2,1)S(1)}, u32[]{:S(2)}, u32[]{:S(2)}) collective-permute-start(bf16[56,2048]{1,0:T(8,128)(2,1)S(1)} %get-tuple-element.33), channel_id=1, source_target_pairs={{0,12},{1,13},{2,14},{3,15},{4,0},{5,1},{6,2},{7,3},{8,4},{9,5},{1... | collective-permute-start | bytes 688136 | tf_op jit(solution)/shard_map/ppermute | solution.py:333
  17.4 4.8 %load_up.1.refs_4_.refs_3_ = bf16[1376,4096]{1,0:T(8,128)(2,1)S(1)} custom-call(s32[2]{0:T(128)S(1)} %pad_add_fusion.s, bf16[1376,4096]{1,0:T(8,128)(2,1)} %bitcast.11, bf16[56,2048]{1,0:T(8,128)(2,1)S(1)} %get-tuple-element.28.refs_0_.rest_0_), custom_call_target="tpu_custom_call" | custom-call | bytes 22544384 | tf_op jit(solution)/shard_map/load_up/pallas_call | solution.py:181
  22.2 4.8 %load_gate.1.refs_3_.refs_2_ = bf16[1376,4096]{1,0:T(8,128)(2,1)S(1)} custom-call(s32[2]{0:T(128)S(1)} %pad_add_fusion.s, bf16[1376,4096]{1,0:T(8,128)(2,1)} %bitcast.12, bf16[56,2048]{1,0:T(8,128)(2,1)S(1)} %get-tuple-element.28.refs_0_.rest_0_), custom_call_target="tpu_custom_call" | custom-call | bytes 22544384 | tf_op jit(solution)/shard_map/load_gate/pallas_call | solution.py:181
  26.9 3.3 %collective-permute-done.3.refs_0_ = bf16[56,2048]{1,0:T(8,128)(2,1)S(1)} collective-permute-done((bf16[56,2048]{1,0:T(8,128)(2,1)S(1)}, bf16[56,2048]{1,0:T(8,128)(2,1)S(1)}, u32[]{:S(2)}, u32[]{:S(2)}) %collective-permute-start.3) | collective-permute-done | bytes 229408 | tf_op jit(solution)/shard_map/ppermute | solution.py:333
  31.8 6.0 %collective-permute-start.6 = (bf16[56,2048]{1,0:T(8,128)(2,1)S(1)}, bf16[56,2048]{1,0:T(8,128)(2,1)S(1)}, u32[]{:S(2)}, u32[]{:S(2)}) collective-permute-start(bf16[56,2048]{1,0:T(8,128)(2,1)S(1)} %get-tuple-element.34), channel_id=1, source_target_pairs={{0,8},{1,9},{2,10},{3,11},{4,12},{5,13},{6,14},{7,15},{8,0},{9,1},... | collective-permute-start | bytes 688136 | tf_op jit(solution)/shard_map/ppermute | solution.py:333
  37.8 3.8 %collective-permute-start.8 = (bf16[56,2048]{1,0:T(8,128)(2,1)S(1)}, bf16[56,2048]{1,0:T(8,128)(2,1)S(1)}, u32[]{:S(2)}, u32[]{:S(2)}) collective-permute-start(bf16[56,2048]{1,0:T(8,128)(2,1)S(1)} %get-tuple-element.38), channel_id=1, source_target_pairs={{0,12},{1,13},{2,14},{3,15},{4,0},{5,1},{6,2},{7,3},{8,4},{9,5},{1... | collective-permute-start | bytes 688136 | tf_op jit(solution)/shard_map/ppermute | solution.py:333
  41.6 11.8 %collective-permute-done.6.refs_5_.refs_0_ = bf16[56,2048]{1,0:T(8,128)(2,1)S(1)} collective-permute-done((bf16[56,2048]{1,0:T(8,128)(2,1)S(1)}, bf16[56,2048]{1,0:T(8,128)(2,1)S(1)}, u32[]{:S(2)}, u32[]{:S(2)}) %collective-permute-start.6) | collective-permute-done | bytes 229408 | tf_op jit(solution)/shard_map/ppermute | solution.py:333
  58.8 12.5 %gate_up.1 = (f32[448,1376]{1,0:T(8,128)S(1)}, f32[448,1376]{1,0:T(8,128)S(1)}, bf16[448,1376]{1,0:T(8,128)(2,1)S(1)}) custom-call(s32[2]{0:T(128)S(1)} %pad_add_fusion.s, bf16[448,2048]{1,0:T(8,128)(2,1)S(1)} %join.7.refs_3_.refs_0_, bf16[448,2048]{1,0:T(8,128)(2,1)S(1)} %collective-permute-done.11.refs_1_, ...), custom_call_target="tpu_custom_call" | custom-call | flops 10099884032 | bytes 26214400 | tf_op jit(solution)/shard_map/gate_up/pallas_call | solution.py:35
  71.4 2.2 %collective-permute-done.10.refs_3_ = bf16[168,2048]{1,0:T(8,128)(2,1)S(1)} collective-permute-done((bf16[168,2048]{1,0:T(8,128)(2,1)S(1)}, bf16[168,2048]{1,0:T(8,128)(2,1)S(1)}, u32[]{:S(2)}, u32[]{:S(2)}) %collective-permute-start.10) | collective-permute-done | bytes 688160 | tf_op jit(solution)/shard_map/ppermute | solution.py:330
  74.3 5.6 %down_grads.2.refs_5_.refs_0_ = bf16[1376,4096]{1,0:T(8,128)(2,1)} custom-call(s32[2]{0:T(128)S(1)} %pad_add_fusion.s, bf16[448,1376]{1,0:T(8,128)(2,1)S(1)} %get-tuple-element.39.refs_4_.h_ref, bf16[448,2048]{1,0:T(8,128)(2,1)S(1)} %join.9.g_ref.refs_0_), custom_call_target="tpu_custom_call" | custom-call | flops 2524971008 | bytes 5636096 | tf_op jit(solution)/shard_map/down_grads/pallas_call | solution.py:298
  79.9 9.1 %hidden_grads.1 = (bf16[448,1376]{1,0:T(8,128)(2,1)S(1)}, bf16[448,1376]{1,0:T(8,128)(2,1)S(1)}) custom-call(s32[2]{0:T(128)S(1)} %pad_add_fusion.s, bf16[448,2048]{1,0:T(8,128)(2,1)S(1)} %join.9.g_ref.refs_0_, bf16[448,2048]{1,0:T(8,128)(2,1)S(1)} %collective-permute-done.12.refs_1_.g_ref, f32[448,1376]{1,0:T(8,128)S(1)} %get-tuple-element.40.refs_2_, ...), custom_call_target="tpu_custom_call" | custom-call | flops 5049942016 | bytes 19873792 | tf_op jit(solution)/shard_map/hidden_grads/pallas_call | solution.py:35
  88.9 3.5 %partial.5 = bf16[224,2048]{1,0:T(8,128)(2,1)S(1)} custom-call(s32[2]{0:T(128)S(1)} %pad_add_fusion.s, bf16[448,1376]{1,0:T(8,128)(2,1)S(1)} %get-tuple-element.42.refs_0_, bf16[448,1376]{1,0:T(8,128)(2,1)S(1)} %get-tuple-element.43.refs_1_, bf16[1376,4096]{1,0:T(8,128)(2,1)S(1)} %load_gate.1.refs_3_.refs_2_, bf16[1376,4096]{1,0:T(8,128)(2,1)S(1)} %load_up.1.refs_4_.refs_3_), custom_call_target="tpu_custom_call" | custom-call | flops 2524971008 | bytes 25010176 | tf_op jit(solution)/shard_map/partial/pallas_call | solution.py:35
  93.1 3.5 %partial.4.refs_0_ = bf16[224,2048]{1,0:T(8,128)(2,1)S(1)} custom-call(s32[2]{0:T(128)S(1)} %pad_add_fusion.s, bf16[448,1376]{1,0:T(8,128)(2,1)S(1)} %get-tuple-element.42.refs_0_, bf16[448,1376]{1,0:T(8,128)(2,1)S(1)} %get-tuple-element.43.refs_1_, bf16[1376,4096]{1,0:T(8,128)(2,1)S(1)} %load_gate.1.refs_3_.refs_2_, ...), custom_call_target="tpu_custom_call" | custom-call | flops 2524971008 | bytes 25010176 | tf_op jit(solution)/shard_map/partial/pallas_call | solution.py:35
  97.3 3.5 %partial.7 = bf16[224,2048]{1,0:T(8,128)(2,1)S(1)} custom-call(s32[2]{0:T(128)S(1)} %pad_add_fusion.s, bf16[448,1376]{1,0:T(8,128)(2,1)S(1)} %get-tuple-element.42.refs_0_, bf16[448,1376]{1,0:T(8,128)(2,1)S(1)} %get-tuple-element.43.refs_1_, bf16[1376,4096]{1,0:T(8,128)(2,1)S(1)} %load_gate.1.refs_3_.refs_2_, bf16[1376,4096]{1,0:T(8,128)(2,1)S(1)} %load_up.1.refs_4_.refs_3_, ...), custom_call_target="tpu_custom_call" | custom-call | flops 2524971008 | bytes 25010176 | tf_op jit(solution)/shard_map/partial/pallas_call | solution.py:35
  100.9 3.8 %partial.6.refs_0_ = bf16[224,2048]{1,0:T(8,128)(2,1)S(1)} custom-call(s32[2]{0:T(128)S(1)} %pad_add_fusion.s, bf16[448,1376]{1,0:T(8,128)(2,1)S(1)} %get-tuple-element.42.refs_0_, bf16[448,1376]{1,0:T(8,128)(2,1)S(1)} %get-tuple-element.43.refs_1_, bf16[1376,4096]{1,0:T(8,128)(2,1)S(1)} %load_gate.1.refs_3_.refs_2_, ...), custom_call_target="tpu_custom_call" | custom-call | flops 2524971008 | bytes 25010176 | tf_op jit(solution)/shard_map/partial/pallas_call | solution.py:35
  110.9 2.2 %collective-permute-done.18.refs_1_ = bf16[56,2048]{1,0:T(8,128)(2,1)S(1)} collective-permute-done((bf16[56,2048]{1,0:T(8,128)(2,1)S(1)}, bf16[56,2048]{1,0:T(8,128)(2,1)S(1)}, u32[]{:S(2)}, u32[]{:S(2)}) %collective-permute-start.18) | collective-permute-done | bytes 229408 | tf_op jit(solution)/shard_map/ppermute | solution.py:330
  113.7 3.4 %collective-permute-start.19 = (bf16[56,2048]{1,0:T(8,128)(2,1)S(1)}, bf16[56,2048]{1,0:T(8,128)(2,1)S(1)}, u32[]{:S(2)}, u32[]{:S(2)}) collective-permute-start(bf16[56,2048]{1,0:T(8,128)(2,1)S(1)} %add_pieces.6.refs_2_), channel_id=1, source_target_pairs={{0,8},{1,9},{2,10},{3,11},{4,12},{5,13},{6,14},{7,15},{8,0},{9,1},... | collective-permute-start | bytes 688136 | tf_op jit(solution)/shard_map/ppermute | solution.py:333
  118.7 4.3 %collective-permute-done.16.refs_1_ = bf16[56,2048]{1,0:T(8,128)(2,1)S(1)} collective-permute-done((bf16[56,2048]{1,0:T(8,128)(2,1)S(1)}, bf16[56,2048]{1,0:T(8,128)(2,1)S(1)}, u32[]{:S(2)}, u32[]{:S(2)}) %collective-permute-start.16) | collective-permute-done | bytes 229408 | tf_op jit(solution)/shard_map/ppermute | solution.py:330
  123.6 2.5 %collective-permute-start.17 = (bf16[56,2048]{1,0:T(8,128)(2,1)S(1)}, bf16[56,2048]{1,0:T(8,128)(2,1)S(1)}, u32[]{:S(2)}, u32[]{:S(2)}) collective-permute-start(bf16[56,2048]{1,0:T(8,128)(2,1)S(1)} %add_pieces.5), channel_id=1, source_target_pairs={{0,12},{1,13},{2,14},{3,15},{4,0},{5,1},{6,2},{7,3},{8,4},{9,5},{1... | collective-permute-start | bytes 688136 | tf_op jit(solution)/shard_map/ppermute | solution.py:333
  128.1 4.4 %collective-permute-start.21 = (bf16[56,2048]{1,0:T(8,128)(2,1)S(1)}, bf16[56,2048]{1,0:T(8,128)(2,1)S(1)}, u32[]{:S(2)}, u32[]{:S(2)}) collective-permute-start(bf16[56,2048]{1,0:T(8,128)(2,1)S(1)} %add_pieces.7), channel_id=1, source_target_pairs={{0,4},{1,5},{2,6},{3,7},{4,8},{5,9},{6,10},{7,11},{8,12},{9,13},{1... | collective-permute-start | bytes 688136 | tf_op jit(solution)/shard_map/ppermute | solution.py:333
  132.5 5.6 %down_grads.3.refs_6_ = bf16[1376,4096]{1,0:T(8,128)(2,1)} custom-call(s32[2]{0:T(128)S(1)} %pad_add_fusion.s, bf16[448,1376]{1,0:T(8,128)(2,1)S(1)} %get-tuple-element.39.refs_4_.h_ref, bf16[448,2048]{1,0:T(8,128)(2,1)S(1)} %collective-permute-done.12.refs_1_.g_ref, bf16[1376,4096]{1,0:T(8,128)(2,1)} %down_grads.2.refs_5_.refs_0_, ...), custom_call_target="tpu_custom_call", output_to_operand_aliasing={{}: (3, {})} | custom-call | flops 2524971008 | bytes 5636096 | tf_op jit(solution)/shard_map/down_grads/pallas_call | solution.py:298
  (54 shorter events, 31.3 us)
Async XLA Ops:
  2.3 0.7 copy-start
  2.5 2.9 %collective-permute-start.1 = (bf16[256,2048]{1,0:T(8,128)(2,1)S(1)}, bf16[256,2048]{1,0:T(8,128)(2,1)S(1)}, u32[]{:S(2)}, u32[]{:S(2)}) collective-permute-start(bf16[256,2048]{1,0:T(8,128)(2,1)S(1)} %pad_maximum_fusion), channel_id=1, source_target_pairs={{0,1},{1,0},{2,3},{3,2},{4,5},{5,4},{6,7},{7,6},{8,9},{9,8},{10,11... | collective-permute-start | bytes 3145736 | tf_op jit(solution)/shard_map/ppermute | solution.py:330
  3.1 2.2 %collective-permute-start = (s32[128,1]{1,0:T(8,128)S(1)}, s32[128,1]{1,0:T(8,128)S(1)}, u32[]{:S(2)}, u32[]{:S(2)}) collective-permute-start(s32[128,1]{1,0:T(8,128)S(1)} %copy.11.refs_0_), channel_id=1, source_target_pairs={{0,1},{1,0},{2,3},{3,2},{4,5},{5,4},{6,7},{7,6},{8,9},{9,8},{10,11... | collective-permute-start | bytes 1544 | tf_op jit(solution)/shard_map/ppermute | solution.py:330
  8.0 22.6 %collective-permute-start.2 = (bf16[112,2048]{1,0:T(8,128)(2,1)S(1)}, bf16[112,2048]{1,0:T(8,128)(2,1)S(1)}, u32[]{:S(2)}, u32[]{:S(2)}) collective-permute-start(bf16[112,2048]{1,0:T(8,128)(2,1)S(1)} %join.5.refs_5_.refs_0_), channel_id=1, source_target_pairs={{0,2},{1,3},{2,0},{3,1},{4,6},{5,7},{6,4},{7,5},{8,10},{9,11},{10,... | collective-permute-start | bytes 1376264 | tf_op jit(solution)/shard_map/ppermute | solution.py:330
  11.0 19.3 %collective-permute-start.3 = (bf16[56,2048]{1,0:T(8,128)(2,1)S(1)}, bf16[56,2048]{1,0:T(8,128)(2,1)S(1)}, u32[]{:S(2)}, u32[]{:S(2)}) collective-permute-start(bf16[56,2048]{1,0:T(8,128)(2,1)S(1)} %get-tuple-element.31), channel_id=1, source_target_pairs={{0,8},{1,9},{2,10},{3,11},{4,12},{5,13},{6,14},{7,15},{8,0},{9,1},... | collective-permute-start | bytes 688136 | tf_op jit(solution)/shard_map/ppermute | solution.py:333
  13.6 16.7 %collective-permute-start.4 = (bf16[56,2048]{1,0:T(8,128)(2,1)S(1)}, bf16[56,2048]{1,0:T(8,128)(2,1)S(1)}, u32[]{:S(2)}, u32[]{:S(2)}) collective-permute-start(bf16[56,2048]{1,0:T(8,128)(2,1)S(1)} %get-tuple-element.32), channel_id=1, source_target_pairs={{0,4},{1,5},{2,6},{3,7},{4,8},{5,9},{6,10},{7,11},{8,12},{9,13},{1... | collective-permute-start | bytes 688136 | tf_op jit(solution)/shard_map/ppermute | solution.py:333
  15.1 15.5 %collective-permute-start.5 = (bf16[56,2048]{1,0:T(8,128)(2,1)S(1)}, bf16[56,2048]{1,0:T(8,128)(2,1)S(1)}, u32[]{:S(2)}, u32[]{:S(2)}) collective-permute-start(bf16[56,2048]{1,0:T(8,128)(2,1)S(1)} %get-tuple-element.33), channel_id=1, source_target_pairs={{0,12},{1,13},{2,14},{3,15},{4,0},{5,1},{6,2},{7,3},{8,4},{9,5},{1... | collective-permute-start | bytes 688136 | tf_op jit(solution)/shard_map/ppermute | solution.py:333
  31.3 23.0 %collective-permute-start.9 = (bf16[168,2048]{1,0:T(8,128)(2,1)S(1)}, bf16[168,2048]{1,0:T(8,128)(2,1)S(1)}, u32[]{:S(2)}, u32[]{:S(2)}) collective-permute-start(bf16[168,2048]{1,0:T(8,128)(2,1)S(1)} %join.6.refs_2_), channel_id=1, source_target_pairs={{0,2},{1,3},{2,0},{3,1},{4,6},{5,7},{6,4},{7,5},{8,10},{9,11},{10,... | collective-permute-start | bytes 2064392 | tf_op jit(solution)/shard_map/ppermute | solution.py:330
  31.8 21.6 %collective-permute-start.6 = (bf16[56,2048]{1,0:T(8,128)(2,1)S(1)}, bf16[56,2048]{1,0:T(8,128)(2,1)S(1)}, u32[]{:S(2)}, u32[]{:S(2)}) collective-permute-start(bf16[56,2048]{1,0:T(8,128)(2,1)S(1)} %get-tuple-element.34), channel_id=1, source_target_pairs={{0,8},{1,9},{2,10},{3,11},{4,12},{5,13},{6,14},{7,15},{8,0},{9,1},... | collective-permute-start | bytes 688136 | tf_op jit(solution)/shard_map/ppermute | solution.py:333
  37.7 15.6 %collective-permute-start.7 = (bf16[56,2048]{1,0:T(8,128)(2,1)S(1)}, bf16[56,2048]{1,0:T(8,128)(2,1)S(1)}, u32[]{:S(2)}, u32[]{:S(2)}) collective-permute-start(bf16[56,2048]{1,0:T(8,128)(2,1)S(1)} %get-tuple-element.36), channel_id=1, source_target_pairs={{0,4},{1,5},{2,6},{3,7},{4,8},{5,9},{6,10},{7,11},{8,12},{9,13},{1... | collective-permute-start | bytes 688136 | tf_op jit(solution)/shard_map/ppermute | solution.py:333
  37.8 16.5 %collective-permute-start.8 = (bf16[56,2048]{1,0:T(8,128)(2,1)S(1)}, bf16[56,2048]{1,0:T(8,128)(2,1)S(1)}, u32[]{:S(2)}, u32[]{:S(2)}) collective-permute-start(bf16[56,2048]{1,0:T(8,128)(2,1)S(1)} %get-tuple-element.38), channel_id=1, source_target_pairs={{0,12},{1,13},{2,14},{3,15},{4,0},{5,1},{6,2},{7,3},{8,4},{9,5},{1... | collective-permute-start | bytes 688136 | tf_op jit(solution)/shard_map/ppermute | solution.py:333
  55.0 3.9 %collective-permute-start.11 = (bf16[448,2048]{1,0:T(8,128)(2,1)S(1)}, bf16[448,2048]{1,0:T(8,128)(2,1)S(1)}, u32[]{:S(2)}, u32[]{:S(2)}) collective-permute-start(bf16[448,2048]{1,0:T(8,128)(2,1)S(1)} %join.7.refs_3_.refs_0_), channel_id=1, source_target_pairs={{0,1},{1,0},{2,3},{3,2},{4,5},{5,4},{6,7},{7,6},{8,9},{9,8},{10,11... | collective-permute-start | bytes 5505032 | tf_op jit(solution)/shard_map/ppermute | solution.py:330
  55.6 17.9 %collective-permute-start.10 = (bf16[168,2048]{1,0:T(8,128)(2,1)S(1)}, bf16[168,2048]{1,0:T(8,128)(2,1)S(1)}, u32[]{:S(2)}, u32[]{:S(2)}) collective-permute-start(bf16[168,2048]{1,0:T(8,128)(2,1)S(1)} %join.8.refs_2_), channel_id=1, source_target_pairs={{0,2},{1,3},{2,0},{3,1},{4,6},{5,7},{6,4},{7,5},{8,10},{9,11},{10,... | collective-permute-start | bytes 2064392 | tf_op jit(solution)/shard_map/ppermute | solution.py:330
  74.2 5.7 %collective-permute-start.12 = (bf16[448,2048]{1,0:T(8,128)(2,1)S(1)}, bf16[448,2048]{1,0:T(8,128)(2,1)S(1)}, u32[]{:S(2)}, u32[]{:S(2)}) collective-permute-start(bf16[448,2048]{1,0:T(8,128)(2,1)S(1)} %join.9.g_ref.refs_0_), channel_id=1, source_target_pairs={{0,1},{1,0},{2,3},{3,2},{4,5},{5,4},{6,7},{7,6},{8,9},{9,8},{10,11... | collective-permute-start | bytes 5505032 | tf_op jit(solution)/shard_map/ppermute | solution.py:330
  92.5 4.1 %collective-permute-start.13 = (bf16[224,2048]{1,0:T(8,128)(2,1)S(1)}, bf16[224,2048]{1,0:T(8,128)(2,1)S(1)}, u32[]{:S(2)}, u32[]{:S(2)}) collective-permute-start(bf16[224,2048]{1,0:T(8,128)(2,1)S(1)} %partial.5), channel_id=1, source_target_pairs={{0,1},{1,0},{2,3},{3,2},{4,5},{5,4},{6,7},{7,6},{8,9},{9,8},{10,11... | collective-permute-start | bytes 2752520 | tf_op jit(solution)/shard_map/ppermute | solution.py:330
  100.8 6.7 %collective-permute-start.15 = (bf16[224,2048]{1,0:T(8,128)(2,1)S(1)}, bf16[224,2048]{1,0:T(8,128)(2,1)S(1)}, u32[]{:S(2)}, u32[]{:S(2)}) collective-permute-start(bf16[224,2048]{1,0:T(8,128)(2,1)S(1)} %partial.7), channel_id=1, source_target_pairs={{0,1},{1,0},{2,3},{3,2},{4,5},{5,4},{6,7},{7,6},{8,9},{9,8},{10,11... | collective-permute-start | bytes 2752520 | tf_op jit(solution)/shard_map/ppermute | solution.py:330
  104.7 8.5 %collective-permute-start.18 = (bf16[56,2048]{1,0:T(8,128)(2,1)S(1)}, bf16[56,2048]{1,0:T(8,128)(2,1)S(1)}, u32[]{:S(2)}, u32[]{:S(2)}) collective-permute-start(bf16[56,2048]{1,0:T(8,128)(2,1)S(1)} %get-tuple-element.46.refs_4_), channel_id=1, source_target_pairs={{0,2},{1,3},{2,0},{3,1},{4,6},{5,7},{6,4},{7,5},{8,10},{9,11},{10,... | collective-permute-start | bytes 688136 | tf_op jit(solution)/shard_map/ppermute | solution.py:330
  106.9 11.1 %collective-permute-start.14 = (bf16[56,2048]{1,0:T(8,128)(2,1)S(1)}, bf16[56,2048]{1,0:T(8,128)(2,1)S(1)}, u32[]{:S(2)}, u32[]{:S(2)}) collective-permute-start(bf16[56,2048]{1,0:T(8,128)(2,1)S(1)} %get-tuple-element.45), channel_id=1, source_target_pairs={{0,2},{1,3},{2,0},{3,1},{4,6},{5,7},{6,4},{7,5},{8,10},{9,11},{10,... | collective-permute-start | bytes 688136 | tf_op jit(solution)/shard_map/ppermute | solution.py:330
  108.1 14.8 %collective-permute-start.16 = (bf16[56,2048]{1,0:T(8,128)(2,1)S(1)}, bf16[56,2048]{1,0:T(8,128)(2,1)S(1)}, u32[]{:S(2)}, u32[]{:S(2)}) collective-permute-start(bf16[56,2048]{1,0:T(8,128)(2,1)S(1)} %get-tuple-element.48), channel_id=1, source_target_pairs={{0,2},{1,3},{2,0},{3,1},{4,6},{5,7},{6,4},{7,5},{8,10},{9,11},{10,... | collective-permute-start | bytes 688136 | tf_op jit(solution)/shard_map/ppermute | solution.py:330
  110.4 17.1 %collective-permute-start.20 = (bf16[56,2048]{1,0:T(8,128)(2,1)S(1)}, bf16[56,2048]{1,0:T(8,128)(2,1)S(1)}, u32[]{:S(2)}, u32[]{:S(2)}) collective-permute-start(bf16[56,2048]{1,0:T(8,128)(2,1)S(1)} %get-tuple-element.51.refs_1_), channel_id=1, source_target_pairs={{0,2},{1,3},{2,0},{3,1},{4,6},{5,7},{6,4},{7,5},{8,10},{9,11},{10,... | collective-permute-start | bytes 688136 | tf_op jit(solution)/shard_map/ppermute | solution.py:330
  113.7 24.3 %collective-permute-start.19 = (bf16[56,2048]{1,0:T(8,128)(2,1)S(1)}, bf16[56,2048]{1,0:T(8,128)(2,1)S(1)}, u32[]{:S(2)}, u32[]{:S(2)}) collective-permute-start(bf16[56,2048]{1,0:T(8,128)(2,1)S(1)} %add_pieces.6.refs_2_), channel_id=1, source_target_pairs={{0,8},{1,9},{2,10},{3,11},{4,12},{5,13},{6,14},{7,15},{8,0},{9,1},... | collective-permute-start | bytes 688136 | tf_op jit(solution)/shard_map/ppermute | solution.py:333
  123.6 14.5 %collective-permute-start.17 = (bf16[56,2048]{1,0:T(8,128)(2,1)S(1)}, bf16[56,2048]{1,0:T(8,128)(2,1)S(1)}, u32[]{:S(2)}, u32[]{:S(2)}) collective-permute-start(bf16[56,2048]{1,0:T(8,128)(2,1)S(1)} %add_pieces.5), channel_id=1, source_target_pairs={{0,12},{1,13},{2,14},{3,15},{4,0},{5,1},{6,2},{7,3},{8,4},{9,5},{1... | collective-permute-start | bytes 688136 | tf_op jit(solution)/shard_map/ppermute | solution.py:333
  128.1 10.1 %collective-permute-start.21 = (bf16[56,2048]{1,0:T(8,128)(2,1)S(1)}, bf16[56,2048]{1,0:T(8,128)(2,1)S(1)}, u32[]{:S(2)}, u32[]{:S(2)}) collective-permute-start(bf16[56,2048]{1,0:T(8,128)(2,1)S(1)} %add_pieces.7), channel_id=1, source_target_pairs={{0,4},{1,5},{2,6},{3,7},{4,8},{5,9},{6,10},{7,11},{8,12},{9,13},{1... | collective-permute-start | bytes 688136 | tf_op jit(solution)/shard_map/ppermute | solution.py:333
  139.5 2.0 %collective-permute-start.22 = (bf16[128,2048]{1,0:T(8,128)(2,1)S(1)}, bf16[128,2048]{1,0:T(8,128)(2,1)S(1)}, u32[]{:S(2)}, u32[]{:S(2)}) collective-permute-start(bf16[128,2048]{1,0:T(8,128)(2,1)S(1)} %get-tuple-element.53), channel_id=1, source_target_pairs={{0,1},{1,0},{2,3},{3,2},{4,5},{5,4},{6,7},{7,6},{8,9},{9,8},{10,11... | collective-permute-start | bytes 1572872 | tf_op jit(solution)/shard_map/ppermute | solution.py:330

commit v3 on v2

--- a/solution.py
+++ b/solution.py
@@ -11,7 +11,7 @@
 TN = (((0,), (0,)), ((), ()))
 MIB = 1024 * 1024
 HBLOCK = 512
-LIMIT = 12
+LIMIT = 8
 
 
 def limit(rows):
@@ -31,7 +31,7 @@
         body(s, refs[:n], refs[n + d : n + d + len(outs)], refs[n + d + len(outs) :])
 
     vmem = pl.BlockSpec(memory_space=pltpu.VMEM)
-    nbytes = sum(a.size * a.dtype.itemsize for a in args)
+    nbytes = sum(a.size * a.dtype.itemsize for a in args) if flops else 1
     return pl.pallas_call(
         run,
         in_specs=[pl.BlockSpec(memory_space=pltpu.SMEM)]
@@ -69,26 +69,51 @@
     return pl.ds(pl.multiple_of((s[1] if mine else 1 - s[1]) * half, 128), half)
 
 
-def pack(info, ids, other_ids, tokens, grads, received, slots, capacity):
-    rows, half = tokens.shape
-
-    def body(s, refs, outs, _):
-        ids_ref, oids_ref, tok_ref, grad_ref, got_ref = refs
+def halves(info, tokens, grads):
+    rows, model = tokens.shape
+    half = model // 2
+
+    def body(s, refs, outs, scratch):
+        copies = [
+            pltpu.make_async_copy(
+                ref.at[:, side(s, half, mine)],
+                outs[0 if mine else 1].at[pl.ds(i * rows, rows)],
+                scratch[0].at[2 * i + mine],
+            )
+            for i, ref in enumerate(refs)
+            for mine in (False, True)
+        ]
+        for copy in copies:
+            copy.start()
+        for copy in copies:
+            copy.wait()
+
+    outs = [jax.ShapeDtypeStruct((2 * rows, half), BF16)] * 2
+    scratch = [pltpu.SemaphoreType.DMA((4,))]
+    return on_core(body, info, (tokens, grads), outs, "halves", 0, LIMIT, (), scratch, (), 2)
+
+
+def pack(info, ids, other_ids, mine, received, slots, capacity):
+    rows, half = mine.shape[0] // 2, mine.shape[1]
+
+    def body(s, refs, outs, _):
+        ids_ref, oids_ref, mine_ref, got_ref = refs
         p = slot_map(ids_ref[...], s[0], slots, s[1], capacity)
         q = slot_map(oids_ref[...], s[0], slots, 1 - s[1], capacity)
-        for i, ref in enumerate((tok_ref, grad_ref)):
-            got = lax.dot_general(p, ref[...], TN, preferred_element_type=F32)
-            got = got + lax.dot_general(
-                q, got_ref[i * rows : (i + 1) * rows], TN, preferred_element_type=F32
-            )
+        for i in range(2):
+            cut = slice(i * rows, (i + 1) * rows)
+            got = lax.dot_general(p, mine_ref[cut], TN, preferred_element_type=F32)
+            got = got + lax.dot_general(q, got_ref[cut], TN, preferred_element_type=F32)
             got = got.astype(BF16)
-            for d in range(EXPERTS):
-                outs[i * EXPERTS + d][...] = got[d * slots : (d + 1) * slots]
-
-    outs = [jax.ShapeDtypeStruct((slots, half), BF16)] * (2 * EXPERTS)
-    args = (ids, other_ids, tokens, grads, received)
+            outs[0][i * slots : (i + 1) * slots] = got[:slots]
+            for d in range(1, EXPERTS):
+                outs[i * (EXPERTS - 1) + d][...] = got[d * slots : (d + 1) * slots]
+
+    outs = [jax.ShapeDtypeStruct((2 * slots, half), BF16)]
+    outs += [jax.ShapeDtypeStruct((slots, half), BF16)] * (2 * EXPERTS - 2)
+    args = (ids, other_ids, mine, received)
     made = on_core(body, info, args, outs, "pack", 8 * rows * 4 * slots * half, LIMIT)
-    return made[:EXPERTS], made[EXPERTS:]
+    return made[0], (None, *made[1:EXPERTS]), (None, *made[EXPERTS:])
 
 
 def unpack(info, ids, other_ids, pieces, slots, capacity, deps):
@@ -127,40 +152,39 @@
     return join(info, arrays, [(i, 0, a.shape[0]) for i, a in enumerate(arrays)], deps)
 
 
-def add_split(info, a, b, parts):
-    rows, width = sum(p[2] for p in parts), a.shape[1]
-    mid = rows // 2
-    each = min(mid, min(p[2] for p in parts))
-    pieces = [(row + i, each) for _, row, n in parts for i in range(0, n, each)]
-
-    def body(s, refs, outs, _):
-        x, y = refs
-        for i, (row, n) in enumerate(pieces):
-            cut, at = slice(row, row + n), i * each
-            total = x[cut].astype(F32) + y[cut].astype(F32)
+def add_split(info, a, b, parts, deps=()):
+    rows, width = sum(p[1] for p in parts), a.shape[1]
+    mid, size = rows // 2, b[0].shape[0]
+    each = min(mid, size, min(p[1] for p in parts))
+    pieces = [row + i for row, n in parts for i in range(0, n, each)]
+
+    def body(s, refs, outs, _):
+        for i, row in enumerate(pieces):
+            at, y = i * each, refs[1 + row // size]
+            total = refs[0][row : row + each].astype(F32)
+            total = total + y[row % size : row % size + each].astype(F32)
             if at < mid:
-                outs[1][at : at + n] = total
+                outs[1][at : at + each] = total
             else:
-                outs[0][at - mid : at - mid + n] = total.astype(BF16)
+                outs[0][at - mid : at - mid + each] = total.astype(BF16)
 
     outs = [
         jax.ShapeDtypeStruct((rows - mid, width), BF16),
         jax.ShapeDtypeStruct((mid, width), F32),
     ]
-    return on_core(body, info, (a, b), outs, "add_split", 2 * a.size, LIMIT)
-
-
-def add_pieces(info, a, b, count, deps=()):
-    rows, width = a.shape
-    each = rows // count
+    return on_core(body, info, (a, *b), outs, "add_split", 0, LIMIT, deps)
+
+
+def add_rounded(info, a, b, count, deps=(), far=()):
+    each = a.shape[0] // count
 
     def body(s, refs, outs, _):
         for i, out in enumerate(outs):
             cut = slice(i * each, (i + 1) * each)
             out[...] = (refs[0][cut].astype(F32) + refs[1][cut].astype(F32)).astype(BF16)
 
-    outs = [jax.ShapeDtypeStruct((each, width), BF16)] * count
-    return on_core(body, info, (a, b), outs, "add_pieces", 2 * a.size, LIMIT, deps)
+    outs = [jax.ShapeDtypeStruct((each, a.shape[1]), BF16)] * count
+    return on_core(body, info, (a, b), outs, "add_rounded", 0, LIMIT, deps, (), far)
 
 
 def in_vmem(x):
@@ -229,70 +253,58 @@
     return on_core(body, info, args, outs, "gate_up", 4 * m * model * hidden, limit(m), deps)
 
 
-def hidden_grads(info, own, other, act, dact, w_down, far=()):
+def hidden_grads(info, own, other, row0, act, dact, w_down, deps=()):
     hidden, model = w_down.shape
     m = own.shape[0]
-    cuts = cuts_of(hidden, HBLOCK)
-
-    def body(s, refs, outs, scratch):
-        own_ref, other_ref, act_ref, dact_ref, d_hbm = refs
+
+    def body(s, refs, outs, _):
+        own_ref, other_ref, act_ref, dact_ref, d_ref = refs
         ug_ref, gg_ref = outs
-        d_ref, sem = scratch
-        copies = [
-            pltpu.make_async_copy(
-                d_hbm.at[pl.ds(at, to - at)], d_ref.at[j % 2, pl.ds(0, to - at)], sem.at[j]
-            )
-            for j, (at, to) in enumerate(cuts)
-        ]
-        for copy in copies[:2]:
-            copy.start()
-        for j, (at, to) in enumerate(cuts):
-            copies[j].wait()
-            h = wide_dot(s, own_ref[...], other_ref[...], d_ref.at[j % 2], slice(0, to - at))
-            if j + 2 < len(cuts):
-                copies[j + 2].start()
-            ug_ref[:, at:to] = (h * act_ref[:, at:to]).astype(BF16)
-            gg_ref[:, at:to] = (h * dact_ref[:, at:to]).astype(BF16)
+        rows = slice(row0, row0 + m)
+        for at, to in cuts_of(hidden, HBLOCK):
+            h = wide_dot(s, own_ref[...], other_ref[...], d_ref, slice(at, to))
+            ug_ref[:, at:to] = (h * act_ref[rows, at:to]).astype(BF16)
+            gg_ref[:, at:to] = (h * dact_ref[rows, at:to]).astype(BF16)
 
     outs = [jax.ShapeDtypeStruct((m, hidden), BF16)] * 2
-    args = (own, other, act, dact, w_down)
-    scratch = [
-        pltpu.VMEM((2, HBLOCK, model), BF16),
-        pltpu.SemaphoreType.DMA((len(cuts),)),
-    ]
+    args = (own, other, act, dact, in_vmem(w_down))
     flops = 2 * m * model * hidden
-    return on_core(body, info, args, outs, "hidden_grads", flops, limit(m), (), scratch, far, 1)
-
-
-def partial(info, up_grad, gate_grad, row0, m, w_gate, w_up, mine, deps=()):
+    return on_core(body, info, args, outs, "hidden_grads", flops, LIMIT, deps)
+
+
+def partial(info, up_grad, gate_grad, row0, m, w_gate, w_up, mine, deps=(), pieces=1):
     hidden, model = w_gate.shape
     half = model // 2
+    each = m // pieces
 
     def body(s, refs, outs, _):
         ug_ref, gg_ref, g_ref, u_ref = refs
         rows = slice(row0, row0 + m)
         o = jnp.dot(gg_ref[rows], g_ref[:, side(s, half, mine)], preferred_element_type=F32)
         o = o + jnp.dot(ug_ref[rows], u_ref[:, side(s, half, mine)], preferred_element_type=F32)
-        outs[0][...] = o.astype(BF16)
-
-    outs = [jax.ShapeDtypeStruct((m, half), BF16)]
+        for i, out in enumerate(outs):
+            out[...] = o[i * each : (i + 1) * each].astype(BF16)
+
+    outs = [jax.ShapeDtypeStruct((each, half), BF16)] * pieces
     args = (up_grad, gate_grad, in_vmem(w_gate), in_vmem(w_up))
-    flops = 4 * m * half * hidden
-    return on_core(body, info, args, outs, "partial", flops, LIMIT, deps)[0]
-
-
-def down_grads(info, hid, g, mine, filled=None, deps=(), db=1024):
+    return on_core(body, info, args, outs, "partial", 0, LIMIT, deps)
+
+
+def down_grads(info, hid, gs, mine, filled=None, deps=(), db=512):
     m, hidden = hid.shape
-    half = g.shape[1]
+    half = gs[0].shape[1]
     db = min(db, half)
     steps = half // db
+    parts = [(i, 0, g.shape[0]) for i, g in enumerate(gs)]
 
     def column(k, s):
         return (0, k + (s[1] if mine else 1 - s[1]) * steps)
 
-    def body(s, h_ref, g_ref, *refs):
+    def body(s, h_ref, *refs):
+        o_ref, g_ref = refs[-2:]
+        stack(g_ref, refs[: len(gs)], parts)
         o = lax.dot_general(h_ref[...], g_ref[...], TN, preferred_element_type=F32)
-        refs[-1][...] = o.astype(BF16)
+        o_ref[...] = o.astype(BF16)
 
     old = [] if filled is None else [in_hbm(filled)]
     return pl.pallas_call(
@@ -301,17 +313,18 @@
             num_scalar_prefetch=1,
             grid=(steps,),
             in_specs=[pl.BlockSpec((m, hidden), lambda k, s: (0, 0))]
-            + [pl.BlockSpec((m, db), lambda k, s: (0, k))]
+            + [pl.BlockSpec((g.shape[0], db), lambda k, s: (0, k)) for g in gs]
             + [pl.BlockSpec(memory_space=pltpu.HBM)] * len(old)
             + [pl.BlockSpec(memory_space=pl.ANY)] * len(deps),
             out_specs=pl.BlockSpec((hidden, db), column),
+            scratch_shapes=[pltpu.VMEM((m, db), BF16)],
         ),
         out_shape=jax.ShapeDtypeStruct((hidden, 2 * half), BF16),
-        input_output_aliases={3: 0} if old else {},
+        input_output_aliases={2 + len(gs): 0} if old else {},
         compiler_params=pltpu.CompilerParams(vmem_limit_bytes=limit(m) * MIB),
-        cost_estimate=cost(2 * m * half * hidden, 2 * half * hidden),
+        cost_estimate=cost(0, 1),
         name="down_grads",
-    )(info, hid, g, *old, *deps)
+    )(info, hid, *gs, *old, *deps)
 
 
 def shards(tokens, token_grad_in, expert_ids, gate_weight, up_weight, down_weight):
@@ -342,84 +355,78 @@
             parts = parts + [flip(p, bit) for p in parts]
         return parts
 
-    def fold(halves):
+    def fold(halves, count, deps=(), far=()):
         for i, bit in enumerate(reversed(bits)):
             out, kept = halves
             got = flip(out, bit)
             if i + 1 < len(bits):
-                halves = add_split(info, kept, got, [(0, 0, kept.shape[0])])
-        return add_pieces(info, kept, got, 1)[0]
+                halves = add_split(info, kept, [got], [(0, kept.shape[0])])
+        return add_rounded(info, kept, got, count, deps, far)
 
     w_gate = jnp.swapaxes(gate_weight[0], 0, 1)
     w_up = jnp.swapaxes(up_weight[0], 0, 1)
     w_down = down_weight[0]
 
-    away, here = (1 - core) * half, core * half
-    sent = jnp.concatenate(
-        [
-            lax.dynamic_slice_in_dim(tokens, away, half, 1),
-            lax.dynamic_slice_in_dim(token_grad_in, away, half, 1),
-        ],
-        axis=0,
-    )
+    mine, sent = halves(info, tokens, token_grad_in)
     received = flip(sent, 0)
     other_ids = flip(expert_ids, 0)
-    tok, grad = pack(
-        info,
-        expert_ids,
-        other_ids,
-        lax.dynamic_slice_in_dim(tokens, here, half, 1),
-        lax.dynamic_slice_in_dim(token_grad_in, here, half, 1),
-        received,
-        slots,
-        capacity,
-    )
+    near, tok, grad = pack(info, expert_ids, other_ids, mine, received, slots, capacity)
 
     t1, t3, t2 = plane_shift(tok[1], 1), plane_shift(tok[3], 3), plane_shift(tok[2], 2)
-    near = spread([joined(info, [tok[0], grad[0]])])
-    w_gate = load(info, w_gate, "load_gate", (tok[0],))
-    w_up = load(info, w_up, "load_up", (tok[0],))
+    near = spread([near])
+    w_up = load(info, w_up, "load_up", (tok[1],))
+    w_gate = load(info, w_gate, "load_gate", (tok[1], w_up))
     chips = len(near)
     n = chips * slots
 
     def by_plane(x, near_row, deps):
         rows = [(c, near_row, slots) for c in range(chips)]
-        rows += [(chips + c, i * slots, slots) for i in range(3) for c in range(chips)]
+        count = x[0].shape[0] // slots
+        rows += [(chips + c, i * slots, slots) for i in range(count) for c in range(chips)]
         return join(info, [*near, *x], rows, deps)
 
-    t = joined(info, [t2, t1, t3], (w_gate, w_up, *near))
-    g2 = plane_shift(after(grad[2], t), 2)
+    t = joined(info, [t1, t3, t2], (w_gate, w_up, *near))
     g1 = plane_shift(after(grad[1], t), 1)
     g3 = plane_shift(after(grad[3], t), 3)
-    t = by_plane(spread([t]), 0, (g1, g2, g3))
+    t = by_plane(spread([t]), 0, (g1, g3))
     t_other = flip(t, 0)
-    g = spread([joined(info, [g2, g1, g3], (t,))])
+    g2 = plane_shift(after(grad[2], t), 2)
+    g13 = spread([joined(info, [g1, g3], (t,))])
     act, dact, hid = gate_up(info, t, t_other, w_gate, w_up)
-    g = by_plane(g, slots, (hid,))
-    g_other = flip(g, 0)
-    down_grad = down_grads(info, hid, g, True)
-    up_grad, gate_grad = hidden_grads(info, g, g_other, act, dact, w_down, (down_grad,))
-
-    def back(row0, mine, deps=()):
-        return partial(info, up_grad, gate_grad, row0, 2 * n, w_gate, w_up, mine, deps)
-
-    def plane(i):
-        return [(0, i * n, n)]
-
-    got = flip(back(0, False), 0)
-    kept = back(0, True)
-    sum2 = add_split(info, kept, got, plane(1))
-    sum0 = add_split(info, kept, got, plane(0))
-    got = flip(back(2 * n, False, (sum2[0],)), 0)
-    far2 = fold(sum2)
+
+    g13 = by_plane(g13, slots, (hid, g2))
+    g13_other = flip(g13, 0)
+    g2 = spread([after(g2, g13)])
+    up_grad, gate_grad = hidden_grads(info, g13, g13_other, 0, act, dact, w_down)
+    g2 = joined(info, g2, (up_grad,))
+    g2_other = flip(g2, 0)
+
+    def back(row0, rows, mine, deps=()):
+        return partial(info, up_grad, gate_grad, row0, rows, w_gate, w_up, mine, deps)[0]
+
+    got = flip(back(n, 2 * n, False, (g2,)), 0)
+    kept = back(n, 2 * n, True)
+    rows13 = [(p * n + c * slots, slots) for c in range(chips) for p in range(2)]
+    sum13 = add_split(info, kept, [got], rows13)
+
+    up_grad2, gate_grad2 = hidden_grads(
+        info, g2, g2_other, 3 * n, act, dact, w_down, (sum13[0],)
+    )
+    halves2 = (up_grad2, gate_grad2, 0, n, w_gate, w_up)
+    got = [flip(x, 0) for x in partial(info, *halves2, False, (), chips)]
+    kept = partial(info, *halves2, True)[0]
+    far1, far3 = fold(sum13, 2)
+    sum2 = add_split(info, kept, got, [(0, n)], (far1,))
+    piece1, piece3 = plane_shift(far1, EXPERTS - 1), plane_shift(far3, EXPERTS - 3)
+
+    got = flip(back(0, n, False, (sum2[0],)), 0)
+    kept = back(0, n, True)
+    (far2,) = fold(sum2, 1, (kept,))
     piece2 = plane_shift(far2, EXPERTS - 2)
-    kept = back(2 * n, True)
-    sum1 = add_split(info, kept, got, plane(0))
-    sum3 = add_split(info, kept, got, plane(1))
-    piece1 = plane_shift(fold(sum1), EXPERTS - 1)
-    down_grad = down_grads(info, hid, g_other, False, down_grad, (sum3[0], far2))
-    piece3 = plane_shift(fold(sum3), EXPERTS - 3)
-    piece0 = fold(sum0)
+    sum0 = add_split(info, kept, [got], [(0, n)])
+    down_grad = down_grads(info, hid, [g13, g2], True, None, (far2, sum0[0]))
+    down_grad = down_grads(info, hid, [g13_other, g2_other], False, down_grad, (piece1, piece3))
+    (piece0,) = fold(sum0, 1)
     pieces = {0: piece0, 1: piece1, 2: piece2, 3: piece3}
     mine, theirs = unpack(
         info,

time: 143 us -> 135 us (0.944)
  starting transfers between devices: 37.8 us -> 18.8 us
  waiting for transfers between devices: 32.8 us -> 41.6 us
  Pallas kernels: 68 us -> 72.3 us
  local copies, waits for them, and re-layouts: 1.82 us -> 0.16 us
    ppermute x9, starting transfers between devices: 26.5 us -> 9.26 us  [plane_shift(): lax.ppermute(x, 'expert', [(i, (i + d * share) % devices) for i in range(...]
    ppermute x9, waiting for transfers between devices: 16.6 us -> 25.1 us  [plane_shift(): lax.ppermute(x, 'expert', [(i, (i + d * share) % devices) for i in range(...]
    pallas_call x21 -> x23, Pallas kernels: 47.3 us -> 51.4 us  [on_core(): pl.pallas_call(run, in_specs=[pl.BlockSpec(memory_space=pltpu.SMEM)] + [v...]
    ppermute x14 -> x17, starting transfers between devices: 11.3 us -> 9.52 us  [flip(): lax.ppermute(x, 'expert', [(i, i ^ 1 << bit) for i in range(devices)])]
    dynamic_slice x1 -> x0, local copies, waits for them, and re-layouts: 1.68 us -> none  [shards(): lax.dynamic_slice_in_dim(token_grad_in, away, half, 1)]
    ppermute x14 -> x17, waiting for transfers between devices: 16.2 us -> 16.5 us  [flip(): lax.ppermute(x, 'expert', [(i, i ^ 1 << bit) for i in range(devices)])]
  transfers between devices with their start and end apart: 23 -> 26, of which waited for: 13 -> 11; matrix products, arithmetic and copies ran while one was open for 0% -> 0% of each run, Pallas kernels for 32% -> 43%
where the time goes in v3:
time: 135 us
  Pallas kernels  72.3 us (54%)
  waiting for transfers between devices  41.6 us (31%)
  starting transfers between devices  18.8 us (14%)
    pallas_call x23, Pallas kernels, on_core(): pl.pallas_call(run, in_specs=[pl.BlockSpec(memory_space=pltpu.SMEM)] + [v...  51.4 us
    ppermute x9, waiting for transfers between devices, plane_shift(): lax.ppermute(x, 'expert', [(i, (i + d * share) % devices) for i in range(...  25.1 us
    ppermute x17, waiting for transfers between devices, flip(): lax.ppermute(x, 'expert', [(i, i ^ 1 << bit) for i in range(devices)])  16.5 us
    pallas_call x2, Pallas kernels, down_grads(): pl.pallas_call(body, grid_spec=pltpu.PrefetchScalarGridSpec(num_scalar_pr...  11.4 us
    ppermute x17, starting transfers between devices, flip(): lax.ppermute(x, 'expert', [(i, i ^ 1 << bit) for i in range(devices)])  9.52 us
    pallas_call x2, Pallas kernels, load(): pl.pallas_call(body, in_specs=[pl.BlockSpec(memory_space=pltpu.SMEM)] + [...  9.5 us
    ppermute x9, starting transfers between devices, plane_shift(): lax.ppermute(x, 'expert', [(i, (i + d * share) % devices) for i in range(...  9.26 us
  transfers between devices with their start and end apart: 26, of which 11 were waited for; matrix products, arithmetic and copies ran while one was open for 0% of the time, Pallas kernels for 43%

profile of v3, /device:TPU:0, one launch (start us, length us, event | category | flops | bytes accessed | tf_op | source)
XLA Modules:
  0.0 135.2 jit_solution(12640054798188652435)
XLA Ops:
  3.6 2.1 %collective-permute-done.refs_1_ = s32[128,1]{1,0:T(8,128)S(1)} collective-permute-done((s32[128,1]{1,0:T(8,128)S(1)}, s32[128,1]{1,0:T(8,128)S(1)}, u32[]{:S(2)}, u32[]{:S(2)}) %collective-permute-start) | collective-permute-done | bytes 544 | tf_op jit(solution)/shard_map/ppermute | solution.py:343
  7.8 2.9 %collective-permute-start.2 = (bf16[112,2048]{1,0:T(8,128)(2,1)S(1)}, bf16[112,2048]{1,0:T(8,128)(2,1)S(1)}, u32[]{:S(2)}, u32[]{:S(2)}) collective-permute-start(bf16[112,2048]{1,0:T(8,128)(2,1)S(1)} %get-tuple-element.36.refs_5_.refs_0_), channel_id=1, source_target_pairs={{0,2},{1,3},{2,0},{3,1},{4,6},{5,7},{6,4},{7,5},{8,10},{9,11},{10,... | collective-permute-start | bytes 1376264 | tf_op jit(solution)/shard_map/ppermute | solution.py:343
  12.4 2.2 %collective-permute-start.4 = (bf16[56,2048]{1,0:T(8,128)(2,1)S(1)}, bf16[56,2048]{1,0:T(8,128)(2,1)S(1)}, u32[]{:S(2)}, u32[]{:S(2)}) collective-permute-start(bf16[56,2048]{1,0:T(8,128)(2,1)S(1)} %get-tuple-element.39), channel_id=1, source_target_pairs={{0,12},{1,13},{2,14},{3,15},{4,0},{5,1},{6,2},{7,3},{8,4},{9,5},{1... | collective-permute-start | bytes 688136 | tf_op jit(solution)/shard_map/ppermute | solution.py:346
  15.4 4.8 %load_up.1.rest_1_.refs_4_.refs_3_ = bf16[1376,4096]{1,0:T(8,128)(2,1)S(1)} custom-call(s32[2]{0:T(128)S(1)} %pad_add_fusion.s, bf16[1376,4096]{1,0:T(8,128)(2,1)} %bitcast.17, bf16[56,2048]{1,0:T(8,128)(2,1)S(1)} %get-tuple-element.38.rest_0_), custom_call_target="tpu_custom_call" | custom-call | bytes 22544384 | tf_op jit(solution)/shard_map/load_up/pallas_call | solution.py:205
  20.2 4.8 %load_gate.1.refs_3_.refs_2_ = bf16[1376,4096]{1,0:T(8,128)(2,1)S(1)} custom-call(s32[2]{0:T(128)S(1)} %pad_add_fusion.s, bf16[1376,4096]{1,0:T(8,128)(2,1)} %bitcast.18, bf16[56,2048]{1,0:T(8,128)(2,1)S(1)} %get-tuple-element.38.rest_0_, bf16[1376,4096]{1,0:T(8,128)(2,1)S(1)} %load_up.1.rest_1_.refs_4_.refs_3_), custom_call_target="tpu_custom_call" | custom-call | bytes 22544384 | tf_op jit(solution)/shard_map/load_gate/pallas_call | solution.py:205
  24.9 9.8 %collective-permute-done.5.refs_2_ = bf16[56,2048]{1,0:T(8,128)(2,1)S(1)} collective-permute-done((bf16[56,2048]{1,0:T(8,128)(2,1)S(1)}, bf16[56,2048]{1,0:T(8,128)(2,1)S(1)}, u32[]{:S(2)}, u32[]{:S(2)}) %collective-permute-start.5) | collective-permute-done | bytes 229408 | tf_op jit(solution)/shard_map/ppermute | solution.py:346
  37.9 10.1 %collective-permute-done.7.refs_5_.refs_1_ = bf16[56,2048]{1,0:T(8,128)(2,1)S(1)} collective-permute-done((bf16[56,2048]{1,0:T(8,128)(2,1)S(1)}, bf16[56,2048]{1,0:T(8,128)(2,1)S(1)}, u32[]{:S(2)}, u32[]{:S(2)}) %collective-permute-start.7) | collective-permute-done | bytes 229408 | tf_op jit(solution)/shard_map/ppermute | solution.py:346
  48.1 4.7 %collective-permute-done.8.refs_3_ = bf16[168,2048]{1,0:T(8,128)(2,1)S(1)} collective-permute-done((bf16[168,2048]{1,0:T(8,128)(2,1)S(1)}, bf16[168,2048]{1,0:T(8,128)(2,1)S(1)}, u32[]{:S(2)}, u32[]{:S(2)}) %collective-permute-start.8) | collective-permute-done | bytes 688160 | tf_op jit(solution)/shard_map/ppermute | solution.py:343
  54.8 2.5 %collective-permute-done.10.refs_1_ = bf16[448,2048]{1,0:T(8,128)(2,1)S(1)} collective-permute-done((bf16[448,2048]{1,0:T(8,128)(2,1)S(1)}, bf16[448,2048]{1,0:T(8,128)(2,1)S(1)}, u32[]{:S(2)}, u32[]{:S(2)}) %collective-permute-start.10) | collective-permute-done | bytes 1835040 | tf_op jit(solution)/shard_map/ppermute | solution.py:343
  57.3 12.5 %gate_up.1 = (f32[448,1376]{1,0:T(8,128)S(1)}, f32[448,1376]{1,0:T(8,128)S(1)}, bf16[448,1376]{1,0:T(8,128)(2,1)S(1)}) custom-call(s32[2]{0:T(128)S(1)} %pad_add_fusion.s, bf16[448,2048]{1,0:T(8,128)(2,1)S(1)} %join.6.refs_2_.refs_0_, bf16[448,2048]{1,0:T(8,128)(2,1)S(1)} %collective-permute-done.10.refs_1_, ...), custom_call_target="tpu_custom_call" | custom-call | flops 10099884032 | bytes 26214400 | tf_op jit(solution)/shard_map/gate_up/pallas_call | solution.py:35
  71.2 2.5 %collective-permute-done.12.refs_1_.refs_0_ = bf16[336,2048]{1,0:T(8,128)(2,1)S(1)} collective-permute-done((bf16[336,2048]{1,0:T(8,128)(2,1)S(1)}, bf16[336,2048]{1,0:T(8,128)(2,1)S(1)}, u32[]{:S(2)}, u32[]{:S(2)}) %collective-permute-start.12) | collective-permute-done | bytes 1376288 | tf_op jit(solution)/shard_map/ppermute | solution.py:343
  73.7 5.2 %hidden_grads.2 = (bf16[336,1376]{1,0:T(8,128)(2,1)S(1)}, bf16[336,1376]{1,0:T(8,128)(2,1)S(1)}) custom-call(s32[2]{0:T(128)S(1)} %pad_add_fusion.s, bf16[336,2048]{1,0:T(8,128)(2,1)S(1)} %join.8.refs_0_, bf16[336,2048]{1,0:T(8,128)(2,1)S(1)} %collective-permute-done.12.refs_1_.refs_0_, f32[448,1376]{1,0:T(8,128)S(1)} %get-tuple-element.47.refs_2_, ...), custom_call_target="tpu_custom_call" | custom-call | flops 3787456512 | bytes 18956288 | tf_op jit(solution)/shard_map/hidden_grads/pallas_call | solution.py:35
  79.5 3.6 %partial.8 = bf16[224,2048]{1,0:T(8,128)(2,1)S(1)} custom-call(s32[2]{0:T(128)S(1)} %pad_add_fusion.s, bf16[336,1376]{1,0:T(8,128)(2,1)S(1)} %get-tuple-element.49.refs_0_.refs_2_, bf16[336,1376]{1,0:T(8,128)(2,1)S(1)} %get-tuple-element.50.refs_1_, bf16[1376,4096]{1,0:T(8,128)(2,1)S(1)} %load_gate.1.refs_3_.refs_2_, ...), custom_call_target="tpu_custom_call" | custom-call | bytes 1 | tf_op jit(solution)/shard_map/partial/pallas_call | solution.py:35
  83.7 3.6 %partial.7.refs_0_ = bf16[224,2048]{1,0:T(8,128)(2,1)S(1)} custom-call(s32[2]{0:T(128)S(1)} %pad_add_fusion.s, bf16[336,1376]{1,0:T(8,128)(2,1)S(1)} %get-tuple-element.49.refs_0_.refs_2_, bf16[336,1376]{1,0:T(8,128)(2,1)S(1)} %get-tuple-element.50.refs_1_, bf16[1376,4096]{1,0:T(8,128)(2,1)S(1)} %load_gate.1.refs_3_.refs_2_, ...), custom_call_target="tpu_custom_call" | custom-call | bytes 1 | tf_op jit(solution)/shard_map/partial/pallas_call | solution.py:35
  88.6 4.3 %hidden_grads.3 = (bf16[112,1376]{1,0:T(8,128)(2,1)S(1)}, bf16[112,1376]{1,0:T(8,128)(2,1)S(1)}) custom-call(s32[2]{0:T(128)S(1)} %pad_add_fusion.s, bf16[112,2048]{1,0:T(8,128)(2,1)S(1)} %join.9.refs_4_.refs_0_.refs_1_, bf16[112,2048]{1,0:T(8,128)(2,1)S(1)} %collective-permute-done.14.refs_1_, f32[448,1376]{1,0:T(8,128)S(1)} %get-tuple-element.47.refs_2_, ...), custom_call_target="tpu_custom_call" | custom-call | flops 1262485504 | bytes 17121280 | tf_op jit(solution)/shard_map/hidden_grads/pallas_call | solution.py:35
  92.9 2.4 %partial.10 = (bf16[56,2048]{1,0:T(8,128)(2,1)S(1)}, bf16[56,2048]{1,0:T(8,128)(2,1)S(1)}) custom-call(s32[2]{0:T(128)S(1)} %pad_add_fusion.s, bf16[112,1376]{1,0:T(8,128)(2,1)S(1)} %get-tuple-element.53.refs_0_, bf16[112,1376]{1,0:T(8,128)(2,1)S(1)} %get-tuple-element.54.refs_1_, bf16[1376,4096]{1,0:T(8,128)(2,1)S(1)} %load_gate.1.refs_3_.refs_2_, ...), custom_call_target="tpu_custom_call" | custom-call | bytes 1 | tf_op jit(solution)/shard_map/partial/pallas_call | solution.py:35
  95.9 2.4 %partial.9.refs_0_ = bf16[112,2048]{1,0:T(8,128)(2,1)S(1)} custom-call(s32[2]{0:T(128)S(1)} %pad_add_fusion.s, bf16[112,1376]{1,0:T(8,128)(2,1)S(1)} %get-tuple-element.53.refs_0_, bf16[112,1376]{1,0:T(8,128)(2,1)S(1)} %get-tuple-element.54.refs_1_, bf16[1376,4096]{1,0:T(8,128)(2,1)S(1)} %load_gate.1.refs_3_.refs_2_, ...), custom_call_target="tpu_custom_call" | custom-call | bytes 1 | tf_op jit(solution)/shard_map/partial/pallas_call | solution.py:35
  98.3 2.3 %collective-permute-done.18.refs_1_ = bf16[112,2048]{1,0:T(8,128)(2,1)S(1)} collective-permute-done((bf16[112,2048]{1,0:T(8,128)(2,1)S(1)}, bf16[112,2048]{1,0:T(8,128)(2,1)S(1)}, u32[]{:S(2)}, u32[]{:S(2)}) %collective-permute-start.18) | collective-permute-done | bytes 458784 | tf_op jit(solution)/shard_map/ppermute | solution.py:343
  101.9 2.4 %partial.11 = bf16[112,2048]{1,0:T(8,128)(2,1)S(1)} custom-call(s32[2]{0:T(128)S(1)} %pad_add_fusion.s, bf16[336,1376]{1,0:T(8,128)(2,1)S(1)} %get-tuple-element.49.refs_0_.refs_2_, bf16[336,1376]{1,0:T(8,128)(2,1)S(1)} %get-tuple-element.50.refs_1_, bf16[1376,4096]{1,0:T(8,128)(2,1)S(1)} %load_gate.1.refs_3_.refs_2_, ...), custom_call_target="tpu_custom_call" | custom-call | bytes 1 | tf_op jit(solution)/shard_map/partial/pallas_call | solution.py:35
  105.0 2.7 %partial.6.refs_0_.refs_2_ = bf16[112,2048]{1,0:T(8,128)(2,1)S(1)} custom-call(s32[2]{0:T(128)S(1)} %pad_add_fusion.s, bf16[336,1376]{1,0:T(8,128)(2,1)S(1)} %get-tuple-element.49.refs_0_.refs_2_, bf16[336,1376]{1,0:T(8,128)(2,1)S(1)} %get-tuple-element.50.refs_1_, bf16[1376,4096]{1,0:T(8,128)(2,1)S(1)} %load_gate.1.refs_3_.refs_2_, ...), custom_call_target="tpu_custom_call" | custom-call | bytes 1 | tf_op jit(solution)/shard_map/partial/pallas_call | solution.py:35
  113.5 5.7 %down_grads.2.refs_2_ = bf16[1376,4096]{1,0:T(8,128)(2,1)} custom-call(s32[2]{0:T(128)S(1)} %pad_add_fusion.s, bf16[448,1376]{1,0:T(8,128)(2,1)S(1)} %get-tuple-element.44.refs_4_.h_ref, bf16[336,2048]{1,0:T(8,128)(2,1)S(1)} %join.8.refs_0_, bf16[112,2048]{1,0:T(8,128)(2,1)S(1)} %join.9.refs_4_.refs_0_.refs_1_, bf16[56,2048]{1,0:T(8,128)(2,1)S(1)} %add_rounded.5.refs_2_, ...), custom_call_target="tpu_custom_call" | custom-call | bytes 1 | tf_op jit(solution)/shard_map/down_grads/pallas_call | solution.py:310
  119.2 2.9 %collective-permute-done.24.refs_4_.refs_5_ = bf16[56,2048]{1,0:T(8,128)(2,1)S(1)} collective-permute-done((bf16[56,2048]{1,0:T(8,128)(2,1)S(1)}, bf16[56,2048]{1,0:T(8,128)(2,1)S(1)}, u32[]{:S(2)}, u32[]{:S(2)}) %collective-permute-start.24) | collective-permute-done | bytes 229408 | tf_op jit(solution)/shard_map/ppermute | solution.py:346
  122.1 5.7 %down_grads.3.refs_6_ = bf16[1376,4096]{1,0:T(8,128)(2,1)} custom-call(s32[2]{0:T(128)S(1)} %pad_add_fusion.s, bf16[448,1376]{1,0:T(8,128)(2,1)S(1)} %get-tuple-element.44.refs_4_.h_ref, bf16[336,2048]{1,0:T(8,128)(2,1)S(1)} %collective-permute-done.12.refs_1_.refs_0_, ...), custom_call_target="tpu_custom_call", output_to_operand_aliasing={{}: (4, {})} | custom-call | bytes 1 | tf_op jit(solution)/shard_map/down_grads/pallas_call | solution.py:310
  128.4 2.3 %collective-permute-done.23.refs_4_ = bf16[56,2048]{1,0:T(8,128)(2,1)S(1)} collective-permute-done((bf16[56,2048]{1,0:T(8,128)(2,1)S(1)}, bf16[56,2048]{1,0:T(8,128)(2,1)S(1)}, u32[]{:S(2)}, u32[]{:S(2)}) %collective-permute-start.23) | collective-permute-done | bytes 229408 | tf_op jit(solution)/shard_map/ppermute | solution.py:346
  (74 shorter events, 29.8 us)
Async XLA Ops:
  2.8 2.9 %collective-permute-start.1 = (bf16[256,2048]{1,0:T(8,128)(2,1)S(1)}, bf16[256,2048]{1,0:T(8,128)(2,1)S(1)}, u32[]{:S(2)}, u32[]{:S(2)}) collective-permute-start(bf16[256,2048]{1,0:T(8,128)(2,1)S(1)} %get-tuple-element.35), channel_id=1, source_target_pairs={{0,1},{1,0},{2,3},{3,2},{4,5},{5,4},{6,7},{7,6},{8,9},{9,8},{10,11... | collective-permute-start | bytes 3145736 | tf_op jit(solution)/shard_map/ppermute | solution.py:343
  7.8 26.9 %collective-permute-start.2 = (bf16[112,2048]{1,0:T(8,128)(2,1)S(1)}, bf16[112,2048]{1,0:T(8,128)(2,1)S(1)}, u32[]{:S(2)}, u32[]{:S(2)}) collective-permute-start(bf16[112,2048]{1,0:T(8,128)(2,1)S(1)} %get-tuple-element.36.refs_5_.refs_0_), channel_id=1, source_target_pairs={{0,2},{1,3},{2,0},{3,1},{4,6},{5,7},{6,4},{7,5},{8,10},{9,11},{10,... | collective-permute-start | bytes 1376264 | tf_op jit(solution)/shard_map/ppermute | solution.py:343
  10.8 14.1 %collective-permute-start.3 = (bf16[56,2048]{1,0:T(8,128)(2,1)S(1)}, bf16[56,2048]{1,0:T(8,128)(2,1)S(1)}, u32[]{:S(2)}, u32[]{:S(2)}) collective-permute-start(bf16[56,2048]{1,0:T(8,128)(2,1)S(1)} %get-tuple-element.38.rest_0_), channel_id=1, source_target_pairs={{0,4},{1,5},{2,6},{3,7},{4,8},{5,9},{6,10},{7,11},{8,12},{9,13},{1... | collective-permute-start | bytes 688136 | tf_op jit(solution)/shard_map/ppermute | solution.py:346
  12.4 12.6 %collective-permute-start.4 = (bf16[56,2048]{1,0:T(8,128)(2,1)S(1)}, bf16[56,2048]{1,0:T(8,128)(2,1)S(1)}, u32[]{:S(2)}, u32[]{:S(2)}) collective-permute-start(bf16[56,2048]{1,0:T(8,128)(2,1)S(1)} %get-tuple-element.39), channel_id=1, source_target_pairs={{0,12},{1,13},{2,14},{3,15},{4,0},{5,1},{6,2},{7,3},{8,4},{9,5},{1... | collective-permute-start | bytes 688136 | tf_op jit(solution)/shard_map/ppermute | solution.py:346
  14.6 20.1 %collective-permute-start.5 = (bf16[56,2048]{1,0:T(8,128)(2,1)S(1)}, bf16[56,2048]{1,0:T(8,128)(2,1)S(1)}, u32[]{:S(2)}, u32[]{:S(2)}) collective-permute-start(bf16[56,2048]{1,0:T(8,128)(2,1)S(1)} %get-tuple-element.40), channel_id=1, source_target_pairs={{0,8},{1,9},{2,10},{3,11},{4,12},{5,13},{6,14},{7,15},{8,0},{9,1},... | collective-permute-start | bytes 688136 | tf_op jit(solution)/shard_map/ppermute | solution.py:346
  35.3 17.4 %collective-permute-start.8 = (bf16[168,2048]{1,0:T(8,128)(2,1)S(1)}, bf16[168,2048]{1,0:T(8,128)(2,1)S(1)}, u32[]{:S(2)}, u32[]{:S(2)}) collective-permute-start(bf16[168,2048]{1,0:T(8,128)(2,1)S(1)} %join.5.refs_2_), channel_id=1, source_target_pairs={{0,2},{1,3},{2,0},{3,1},{4,6},{5,7},{6,4},{7,5},{8,10},{9,11},{10,... | collective-permute-start | bytes 2064392 | tf_op jit(solution)/shard_map/ppermute | solution.py:343
  35.9 12.2 %collective-permute-start.7 = (bf16[56,2048]{1,0:T(8,128)(2,1)S(1)}, bf16[56,2048]{1,0:T(8,128)(2,1)S(1)}, u32[]{:S(2)}, u32[]{:S(2)}) collective-permute-start(bf16[56,2048]{1,0:T(8,128)(2,1)S(1)} %get-tuple-element.43), channel_id=1, source_target_pairs={{0,12},{1,13},{2,14},{3,15},{4,0},{5,1},{6,2},{7,3},{8,4},{9,5},{1... | collective-permute-start | bytes 688136 | tf_op jit(solution)/shard_map/ppermute | solution.py:346
  37.5 10.5 %collective-permute-start.6 = (bf16[56,2048]{1,0:T(8,128)(2,1)S(1)}, bf16[56,2048]{1,0:T(8,128)(2,1)S(1)}, u32[]{:S(2)}, u32[]{:S(2)}) collective-permute-start(bf16[56,2048]{1,0:T(8,128)(2,1)S(1)} %get-tuple-element.41), channel_id=1, source_target_pairs={{0,4},{1,5},{2,6},{3,7},{4,8},{5,9},{6,10},{7,11},{8,12},{9,13},{1... | collective-permute-start | bytes 688136 | tf_op jit(solution)/shard_map/ppermute | solution.py:346
  53.4 3.9 %collective-permute-start.10 = (bf16[448,2048]{1,0:T(8,128)(2,1)S(1)}, bf16[448,2048]{1,0:T(8,128)(2,1)S(1)}, u32[]{:S(2)}, u32[]{:S(2)}) collective-permute-start(bf16[448,2048]{1,0:T(8,128)(2,1)S(1)} %join.6.refs_2_.refs_0_), channel_id=1, source_target_pairs={{0,1},{1,0},{2,3},{3,2},{4,5},{5,4},{6,7},{7,6},{8,9},{9,8},{10,11... | collective-permute-start | bytes 5505032 | tf_op jit(solution)/shard_map/ppermute | solution.py:343
  53.5 16.3 %collective-permute-start.11 = (bf16[56,2048]{1,0:T(8,128)(2,1)S(1)}, bf16[56,2048]{1,0:T(8,128)(2,1)S(1)}, u32[]{:S(2)}, u32[]{:S(2)}) collective-permute-start(bf16[56,2048]{1,0:T(8,128)(2,1)S(1)} %get-tuple-element.46), channel_id=1, source_target_pairs={{0,8},{1,9},{2,10},{3,11},{4,12},{5,13},{6,14},{7,15},{8,0},{9,1},... | collective-permute-start | bytes 688136 | tf_op jit(solution)/shard_map/ppermute | solution.py:346
  54.2 15.6 %collective-permute-start.9 = (bf16[112,2048]{1,0:T(8,128)(2,1)S(1)}, bf16[112,2048]{1,0:T(8,128)(2,1)S(1)}, u32[]{:S(2)}, u32[]{:S(2)}) collective-permute-start(bf16[112,2048]{1,0:T(8,128)(2,1)S(1)} %join.7.refs_2_), channel_id=1, source_target_pairs={{0,2},{1,3},{2,0},{3,1},{4,6},{5,7},{6,4},{7,5},{8,10},{9,11},{10,... | collective-permute-start | bytes 1376264 | tf_op jit(solution)/shard_map/ppermute | solution.py:343
  70.5 3.2 %collective-permute-start.12 = (bf16[336,2048]{1,0:T(8,128)(2,1)S(1)}, bf16[336,2048]{1,0:T(8,128)(2,1)S(1)}, u32[]{:S(2)}, u32[]{:S(2)}) collective-permute-start(bf16[336,2048]{1,0:T(8,128)(2,1)S(1)} %join.8.refs_0_), channel_id=1, source_target_pairs={{0,1},{1,0},{2,3},{3,2},{4,5},{5,4},{6,7},{7,6},{8,9},{9,8},{10,11... | collective-permute-start | bytes 4128776 | tf_op jit(solution)/shard_map/ppermute | solution.py:343
  70.7 8.2 %collective-permute-start.13 = (bf16[56,2048]{1,0:T(8,128)(2,1)S(1)}, bf16[56,2048]{1,0:T(8,128)(2,1)S(1)}, u32[]{:S(2)}, u32[]{:S(2)}) collective-permute-start(bf16[56,2048]{1,0:T(8,128)(2,1)S(1)} %collective-permute-done.11.refs_5_.refs_0_), channel_id=1, source_target_pairs={{0,2},{1,3},{2,0},{3,1},{4,6},{5,7},{6,4},{7,5},{8,10},{9,11},{10,... | collective-permute-start | bytes 688136 | tf_op jit(solution)/shard_map/ppermute | solution.py:343
  83.1 4.2 %collective-permute-start.15 = (bf16[224,2048]{1,0:T(8,128)(2,1)S(1)}, bf16[224,2048]{1,0:T(8,128)(2,1)S(1)}, u32[]{:S(2)}, u32[]{:S(2)}) collective-permute-start(bf16[224,2048]{1,0:T(8,128)(2,1)S(1)} %partial.8), channel_id=1, source_target_pairs={{0,1},{1,0},{2,3},{3,2},{4,5},{5,4},{6,7},{7,6},{8,9},{9,8},{10,11... | collective-permute-start | bytes 2752520 | tf_op jit(solution)/shard_map/ppermute | solution.py:343
  83.3 5.3 %collective-permute-start.14 = (bf16[112,2048]{1,0:T(8,128)(2,1)S(1)}, bf16[112,2048]{1,0:T(8,128)(2,1)S(1)}, u32[]{:S(2)}, u32[]{:S(2)}) collective-permute-start(bf16[112,2048]{1,0:T(8,128)(2,1)S(1)} %join.9.refs_4_.refs_0_.refs_1_), channel_id=1, source_target_pairs={{0,1},{1,0},{2,3},{3,2},{4,5},{5,4},{6,7},{7,6},{8,9},{9,8},{10,11... | collective-permute-start | bytes 1376264 | tf_op jit(solution)/shard_map/ppermute | solution.py:343
  88.0 12.6 %collective-permute-start.18 = (bf16[112,2048]{1,0:T(8,128)(2,1)S(1)}, bf16[112,2048]{1,0:T(8,128)(2,1)S(1)}, u32[]{:S(2)}, u32[]{:S(2)}) collective-permute-start(bf16[112,2048]{1,0:T(8,128)(2,1)S(1)} %get-tuple-element.52.refs_5_), channel_id=1, source_target_pairs={{0,2},{1,3},{2,0},{3,1},{4,6},{5,7},{6,4},{7,5},{8,10},{9,11},{10,... | collective-permute-start | bytes 1376264 | tf_op jit(solution)/shard_map/ppermute | solution.py:343
  95.3 6.0 %collective-permute-start.16 = (bf16[56,2048]{1,0:T(8,128)(2,1)S(1)}, bf16[56,2048]{1,0:T(8,128)(2,1)S(1)}, u32[]{:S(2)}, u32[]{:S(2)}) collective-permute-start(bf16[56,2048]{1,0:T(8,128)(2,1)S(1)} %get-tuple-element.55), channel_id=1, source_target_pairs={{0,1},{1,0},{2,3},{3,2},{4,5},{5,4},{6,7},{7,6},{8,9},{9,8},{10,11... | collective-permute-start | bytes 688136 | tf_op jit(solution)/shard_map/ppermute | solution.py:343
  95.4 5.9 %collective-permute-start.17 = (bf16[56,2048]{1,0:T(8,128)(2,1)S(1)}, bf16[56,2048]{1,0:T(8,128)(2,1)S(1)}, u32[]{:S(2)}, u32[]{:S(2)}) collective-permute-start(bf16[56,2048]{1,0:T(8,128)(2,1)S(1)} %get-tuple-element.56), channel_id=1, source_target_pairs={{0,1},{1,0},{2,3},{3,2},{4,5},{5,4},{6,7},{7,6},{8,9},{9,8},{10,11... | collective-permute-start | bytes 688136 | tf_op jit(solution)/shard_map/ppermute | solution.py:343
  104.4 5.4 %collective-permute-start.19 = (bf16[112,2048]{1,0:T(8,128)(2,1)S(1)}, bf16[112,2048]{1,0:T(8,128)(2,1)S(1)}, u32[]{:S(2)}, u32[]{:S(2)}) collective-permute-start(bf16[112,2048]{1,0:T(8,128)(2,1)S(1)} %partial.11), channel_id=1, source_target_pairs={{0,1},{1,0},{2,3},{3,2},{4,5},{5,4},{6,7},{7,6},{8,9},{9,8},{10,11... | collective-permute-start | bytes 1376264 | tf_op jit(solution)/shard_map/ppermute | solution.py:343
  104.5 8.0 %collective-permute-start.22 = (bf16[56,2048]{1,0:T(8,128)(2,1)S(1)}, bf16[56,2048]{1,0:T(8,128)(2,1)S(1)}, u32[]{:S(2)}, u32[]{:S(2)}) collective-permute-start(bf16[56,2048]{1,0:T(8,128)(2,1)S(1)} %get-tuple-element.59.refs_4_), channel_id=1, source_target_pairs={{0,2},{1,3},{2,0},{3,1},{4,6},{5,7},{6,4},{7,5},{8,10},{9,11},{10,... | collective-permute-start | bytes 688136 | tf_op jit(solution)/shard_map/ppermute | solution.py:343
  107.7 11.5 %collective-permute-start.21 = (bf16[56,2048]{1,0:T(8,128)(2,1)S(1)}, bf16[56,2048]{1,0:T(8,128)(2,1)S(1)}, u32[]{:S(2)}, u32[]{:S(2)}) collective-permute-start(bf16[56,2048]{1,0:T(8,128)(2,1)S(1)} %get-tuple-element.58.refs_3_), channel_id=1, source_target_pairs={{0,12},{1,13},{2,14},{3,15},{4,0},{5,1},{6,2},{7,3},{8,4},{9,5},{1... | collective-permute-start | bytes 688136 | tf_op jit(solution)/shard_map/ppermute | solution.py:346
  108.4 13.7 %collective-permute-start.24 = (bf16[56,2048]{1,0:T(8,128)(2,1)S(1)}, bf16[56,2048]{1,0:T(8,128)(2,1)S(1)}, u32[]{:S(2)}, u32[]{:S(2)}) collective-permute-start(bf16[56,2048]{1,0:T(8,128)(2,1)S(1)} %get-tuple-element.63), channel_id=1, source_target_pairs={{0,4},{1,5},{2,6},{3,7},{4,8},{5,9},{6,10},{7,11},{8,12},{9,13},{1... | collective-permute-start | bytes 688136 | tf_op jit(solution)/shard_map/ppermute | solution.py:346
  110.5 17.3 %collective-permute-start.20 = (bf16[56,2048]{1,0:T(8,128)(2,1)S(1)}, bf16[56,2048]{1,0:T(8,128)(2,1)S(1)}, u32[]{:S(2)}, u32[]{:S(2)}) collective-permute-start(bf16[56,2048]{1,0:T(8,128)(2,1)S(1)} %get-tuple-element.61.refs_3_), channel_id=1, source_target_pairs={{0,2},{1,3},{2,0},{3,1},{4,6},{5,7},{6,4},{7,5},{8,10},{9,11},{10,... | collective-permute-start | bytes 688136 | tf_op jit(solution)/shard_map/ppermute | solution.py:343
  113.1 17.6 %collective-permute-start.23 = (bf16[56,2048]{1,0:T(8,128)(2,1)S(1)}, bf16[56,2048]{1,0:T(8,128)(2,1)S(1)}, u32[]{:S(2)}, u32[]{:S(2)}) collective-permute-start(bf16[56,2048]{1,0:T(8,128)(2,1)S(1)} %add_rounded.5.refs_2_), channel_id=1, source_target_pairs={{0,8},{1,9},{2,10},{3,11},{4,12},{5,13},{6,14},{7,15},{8,0},{9,1},... | collective-permute-start | bytes 688136 | tf_op jit(solution)/shard_map/ppermute | solution.py:346
  (9 other events, 89.8 us)

commit v4 on v3

--- a/solution.py
+++ b/solution.py
@@ -11,7 +11,7 @@
 TN = (((0,), (0,)), ((), ()))
 MIB = 1024 * 1024
 HBLOCK = 512
-LIMIT = 8
+LIMIT = 12
 
 
 def limit(rows):
@@ -105,15 +105,13 @@
             got = lax.dot_general(p, mine_ref[cut], TN, preferred_element_type=F32)
             got = got + lax.dot_general(q, got_ref[cut], TN, preferred_element_type=F32)
             got = got.astype(BF16)
-            outs[0][i * slots : (i + 1) * slots] = got[:slots]
-            for d in range(1, EXPERTS):
-                outs[i * (EXPERTS - 1) + d][...] = got[d * slots : (d + 1) * slots]
-
-    outs = [jax.ShapeDtypeStruct((2 * slots, half), BF16)]
-    outs += [jax.ShapeDtypeStruct((slots, half), BF16)] * (2 * EXPERTS - 2)
+            for d in range(EXPERTS):
+                outs[i * EXPERTS + d][...] = got[d * slots : (d + 1) * slots]
+
+    outs = [jax.ShapeDtypeStruct((slots, half), BF16)] * (2 * EXPERTS)
     args = (ids, other_ids, mine, received)
     made = on_core(body, info, args, outs, "pack", 8 * rows * 4 * slots * half, LIMIT)
-    return made[0], (None, *made[1:EXPERTS]), (None, *made[EXPERTS:])
+    return made[:EXPERTS], made[EXPERTS:]
 
 
 def unpack(info, ids, other_ids, pieces, slots, capacity, deps):
@@ -240,36 +238,60 @@
             u = wide_dot(s, own_ref[...], other_ref[...], u_ref, cut)
             sig = jax.nn.sigmoid(g)
             act = g * sig
-            act_ref[:, cut] = act
-            dact_ref[:, cut] = u * sig * (1.0 + g * (1.0 - sig))
+            act_ref[:, cut] = act.astype(BF16)
+            dact_ref[:, cut] = (u * sig * (1.0 + g * (1.0 - sig))).astype(BF16)
             hid_ref[:, cut] = (act * u).astype(BF16)
 
     outs = [
-        jax.ShapeDtypeStruct((m, hidden), F32),
-        jax.ShapeDtypeStruct((m, hidden), F32),
+        jax.ShapeDtypeStruct((m, hidden), BF16),
+        jax.ShapeDtypeStruct((m, hidden), BF16),
         jax.ShapeDtypeStruct((m, hidden), BF16),
     ]
     args = (own, other, in_vmem(w_gate), in_vmem(w_up))
     return on_core(body, info, args, outs, "gate_up", 4 * m * model * hidden, limit(m), deps)
 
 
-def hidden_grads(info, own, other, row0, act, dact, w_down, deps=()):
+def hidden_grads(info, own, other, row0, act, dact, w_down, deps=(), stream=False):
     hidden, model = w_down.shape
     m = own.shape[0]
 
-    def body(s, refs, outs, _):
+    def body(s, refs, outs, scratch):
         own_ref, other_ref, act_ref, dact_ref, d_ref = refs
         ug_ref, gg_ref = outs
         rows = slice(row0, row0 + m)
-        for at, to in cuts_of(hidden, HBLOCK):
-            h = wide_dot(s, own_ref[...], other_ref[...], d_ref, slice(at, to))
+        cuts, copies = cuts_of(hidden, HBLOCK), []
+        if stream:
+            ring, sem = scratch
+            copies = [
+                pltpu.make_async_copy(
+                    d_ref.at[pl.ds(at, to - at)], ring.at[j % 2, pl.ds(0, to - at)], sem.at[j]
+                )
+                for j, (at, to) in enumerate(cuts)
+            ]
+            for copy in copies[:2]:
+                copy.start()
+        for j, (at, to) in enumerate(cuts):
+            if stream:
+                copies[j].wait()
+                block, cut = ring.at[j % 2], slice(0, to - at)
+            else:
+                block, cut = d_ref, slice(at, to)
+            h = wide_dot(s, own_ref[...], other_ref[...], block, cut)
+            if j + 2 < len(copies):
+                copies[j + 2].start()
             ug_ref[:, at:to] = (h * act_ref[rows, at:to]).astype(BF16)
             gg_ref[:, at:to] = (h * dact_ref[rows, at:to]).astype(BF16)
 
     outs = [jax.ShapeDtypeStruct((m, hidden), BF16)] * 2
+    if stream:
+        scratch = [
+            pltpu.VMEM((2, HBLOCK, model), BF16),
+            pltpu.SemaphoreType.DMA((pl.cdiv(hidden, HBLOCK),)),
+        ]
+        args = (own, other, act, dact, w_down)
+        return on_core(body, info, args, outs, "hidden_grads", 0, limit(m), deps, scratch, (), 1)
     args = (own, other, act, dact, in_vmem(w_down))
-    flops = 2 * m * model * hidden
-    return on_core(body, info, args, outs, "hidden_grads", flops, LIMIT, deps)
+    return on_core(body, info, args, outs, "hidden_grads", 0, LIMIT, deps)
 
 
 def partial(info, up_grad, gate_grad, row0, m, w_gate, w_up, mine, deps=(), pieces=1):
@@ -290,19 +312,27 @@
     return on_core(body, info, args, outs, "partial", 0, LIMIT, deps)
 
 
-def down_grads(info, hid, gs, mine, filled=None, deps=(), db=512):
-    m, hidden = hid.shape
+def down_grads(info, hids, gs, mine, filled=None, deps=(), turns=(0, 1), db=512):
+    m, hidden = sum(h.shape[0] for h in hids), hids[0].shape[1]
     half = gs[0].shape[1]
-    db = min(db, half)
     steps = half // db
+    count = steps // turns[1]
+    first = turns[0] * count
     parts = [(i, 0, g.shape[0]) for i, g in enumerate(gs)]
 
     def column(k, s):
-        return (0, k + (s[1] if mine else 1 - s[1]) * steps)
-
-    def body(s, h_ref, *refs):
-        o_ref, g_ref = refs[-2:]
-        stack(g_ref, refs[: len(gs)], parts)
+        return (0, first + k + (s[1] if mine else 1 - s[1]) * steps)
+
+    hid_parts = [(i, 0, h.shape[0]) for i, h in enumerate(hids)]
+
+    def body(s, *refs):
+        o_ref, g_ref, h_ref = refs[-3:]
+
+        @pl.when(pl.program_id(0) == 0)
+        def _():
+            stack(h_ref, refs[: len(hids)], hid_parts)
+
+        stack(g_ref, refs[len(hids) : len(hids) + len(gs)], parts)
         o = lax.dot_general(h_ref[...], g_ref[...], TN, preferred_element_type=F32)
         o_ref[...] = o.astype(BF16)
 
@@ -311,20 +341,20 @@
         body,
         grid_spec=pltpu.PrefetchScalarGridSpec(
             num_scalar_prefetch=1,
-            grid=(steps,),
-            in_specs=[pl.BlockSpec((m, hidden), lambda k, s: (0, 0))]
-            + [pl.BlockSpec((g.shape[0], db), lambda k, s: (0, k)) for g in gs]
+            grid=(count,),
+            in_specs=[pl.BlockSpec(h.shape, lambda k, s: (0, 0)) for h in hids]
+            + [pl.BlockSpec((g.shape[0], db), lambda k, s: (0, first + k)) for g in gs]
             + [pl.BlockSpec(memory_space=pltpu.HBM)] * len(old)
             + [pl.BlockSpec(memory_space=pl.ANY)] * len(deps),
             out_specs=pl.BlockSpec((hidden, db), column),
-            scratch_shapes=[pltpu.VMEM((m, db), BF16)],
+            scratch_shapes=[pltpu.VMEM((m, db), BF16), pltpu.VMEM((m, hidden), BF16)],
         ),
         out_shape=jax.ShapeDtypeStruct((hidden, 2 * half), BF16),
-        input_output_aliases={2 + len(gs): 0} if old else {},
+        input_output_aliases={1 + len(hids) + len(gs): 0} if old else {},
         compiler_params=pltpu.CompilerParams(vmem_limit_bytes=limit(m) * MIB),
         cost_estimate=cost(0, 1),
         name="down_grads",
-    )(info, hid, *gs, *old, *deps)
+    )(info, *hids, *gs, *old, *deps)
 
 
 def shards(tokens, token_grad_in, expert_ids, gate_weight, up_weight, down_weight):
@@ -370,63 +400,70 @@
     mine, sent = halves(info, tokens, token_grad_in)
     received = flip(sent, 0)
     other_ids = flip(expert_ids, 0)
-    near, tok, grad = pack(info, expert_ids, other_ids, mine, received, slots, capacity)
+    tok, grad = pack(info, expert_ids, other_ids, mine, received, slots, capacity)
 
     t1, t3, t2 = plane_shift(tok[1], 1), plane_shift(tok[3], 3), plane_shift(tok[2], 2)
-    near = spread([near])
+    near_tok, near_grad = spread([tok[0]]), spread([grad[0]])
     w_up = load(info, w_up, "load_up", (tok[1],))
     w_gate = load(info, w_gate, "load_gate", (tok[1], w_up))
-    chips = len(near)
+    chips = len(near_tok)
     n = chips * slots
 
-    def by_plane(x, near_row, deps):
-        rows = [(c, near_row, slots) for c in range(chips)]
+    def by_plane(x, deps):
         count = x[0].shape[0] // slots
-        rows += [(chips + c, i * slots, slots) for i in range(count) for c in range(chips)]
-        return join(info, [*near, *x], rows, deps)
-
-    t = joined(info, [t1, t3, t2], (w_gate, w_up, *near))
+        rows = [(c, i * slots, slots) for i in range(count) for c in range(chips)]
+        return join(info, x, rows, deps)
+
+    def back(grads, row0, rows, mine, deps=(), pieces=1):
+        return partial(info, *grads, row0, rows, w_gate, w_up, mine, deps, pieces)
+
+    t = joined(info, [t1, t3, t2], (w_gate, w_up, *near_tok, *near_grad))
     g1 = plane_shift(after(grad[1], t), 1)
     g3 = plane_shift(after(grad[3], t), 3)
-    t = by_plane(spread([t]), 0, (g1, g3))
+    t = spread([t])
+
+    near_t, near_g = joined(info, near_tok), joined(info, near_grad)
+    near_t_other, near_g_other = flip(near_t, 0), flip(near_g, 0)
+    act0, dact0, hid0 = gate_up(info, near_t, near_t_other, w_gate, w_up)
+    grads0 = hidden_grads(info, near_g, near_g_other, 0, act0, dact0, w_down)
+
+    t = by_plane(t, (g1, g3, grads0[0]))
     t_other = flip(t, 0)
-    g2 = plane_shift(after(grad[2], t), 2)
-    g13 = spread([joined(info, [g1, g3], (t,))])
-    act, dact, hid = gate_up(info, t, t_other, w_gate, w_up)
-
-    g13 = by_plane(g13, slots, (hid, g2))
+    g13 = joined(info, [g1, g3], (t,))
+    g2 = plane_shift(after(grad[2], g13), 2)
+    kept0 = back(grads0, 0, n, True, (g13,))[0]
+    g13 = spread([g13])
+    act, dact, hid = gate_up(info, t, t_other, w_gate, w_up, (kept0,))
+
+    g13 = by_plane(g13, (hid, g2))
     g13_other = flip(g13, 0)
     g2 = spread([after(g2, g13)])
-    up_grad, gate_grad = hidden_grads(info, g13, g13_other, 0, act, dact, w_down)
-    g2 = joined(info, g2, (up_grad,))
+    sent0 = back(grads0, 0, n, False, (g13,))[0]
+    got0 = flip(sent0, 0)
+    grads13 = hidden_grads(info, g13, g13_other, 0, act, dact, w_down, (sent0,))
+    g2 = joined(info, g2, (grads13[0],))
     g2_other = flip(g2, 0)
-
-    def back(row0, rows, mine, deps=()):
-        return partial(info, up_grad, gate_grad, row0, rows, w_gate, w_up, mine, deps)[0]
-
-    got = flip(back(n, 2 * n, False, (g2,)), 0)
-    kept = back(n, 2 * n, True)
+    got = flip(back(grads13, 0, 2 * n, False, (g2,))[0], 0)
+    kept = back(grads13, 0, 2 * n, True)[0]
     rows13 = [(p * n + c * slots, slots) for c in range(chips) for p in range(2)]
     sum13 = add_split(info, kept, [got], rows13)
-
-    up_grad2, gate_grad2 = hidden_grads(
-        info, g2, g2_other, 3 * n, act, dact, w_down, (sum13[0],)
+    sum0 = add_split(info, kept0, [got0], [(0, n)], (sum13[0],))
+    grads2 = hidden_grads(
+        info, g2, g2_other, 2 * n, act, dact, w_down, (sum13[0],), True
     )
-    halves2 = (up_grad2, gate_grad2, 0, n, w_gate, w_up)
-    got = [flip(x, 0) for x in partial(info, *halves2, False, (), chips)]
-    kept = partial(info, *halves2, True)[0]
+    got = [flip(x, 0) for x in back(grads2, 0, n, False, (), chips)]
+    kept = back(grads2, 0, n, True)[0]
     far1, far3 = fold(sum13, 2)
     sum2 = add_split(info, kept, got, [(0, n)], (far1,))
     piece1, piece3 = plane_shift(far1, EXPERTS - 1), plane_shift(far3, EXPERTS - 3)
 
-    got = flip(back(0, n, False, (sum2[0],)), 0)
-    kept = back(0, n, True)
-    (far2,) = fold(sum2, 1, (kept,))
+    hids, gs = [hid0, hid], [near_g, g13, g2]
+    down_grad = down_grads(info, hids, gs, True, None, (sum2[0], far1))
+    (far2,) = fold(sum2, 1, (), (down_grad,))
     piece2 = plane_shift(far2, EXPERTS - 2)
-    sum0 = add_split(info, kept, [got], [(0, n)])
-    down_grad = down_grads(info, hid, [g13, g2], True, None, (far2, sum0[0]))
-    down_grad = down_grads(info, hid, [g13_other, g2_other], False, down_grad, (piece1, piece3))
-    (piece0,) = fold(sum0, 1)
+    gs = [near_g_other, g13_other, g2_other]
+    down_grad = down_grads(info, hids, gs, False, down_grad, (far2, piece1, piece3))
+    (piece0,) = fold(sum0, 1, (), (down_grad,))
     pieces = {0: piece0, 1: piece1, 2: piece2, 3: piece3}
     mine, theirs = unpack(
         info,

time: 135 us -> 134 us (level)
  waiting for transfers between devices: 41.6 us -> 20.9 us
  Pallas kernels: 72.3 us -> 85.3 us
  starting transfers between devices: 18.8 us -> 24.9 us
    pallas_call x23 -> x27, Pallas kernels: 51.4 us -> 64.3 us  [on_core(): pl.pallas_call(run, in_specs=[pl.BlockSpec(memory_space=pltpu.SMEM)] + [v...]
    ppermute x9, waiting for transfers between devices: 25.1 us -> 14.4 us  [plane_shift(): lax.ppermute(x, 'expert', [(i, (i + d * share) % devices) for i in range(...]
    ppermute x17 -> x20, waiting for transfers between devices: 16.5 us -> 6.47 us  [flip(): lax.ppermute(x, 'expert', [(i, i ^ 1 << bit) for i in range(devices)])]
    ppermute x17 -> x20, starting transfers between devices: 9.52 us -> 13.2 us  [flip(): lax.ppermute(x, 'expert', [(i, i ^ 1 << bit) for i in range(devices)])]
    ppermute x9, starting transfers between devices: 9.26 us -> 11.7 us  [plane_shift(): lax.ppermute(x, 'expert', [(i, (i + d * share) % devices) for i in range(...]
  transfers between devices with their start and end apart: 26 -> 29, of which waited for: 11 -> 7; matrix products, arithmetic and copies ran while one was open for 0% -> 0% of each run, Pallas kernels for 43% -> 56%
where the time goes in v4:
time: 134 us
  Pallas kernels  85.3 us (64%)
  starting transfers between devices  24.9 us (19%)
  waiting for transfers between devices  20.9 us (16%)
    pallas_call x27, Pallas kernels, on_core(): pl.pallas_call(run, in_specs=[pl.BlockSpec(memory_space=pltpu.SMEM)] + [v...  64.3 us
    ppermute x9, waiting for transfers between devices, plane_shift(): lax.ppermute(x, 'expert', [(i, (i + d * share) % devices) for i in range(...  14.4 us
    ppermute x20, starting transfers between devices, flip(): lax.ppermute(x, 'expert', [(i, i ^ 1 << bit) for i in range(devices)])  13.2 us
    ppermute x9, starting transfers between devices, plane_shift(): lax.ppermute(x, 'expert', [(i, (i + d * share) % devices) for i in range(...  11.7 us
    pallas_call x2, Pallas kernels, down_grads(): pl.pallas_call(body, grid_spec=pltpu.PrefetchScalarGridSpec(num_scalar_pr...  11.5 us
    pallas_call x2, Pallas kernels, load(): pl.pallas_call(body, in_specs=[pl.BlockSpec(memory_space=pltpu.SMEM)] + [...  9.5 us
    ppermute x20, waiting for transfers between devices, flip(): lax.ppermute(x, 'expert', [(i, i ^ 1 << bit) for i in range(devices)])  6.47 us
  transfers between devices with their start and end apart: 29, of which 7 were waited for; matrix products, arithmetic and copies ran while one was open for 0% of the time, Pallas kernels for 56%

profile of v4, /device:TPU:0, one launch (start us, length us, event | category | flops | bytes accessed | tf_op | source)
XLA Modules:
  0.0 133.6 jit_solution(8450623624440952838)
XLA Ops:
  0.7 2.1 %halves.1 = (bf16[256,2048]{1,0:T(8,128)(2,1)S(1)}, bf16[256,2048]{1,0:T(8,128)(2,1)S(1)}) custom-call(s32[2]{0:T(128)S(1)} %pad_add_fusion.s, bf16[128,4096]{1,0:T(8,128)(2,1)} %refs_0_.3, bf16[128,4096]{1,0:T(8,128)(2,1)} %refs_1_.1), custom_call_target="tpu_custom_call" | custom-call | bytes 1 | tf_op jit(solution)/shard_map/halves/pallas_call | solution.py:35
  3.6 2.1 %collective-permute-done.refs_1_ = s32[128,1]{1,0:T(8,128)S(1)} collective-permute-done((s32[128,1]{1,0:T(8,128)S(1)}, s32[128,1]{1,0:T(8,128)S(1)}, u32[]{:S(2)}, u32[]{:S(2)}) %collective-permute-start) | collective-permute-done | bytes 544 | tf_op jit(solution)/shard_map/ppermute | solution.py:373
  5.7 2.1 %pack.1 = (bf16[56,2048]{1,0:T(8,128)(2,1)S(1)}, bf16[56,2048]{1,0:T(8,128)(2,1)S(1)}, bf16[56,2048]{1,0:T(8,128)(2,1)S(1)}, bf16[56,2048]{1,0:T(8,128)(2,1)S(1)...) custom-call(s32[2]{0:T(128)S(1)} %pad_add_fusion.s, ...), custom_call_target="tpu_custom_call" | custom-call | flops 469762048 | bytes 2098176 | tf_op jit(solution)/shard_map/pack/pallas_call | solution.py:35
  7.8 2.9 %collective-permute-start.4 = (bf16[56,2048]{1,0:T(8,128)(2,1)S(1)}, bf16[56,2048]{1,0:T(8,128)(2,1)S(1)}, u32[]{:S(2)}, u32[]{:S(2)}) collective-permute-start(bf16[56,2048]{1,0:T(8,128)(2,1)S(1)} %get-tuple-element.43.refs_0_.refs_5_), channel_id=1, source_target_pairs={{0,2},{1,3},{2,0},{3,1},{4,6},{5,7},{6,4},{7,5},{8,10},{9,11},{10,... | collective-permute-start | bytes 688136 | tf_op jit(solution)/shard_map/ppermute | solution.py:373
  12.9 2.0 %collective-permute-start.7 = (bf16[56,2048]{1,0:T(8,128)(2,1)S(1)}, bf16[56,2048]{1,0:T(8,128)(2,1)S(1)}, u32[]{:S(2)}, u32[]{:S(2)}) collective-permute-start(bf16[56,2048]{1,0:T(8,128)(2,1)S(1)} %get-tuple-element.50), channel_id=1, source_target_pairs={{0,12},{1,13},{2,14},{3,15},{4,0},{5,1},{6,2},{7,3},{8,4},{9,5},{1... | collective-permute-start | bytes 688136 | tf_op jit(solution)/shard_map/ppermute | solution.py:376
  17.8 4.8 %load_up.1.rest_1_.refs_3_.refs_4_ = bf16[1376,4096]{1,0:T(8,128)(2,1)S(1)} custom-call(s32[2]{0:T(128)S(1)} %pad_add_fusion.s, bf16[1376,4096]{1,0:T(8,128)(2,1)} %bitcast.18, bf16[56,2048]{1,0:T(8,128)(2,1)S(1)} %get-tuple-element.44.rest_0_), custom_call_target="tpu_custom_call" | custom-call | bytes 22544384 | tf_op jit(solution)/shard_map/load_up/pallas_call | solution.py:203
  22.6 4.8 %load_gate.1.refs_2_.refs_3_ = bf16[1376,4096]{1,0:T(8,128)(2,1)S(1)} custom-call(s32[2]{0:T(128)S(1)} %pad_add_fusion.s, bf16[1376,4096]{1,0:T(8,128)(2,1)} %bitcast.19, bf16[56,2048]{1,0:T(8,128)(2,1)S(1)} %get-tuple-element.44.rest_0_, bf16[1376,4096]{1,0:T(8,128)(2,1)S(1)} %load_up.1.rest_1_.refs_3_.refs_4_), custom_call_target="tpu_custom_call" | custom-call | bytes 22544384 | tf_op jit(solution)/shard_map/load_gate/pallas_call | solution.py:203
  27.4 7.6 %collective-permute-done.8.refs_2_ = bf16[56,2048]{1,0:T(8,128)(2,1)S(1)} collective-permute-done((bf16[56,2048]{1,0:T(8,128)(2,1)S(1)}, bf16[56,2048]{1,0:T(8,128)(2,1)S(1)}, u32[]{:S(2)}, u32[]{:S(2)}) %collective-permute-start.8) | collective-permute-done | bytes 229408 | tf_op jit(solution)/shard_map/ppermute | solution.py:376
  39.9 7.6 %gate_up.2 = (bf16[112,1376]{1,0:T(8,128)(2,1)S(1)}, bf16[112,1376]{1,0:T(8,128)(2,1)S(1)}, bf16[112,1376]{1,0:T(8,128)(2,1)S(1)}) custom-call(s32[2]{0:T(128)S(1)} %pad_add_fusion.s, bf16[112,2048]{1,0:T(8,128)(2,1)S(1)} %join.8.refs_0_, bf16[112,2048]{1,0:T(8,128)(2,1)S(1)} %collective-permute-done.5.refs_1_, ...), custom_call_target="tpu_custom_call" | custom-call | flops 2524971008 | bytes 23461888 | tf_op jit(solution)/shard_map/gate_up/pallas_call | solution.py:35
  47.6 4.3 %hidden_grads.3 = (bf16[112,1376]{1,0:T(8,128)(2,1)S(1)}, bf16[112,1376]{1,0:T(8,128)(2,1)S(1)}) custom-call(s32[2]{0:T(128)S(1)} %pad_add_fusion.s, bf16[112,2048]{1,0:T(8,128)(2,1)S(1)} %join.7.refs_0_.refs_2_, bf16[112,2048]{1,0:T(8,128)(2,1)S(1)} %collective-permute-done.3.refs_1_.refs_2_, bf16[112,1376]{1,0:T(8,128)(2,1)S(1)} %get-tuple-element.45.refs_2_, ...), custom_call_target="tpu_custom_call" | custom-call | bytes 1 | tf_op jit(solution)/shard_map/hidden_grads/pallas_call | solution.py:35
  55.9 2.5 %partial.6.refs_4_.refs_0_ = bf16[112,2048]{1,0:T(8,128)(2,1)S(1)} custom-call(s32[2]{0:T(128)S(1)} %pad_add_fusion.s, bf16[112,1376]{1,0:T(8,128)(2,1)S(1)} %get-tuple-element.47.refs_4_.refs_0_, bf16[112,1376]{1,0:T(8,128)(2,1)S(1)} %get-tuple-element.48.refs_1_, bf16[1376,4096]{1,0:T(8,128)(2,1)S(1)} %load_gate.1.refs_2_.refs_3_, ...), custom_call_target="tpu_custom_call" | custom-call | bytes 1 | tf_op jit(solution)/shard_map/partial/pallas_call | solution.py:35
  58.4 9.8 %gate_up.3 = (bf16[336,1376]{1,0:T(8,128)(2,1)S(1)}, bf16[336,1376]{1,0:T(8,128)(2,1)S(1)}, bf16[336,1376]{1,0:T(8,128)(2,1)S(1)}) custom-call(s32[2]{0:T(128)S(1)} %pad_add_fusion.s, bf16[336,2048]{1,0:T(8,128)(2,1)S(1)} %join.10.refs_2_.refs_0_, bf16[336,2048]{1,0:T(8,128)(2,1)S(1)} %collective-permute-done.13.refs_1_, ...), custom_call_target="tpu_custom_call" | custom-call | flops 7574913024 | bytes 25296896 | tf_op jit(solution)/shard_map/gate_up/pallas_call | solution.py:35
  70.4 2.5 %partial.7.refs_5_ = bf16[112,2048]{1,0:T(8,128)(2,1)S(1)} custom-call(s32[2]{0:T(128)S(1)} %pad_add_fusion.s, bf16[112,1376]{1,0:T(8,128)(2,1)S(1)} %get-tuple-element.47.refs_4_.refs_0_, bf16[112,1376]{1,0:T(8,128)(2,1)S(1)} %get-tuple-element.48.refs_1_, bf16[1376,4096]{1,0:T(8,128)(2,1)S(1)} %load_gate.1.refs_2_.refs_3_, ...), custom_call_target="tpu_custom_call" | custom-call | bytes 1 | tf_op jit(solution)/shard_map/partial/pallas_call | solution.py:35
  72.9 4.3 %hidden_grads.4 = (bf16[224,1376]{1,0:T(8,128)(2,1)S(1)}, bf16[224,1376]{1,0:T(8,128)(2,1)S(1)}) custom-call(s32[2]{0:T(128)S(1)} %pad_add_fusion.s, bf16[224,2048]{1,0:T(8,128)(2,1)S(1)} %join.12.refs_4_.refs_0_.refs_3_, bf16[224,2048]{1,0:T(8,128)(2,1)S(1)} %collective-permute-done.16.refs_1_.refs_3_, bf16[336,1376]{1,0:T(8,128)(2,1)S(1)} %get-tuple-element.58.refs_2_, ...), custom_call_target="tpu_custom_call" | custom-call | bytes 1 | tf_op jit(solution)/shard_map/hidden_grads/pallas_call | solution.py:35
  77.8 3.6 %partial.9 = bf16[224,2048]{1,0:T(8,128)(2,1)S(1)} custom-call(s32[2]{0:T(128)S(1)} %pad_add_fusion.s, bf16[224,1376]{1,0:T(8,128)(2,1)S(1)} %get-tuple-element.60.refs_0_.refs_2_, bf16[224,1376]{1,0:T(8,128)(2,1)S(1)} %get-tuple-element.61.refs_1_, bf16[1376,4096]{1,0:T(8,128)(2,1)S(1)} %load_gate.1.refs_2_.refs_3_, ...), custom_call_target="tpu_custom_call" | custom-call | bytes 1 | tf_op jit(solution)/shard_map/partial/pallas_call | solution.py:35
  82.0 3.6 %partial.8.refs_0_ = bf16[224,2048]{1,0:T(8,128)(2,1)S(1)} custom-call(s32[2]{0:T(128)S(1)} %pad_add_fusion.s, bf16[224,1376]{1,0:T(8,128)(2,1)S(1)} %get-tuple-element.60.refs_0_.refs_2_, bf16[224,1376]{1,0:T(8,128)(2,1)S(1)} %get-tuple-element.61.refs_1_, bf16[1376,4096]{1,0:T(8,128)(2,1)S(1)} %load_gate.1.refs_2_.refs_3_, ...), custom_call_target="tpu_custom_call" | custom-call | bytes 1 | tf_op jit(solution)/shard_map/partial/pallas_call | solution.py:35
  87.6 7.6 %hidden_grads.5 = (bf16[112,1376]{1,0:T(8,128)(2,1)S(1)}, bf16[112,1376]{1,0:T(8,128)(2,1)S(1)}) custom-call(s32[2]{0:T(128)S(1)} %pad_add_fusion.s, bf16[112,2048]{1,0:T(8,128)(2,1)S(1)} %join.13.refs_4_.refs_0_, bf16[112,2048]{1,0:T(8,128)(2,1)S(1)} %collective-permute-done.20.refs_1_.refs_4_, bf16[336,1376]{1,0:T(8,128)(2,1)S(1)} %get-tuple-element.58.refs_2_, ...), custom_call_target="tpu_custom_call" | custom-call | bytes 1 | tf_op jit(solution)/shard_map/hidden_grads/pallas_call | solution.py:35
  95.2 2.5 %partial.11 = (bf16[56,2048]{1,0:T(8,128)(2,1)S(1)}, bf16[56,2048]{1,0:T(8,128)(2,1)S(1)}) custom-call(s32[2]{0:T(128)S(1)} %pad_add_fusion.s, bf16[112,1376]{1,0:T(8,128)(2,1)S(1)} %get-tuple-element.67.refs_0_, bf16[112,1376]{1,0:T(8,128)(2,1)S(1)} %get-tuple-element.68.refs_1_, bf16[1376,4096]{1,0:T(8,128)(2,1)S(1)} %load_gate.1.refs_2_.refs_3_, ...), custom_call_target="tpu_custom_call" | custom-call | bytes 1 | tf_op jit(solution)/shard_map/partial/pallas_call | solution.py:35
  98.4 2.5 %partial.10.refs_0_ = bf16[112,2048]{1,0:T(8,128)(2,1)S(1)} custom-call(s32[2]{0:T(128)S(1)} %pad_add_fusion.s, bf16[112,1376]{1,0:T(8,128)(2,1)S(1)} %get-tuple-element.67.refs_0_, bf16[112,1376]{1,0:T(8,128)(2,1)S(1)} %get-tuple-element.68.refs_1_, bf16[1376,4096]{1,0:T(8,128)(2,1)S(1)} %load_gate.1.refs_2_.refs_3_, ...), custom_call_target="tpu_custom_call" | custom-call | bytes 1 | tf_op jit(solution)/shard_map/partial/pallas_call | solution.py:35
  107.1 5.7 %down_grads.2.refs_2_.refs_5_ = bf16[1376,4096]{1,0:T(8,128)(2,1)} custom-call(s32[2]{0:T(128)S(1)} %pad_add_fusion.s, bf16[112,1376]{1,0:T(8,128)(2,1)S(1)} %get-tuple-element.66.refs_0_, bf16[336,1376]{1,0:T(8,128)(2,1)S(1)} %get-tuple-element.55.refs_2_.refs_1_, bf16[112,2048]{1,0:T(8,128)(2,1)S(1)} %join.7.refs_0_.refs_2_, ...), custom_call_target="tpu_custom_call" | custom-call | bytes 1 | tf_op jit(solution)/shard_map/down_grads/pallas_call | solution.py:340
  113.4 2.6 %collective-permute-start.27 = (bf16[56,2048]{1,0:T(8,128)(2,1)S(1)}, bf16[56,2048]{1,0:T(8,128)(2,1)S(1)}, u32[]{:S(2)}, u32[]{:S(2)}) collective-permute-start(bf16[56,2048]{1,0:T(8,128)(2,1)S(1)} %add_rounded.4.refs_6_), channel_id=1, source_target_pairs={{0,8},{1,9},{2,10},{3,11},{4,12},{5,13},{6,14},{7,15},{8,0},{9,1},... | collective-permute-start | bytes 688136 | tf_op jit(solution)/shard_map/ppermute | solution.py:376
  116.0 4.5 %collective-permute-done.26.refs_8_.refs_5_ = bf16[56,2048]{1,0:T(8,128)(2,1)S(1)} collective-permute-done((bf16[56,2048]{1,0:T(8,128)(2,1)S(1)}, bf16[56,2048]{1,0:T(8,128)(2,1)S(1)}, u32[]{:S(2)}, u32[]{:S(2)}) %collective-permute-start.26) | collective-permute-done | bytes 229408 | tf_op jit(solution)/shard_map/ppermute | solution.py:376
  120.5 5.7 %down_grads.3.refs_2_.refs_6_ = bf16[1376,4096]{1,0:T(8,128)(2,1)} custom-call(s32[2]{0:T(128)S(1)} %pad_add_fusion.s, bf16[112,1376]{1,0:T(8,128)(2,1)S(1)} %get-tuple-element.66.refs_0_, bf16[336,1376]{1,0:T(8,128)(2,1)S(1)} %get-tuple-element.55.refs_2_.refs_1_, ...), custom_call_target="tpu_custom_call", output_to_operand_aliasing={{}: (6, {})} | custom-call | bytes 1 | tf_op jit(solution)/shard_map/down_grads/pallas_call | solution.py:340
  126.8 2.3 %collective-permute-done.27.refs_4_ = bf16[56,2048]{1,0:T(8,128)(2,1)S(1)} collective-permute-done((bf16[56,2048]{1,0:T(8,128)(2,1)S(1)}, bf16[56,2048]{1,0:T(8,128)(2,1)S(1)}, u32[]{:S(2)}, u32[]{:S(2)}) %collective-permute-start.27) | collective-permute-done | bytes 229408 | tf_op jit(solution)/shard_map/ppermute | solution.py:376
  (84 shorter events, 32.5 us)
Async XLA Ops:
  7.8 9.3 %collective-permute-start.4 = (bf16[56,2048]{1,0:T(8,128)(2,1)S(1)}, bf16[56,2048]{1,0:T(8,128)(2,1)S(1)}, u32[]{:S(2)}, u32[]{:S(2)}) collective-permute-start(bf16[56,2048]{1,0:T(8,128)(2,1)S(1)} %get-tuple-element.43.refs_0_.refs_5_), channel_id=1, source_target_pairs={{0,2},{1,3},{2,0},{3,1},{4,6},{5,7},{6,4},{7,5},{8,10},{9,11},{10,... | collective-permute-start | bytes 688136 | tf_op jit(solution)/shard_map/ppermute | solution.py:373
  10.8 16.6 %collective-permute-start.2 = (bf16[56,2048]{1,0:T(8,128)(2,1)S(1)}, bf16[56,2048]{1,0:T(8,128)(2,1)S(1)}, u32[]{:S(2)}, u32[]{:S(2)}) collective-permute-start(bf16[56,2048]{1,0:T(8,128)(2,1)S(1)} %get-tuple-element.42.refs_0_.refs_7_), channel_id=1, source_target_pairs={{0,2},{1,3},{2,0},{3,1},{4,6},{5,7},{6,4},{7,5},{8,10},{9,11},{10,... | collective-permute-start | bytes 688136 | tf_op jit(solution)/shard_map/ppermute | solution.py:373
  10.9 16.5 %collective-permute-start.6 = (bf16[56,2048]{1,0:T(8,128)(2,1)S(1)}, bf16[56,2048]{1,0:T(8,128)(2,1)S(1)}, u32[]{:S(2)}, u32[]{:S(2)}) collective-permute-start(bf16[56,2048]{1,0:T(8,128)(2,1)S(1)} %get-tuple-element.44.rest_0_), channel_id=1, source_target_pairs={{0,4},{1,5},{2,6},{3,7},{4,8},{5,9},{6,10},{7,11},{8,12},{9,13},{1... | collective-permute-start | bytes 688136 | tf_op jit(solution)/shard_map/ppermute | solution.py:376
  12.9 14.5 %collective-permute-start.7 = (bf16[56,2048]{1,0:T(8,128)(2,1)S(1)}, bf16[56,2048]{1,0:T(8,128)(2,1)S(1)}, u32[]{:S(2)}, u32[]{:S(2)}) collective-permute-start(bf16[56,2048]{1,0:T(8,128)(2,1)S(1)} %get-tuple-element.50), channel_id=1, source_target_pairs={{0,12},{1,13},{2,14},{3,15},{4,0},{5,1},{6,2},{7,3},{8,4},{9,5},{1... | collective-permute-start | bytes 688136 | tf_op jit(solution)/shard_map/ppermute | solution.py:376
  14.9 20.1 %collective-permute-start.8 = (bf16[56,2048]{1,0:T(8,128)(2,1)S(1)}, bf16[56,2048]{1,0:T(8,128)(2,1)S(1)}, u32[]{:S(2)}, u32[]{:S(2)}) collective-permute-start(bf16[56,2048]{1,0:T(8,128)(2,1)S(1)} %get-tuple-element.51), channel_id=1, source_target_pairs={{0,8},{1,9},{2,10},{3,11},{4,12},{5,13},{6,14},{7,15},{8,0},{9,1},... | collective-permute-start | bytes 688136 | tf_op jit(solution)/shard_map/ppermute | solution.py:376
  17.7 22.1 %collective-permute-start.5 = (bf16[112,2048]{1,0:T(8,128)(2,1)S(1)}, bf16[112,2048]{1,0:T(8,128)(2,1)S(1)}, u32[]{:S(2)}, u32[]{:S(2)}) collective-permute-start(bf16[112,2048]{1,0:T(8,128)(2,1)S(1)} %join.8.refs_0_), channel_id=1, source_target_pairs={{0,1},{1,0},{2,3},{3,2},{4,5},{5,4},{6,7},{7,6},{8,9},{9,8},{10,11... | collective-permute-start | bytes 1376264 | tf_op jit(solution)/shard_map/ppermute | solution.py:373
  35.6 17.4 %collective-permute-start.11 = (bf16[168,2048]{1,0:T(8,128)(2,1)S(1)}, bf16[168,2048]{1,0:T(8,128)(2,1)S(1)}, u32[]{:S(2)}, u32[]{:S(2)}) collective-permute-start(bf16[168,2048]{1,0:T(8,128)(2,1)S(1)} %join.9.refs_0_), channel_id=1, source_target_pairs={{0,2},{1,3},{2,0},{3,1},{4,6},{5,7},{6,4},{7,5},{8,10},{9,11},{10,... | collective-permute-start | bytes 2064392 | tf_op jit(solution)/shard_map/ppermute | solution.py:373
  37.7 9.8 %collective-permute-start.3 = (bf16[112,2048]{1,0:T(8,128)(2,1)S(1)}, bf16[112,2048]{1,0:T(8,128)(2,1)S(1)}, u32[]{:S(2)}, u32[]{:S(2)}) collective-permute-start(bf16[112,2048]{1,0:T(8,128)(2,1)S(1)} %join.7.refs_0_.refs_2_), channel_id=1, source_target_pairs={{0,1},{1,0},{2,3},{3,2},{4,5},{5,4},{6,7},{7,6},{8,9},{9,8},{10,11... | collective-permute-start | bytes 1376264 | tf_op jit(solution)/shard_map/ppermute | solution.py:373
  37.8 14.0 %collective-permute-start.10 = (bf16[56,2048]{1,0:T(8,128)(2,1)S(1)}, bf16[56,2048]{1,0:T(8,128)(2,1)S(1)}, u32[]{:S(2)}, u32[]{:S(2)}) collective-permute-start(bf16[56,2048]{1,0:T(8,128)(2,1)S(1)} %get-tuple-element.54), channel_id=1, source_target_pairs={{0,12},{1,13},{2,14},{3,15},{4,0},{5,1},{6,2},{7,3},{8,4},{9,5},{1... | collective-permute-start | bytes 688136 | tf_op jit(solution)/shard_map/ppermute | solution.py:376
  39.5 12.4 %collective-permute-start.9 = (bf16[56,2048]{1,0:T(8,128)(2,1)S(1)}, bf16[56,2048]{1,0:T(8,128)(2,1)S(1)}, u32[]{:S(2)}, u32[]{:S(2)}) collective-permute-start(bf16[56,2048]{1,0:T(8,128)(2,1)S(1)} %get-tuple-element.52), channel_id=1, source_target_pairs={{0,4},{1,5},{2,6},{3,7},{4,8},{5,9},{6,10},{7,11},{8,12},{9,13},{1... | collective-permute-start | bytes 688136 | tf_op jit(solution)/shard_map/ppermute | solution.py:376
  53.6 4.8 %collective-permute-start.13 = (bf16[336,2048]{1,0:T(8,128)(2,1)S(1)}, bf16[336,2048]{1,0:T(8,128)(2,1)S(1)}, u32[]{:S(2)}, u32[]{:S(2)}) collective-permute-start(bf16[336,2048]{1,0:T(8,128)(2,1)S(1)} %join.10.refs_2_.refs_0_), channel_id=1, source_target_pairs={{0,1},{1,0},{2,3},{3,2},{4,5},{5,4},{6,7},{7,6},{8,9},{9,8},{10,11... | collective-permute-start | bytes 4128776 | tf_op jit(solution)/shard_map/ppermute | solution.py:373
  54.3 13.9 %collective-permute-start.12 = (bf16[112,2048]{1,0:T(8,128)(2,1)S(1)}, bf16[112,2048]{1,0:T(8,128)(2,1)S(1)}, u32[]{:S(2)}, u32[]{:S(2)}) collective-permute-start(bf16[112,2048]{1,0:T(8,128)(2,1)S(1)} %join.11.refs_4_.refs_0_), channel_id=1, source_target_pairs={{0,2},{1,3},{2,0},{3,1},{4,6},{5,7},{6,4},{7,5},{8,10},{9,11},{10,... | collective-permute-start | bytes 1376264 | tf_op jit(solution)/shard_map/ppermute | solution.py:373
  55.9 12.4 %collective-permute-start.14 = (bf16[56,2048]{1,0:T(8,128)(2,1)S(1)}, bf16[56,2048]{1,0:T(8,128)(2,1)S(1)}, u32[]{:S(2)}, u32[]{:S(2)}) collective-permute-start(bf16[56,2048]{1,0:T(8,128)(2,1)S(1)} %get-tuple-element.57), channel_id=1, source_target_pairs={{0,8},{1,9},{2,10},{3,11},{4,12},{5,13},{6,14},{7,15},{8,0},{9,1},... | collective-permute-start | bytes 688136 | tf_op jit(solution)/shard_map/ppermute | solution.py:376
  68.9 4.0 %collective-permute-start.16 = (bf16[224,2048]{1,0:T(8,128)(2,1)S(1)}, bf16[224,2048]{1,0:T(8,128)(2,1)S(1)}, u32[]{:S(2)}, u32[]{:S(2)}) collective-permute-start(bf16[224,2048]{1,0:T(8,128)(2,1)S(1)} %join.12.refs_4_.refs_0_.refs_3_), channel_id=1, source_target_pairs={{0,1},{1,0},{2,3},{3,2},{4,5},{5,4},{6,7},{7,6},{8,9},{9,8},{10,11... | collective-permute-start | bytes 2752520 | tf_op jit(solution)/shard_map/ppermute | solution.py:373
  69.2 8.0 %collective-permute-start.17 = (bf16[56,2048]{1,0:T(8,128)(2,1)S(1)}, bf16[56,2048]{1,0:T(8,128)(2,1)S(1)}, u32[]{:S(2)}, u32[]{:S(2)}) collective-permute-start(bf16[56,2048]{1,0:T(8,128)(2,1)S(1)} %collective-permute-done.14.refs_3_.refs_0_), channel_id=1, source_target_pairs={{0,2},{1,3},{2,0},{3,1},{4,6},{5,7},{6,4},{7,5},{8,10},{9,11},{10,... | collective-permute-start | bytes 688136 | tf_op jit(solution)/shard_map/ppermute | solution.py:373
  81.4 4.2 %collective-permute-start.18 = (bf16[224,2048]{1,0:T(8,128)(2,1)S(1)}, bf16[224,2048]{1,0:T(8,128)(2,1)S(1)}, u32[]{:S(2)}, u32[]{:S(2)}) collective-permute-start(bf16[224,2048]{1,0:T(8,128)(2,1)S(1)} %partial.9), channel_id=1, source_target_pairs={{0,1},{1,0},{2,3},{3,2},{4,5},{5,4},{6,7},{7,6},{8,9},{9,8},{10,11... | collective-permute-start | bytes 2752520 | tf_op jit(solution)/shard_map/ppermute | solution.py:373
  81.7 6.0 %collective-permute-start.20 = (bf16[112,2048]{1,0:T(8,128)(2,1)S(1)}, bf16[112,2048]{1,0:T(8,128)(2,1)S(1)}, u32[]{:S(2)}, u32[]{:S(2)}) collective-permute-start(bf16[112,2048]{1,0:T(8,128)(2,1)S(1)} %join.13.refs_4_.refs_0_), channel_id=1, source_target_pairs={{0,1},{1,0},{2,3},{3,2},{4,5},{5,4},{6,7},{7,6},{8,9},{9,8},{10,11... | collective-permute-start | bytes 1376264 | tf_op jit(solution)/shard_map/ppermute | solution.py:373
  86.4 14.5 %collective-permute-start.23 = (bf16[112,2048]{1,0:T(8,128)(2,1)S(1)}, bf16[112,2048]{1,0:T(8,128)(2,1)S(1)}, u32[]{:S(2)}, u32[]{:S(2)}) collective-permute-start(bf16[112,2048]{1,0:T(8,128)(2,1)S(1)} %get-tuple-element.63.refs_2_.refs_5_), channel_id=1, source_target_pairs={{0,2},{1,3},{2,0},{3,1},{4,6},{5,7},{6,4},{7,5},{8,10},{9,11},{10,... | collective-permute-start | bytes 1376264 | tf_op jit(solution)/shard_map/ppermute | solution.py:373
  87.6 15.6 %collective-permute-start.15 = (bf16[112,2048]{1,0:T(8,128)(2,1)S(1)}, bf16[112,2048]{1,0:T(8,128)(2,1)S(1)}, u32[]{:S(2)}, u32[]{:S(2)}) collective-permute-start(bf16[112,2048]{1,0:T(8,128)(2,1)S(1)} %partial.7.refs_5_), channel_id=1, source_target_pairs={{0,1},{1,0},{2,3},{3,2},{4,5},{5,4},{6,7},{7,6},{8,9},{9,8},{10,11... | collective-permute-start | bytes 1376264 | tf_op jit(solution)/shard_map/ppermute | solution.py:373
  102.2 10.6 %collective-permute-start.24 = (bf16[56,2048]{1,0:T(8,128)(2,1)S(1)}, bf16[56,2048]{1,0:T(8,128)(2,1)S(1)}, u32[]{:S(2)}, u32[]{:S(2)}) collective-permute-start(bf16[56,2048]{1,0:T(8,128)(2,1)S(1)} %get-tuple-element.73.refs_5_), channel_id=1, source_target_pairs={{0,2},{1,3},{2,0},{3,1},{4,6},{5,7},{6,4},{7,5},{8,10},{9,11},{10,... | collective-permute-start | bytes 688136 | tf_op jit(solution)/shard_map/ppermute | solution.py:373
  103.9 22.4 %collective-permute-start.19 = (bf16[56,2048]{1,0:T(8,128)(2,1)S(1)}, bf16[56,2048]{1,0:T(8,128)(2,1)S(1)}, u32[]{:S(2)}, u32[]{:S(2)}) collective-permute-start(bf16[56,2048]{1,0:T(8,128)(2,1)S(1)} %get-tuple-element.65), channel_id=1, source_target_pairs={{0,2},{1,3},{2,0},{3,1},{4,6},{5,7},{6,4},{7,5},{8,10},{9,11},{10,... | collective-permute-start | bytes 688136 | tf_op jit(solution)/shard_map/ppermute | solution.py:373
  105.1 10.9 %collective-permute-start.25 = (bf16[56,2048]{1,0:T(8,128)(2,1)S(1)}, bf16[56,2048]{1,0:T(8,128)(2,1)S(1)}, u32[]{:S(2)}, u32[]{:S(2)}) collective-permute-start(bf16[56,2048]{1,0:T(8,128)(2,1)S(1)} %get-tuple-element.72.refs_3_.refs_6_), channel_id=1, source_target_pairs={{0,12},{1,13},{2,14},{3,15},{4,0},{5,1},{6,2},{7,3},{8,4},{9,5},{1... | collective-permute-start | bytes 688136 | tf_op jit(solution)/shard_map/ppermute | solution.py:376
  107.0 13.5 %collective-permute-start.26 = (bf16[56,2048]{1,0:T(8,128)(2,1)S(1)}, bf16[56,2048]{1,0:T(8,128)(2,1)S(1)}, u32[]{:S(2)}, u32[]{:S(2)}) collective-permute-start(bf16[56,2048]{1,0:T(8,128)(2,1)S(1)} %get-tuple-element.75), channel_id=1, source_target_pairs={{0,4},{1,5},{2,6},{3,7},{4,8},{5,9},{6,10},{7,11},{8,12},{9,13},{1... | collective-permute-start | bytes 688136 | tf_op jit(solution)/shard_map/ppermute | solution.py:376
  113.4 15.7 %collective-permute-start.27 = (bf16[56,2048]{1,0:T(8,128)(2,1)S(1)}, bf16[56,2048]{1,0:T(8,128)(2,1)S(1)}, u32[]{:S(2)}, u32[]{:S(2)}) collective-permute-start(bf16[56,2048]{1,0:T(8,128)(2,1)S(1)} %add_rounded.4.refs_6_), channel_id=1, source_target_pairs={{0,8},{1,9},{2,10},{3,11},{4,12},{5,13},{6,14},{7,15},{8,0},{9,1},... | collective-permute-start | bytes 688136 | tf_op jit(solution)/shard_map/ppermute | solution.py:376
  (12 other events, 53.9 us)
